TPU v7x, 32 devices: a whole 2x2x4 slice. The times are simulated.
32 devices in a mesh: date: 4 (over y, core), tile: 8 (over z, x).
Axes of the slice: x: 2, y: 2, z: 4, core: 2. Of those that a mesh axis runs over, the one named last changes fastest.
Arguments:
- radar_echoes: bfloat16 [512, 16, 16, 2, 256], P('tile', None, 'date')
- destination_panel: int32 [512, 1], P('tile'), may hold values from 0 to 7; in each aligned block of 64 rows (0 to 63, 64 to 127, ...) at most 12 rows name the same one
- panel_line_shift: int32 [512], P('tile'), may hold values from 0 to 240
- epoch_couples: int32 [32, 2], replicated, may hold values from 0 to 15, as said below
Outputs:
- coherence: float32 [2048, 32, 256], P('tile', 'date')
Inputs may be any that keep to these rules, and one draw needn't show every extreme that they name: `destination_panel`: of the blocks held by one index of tile, at most 12 land on the same tile; some index reaches it. `epoch_couples`: each row names an earlier date and a later one, 1 to 3 dates apart.
All inputs are finite; a program needn't handle non-finite values.
Results may differ from a plain program's by a relative error of at most 0.00079.
Values may be sent and summed in bfloat16 or wider, within the bound.
No kernel may reach another device: no remote copies, remote signals or barrier semaphores. Data moves between devices by JAX's collectives and lax.ppermute only.
A program may use at most 64 MiB of HBM per device.

v0:
```python
import jax
import jax.numpy as jnp
from jax import lax
from jax.sharding import PartitionSpec as P

TR = 256


def extended(block, sides, width):
    for axis, dim in sides:
        count = lax.axis_size(axis)
        forward = [(i, i + 1) for i in range(count - 1)]
        backward = [(target, source) for source, target in forward]
        low = lax.ppermute(
            lax.slice_in_dim(block, block.shape[dim] - width, None, axis=dim), axis, forward
        )
        high = lax.ppermute(lax.slice_in_dim(block, 0, width, axis=dim), axis, backward)
        block = jnp.concatenate([low, block, high], axis=dim)
    return block


def window_sum(field, rows):
    total = field[0:rows]
    for row_lag in range(1, 7):
        total = total + field[row_lag : row_lag + rows]
    cols = total.shape[-1]
    padded = jnp.pad(total, ((0, 0), (0, 0), (7, 7)))
    result = padded[..., 0:cols]
    for column_lag in range(1, 15):
        result = result + padded[..., column_lag : column_lag + cols]
    return result


def coherence_of(first, second, rows):
    first = first.astype(jnp.float32)
    second = second.astype(jnp.float32)
    first_re, first_im = (first[:, :, 0], first[:, :, 1])
    second_re, second_im = (second[:, :, 0], second[:, :, 1])
    cross_re = first_re * second_re + first_im * second_im
    cross_im = first_im * second_re - first_re * second_im
    power_a = first_re * first_re + first_im * first_im
    power_e = second_re * second_re + second_im * second_im
    box_re = window_sum(cross_re, rows)
    box_im = window_sum(cross_im, rows)
    box_a = window_sum(power_a, rows)
    box_e = window_sum(power_e, rows)
    return jnp.sqrt(box_re * box_re + box_im * box_im) / jnp.sqrt(jnp.maximum(box_a * box_e, 1.0))


def local(radar_echoes, destination_panel, panel_line_shift, epoch_couples):
    patch_number = radar_echoes.shape[0]
    patch_height = radar_echoes.shape[1]
    epoch_here = radar_echoes.shape[2]
    panel_width = radar_echoes.shape[4]
    tile_count = lax.axis_size("tile")
    capacity = max(2, patch_number // tile_count + max(1, patch_number // (2 * tile_count)))
    slot_count = tile_count * capacity
    target = destination_panel[:, 0]
    ordinal = jnp.arange(patch_number)
    earlier_same = (target[:, None] == target[None, :]) & (ordinal[None, :] < ordinal[:, None])
    rank_within = jnp.sum(earlier_same.astype(jnp.int32), axis=1)
    slot_of = target * capacity + rank_within
    chooser = jnp.arange(slot_count)[:, None] == slot_of[None, :]
    serial_patches = radar_echoes.reshape(patch_number, -1)
    send_blocks = jnp.dot(
        chooser.astype(jnp.bfloat16), serial_patches, preferred_element_type=jnp.float32
    )
    send_blocks = send_blocks.astype(jnp.bfloat16).reshape(
        slot_count, patch_height, epoch_here, 2, panel_width
    )
    send_offset = jnp.sum(jnp.where(chooser, panel_line_shift[None, :], 0), axis=1)
    got_blocks, got_offset = (
        lax.all_to_all(send_blocks, "tile", split_axis=0, concat_axis=0, tiled=True),
        lax.all_to_all(send_offset, "tile", split_axis=0, concat_axis=0, tiled=True),
    )
    tile_row = jnp.arange(TR)[:, None, None]
    inner_row = jnp.arange(patch_height)[None, None, :]
    placing = (tile_row == got_offset[None, :, None] + inner_row).astype(jnp.bfloat16)
    placing = placing.reshape(TR, slot_count * patch_height)
    panel_raster = jnp.dot(
        placing,
        got_blocks.reshape(slot_count * patch_height, -1),
        preferred_element_type=jnp.float32,
    )
    panel_raster = panel_raster.astype(jnp.bfloat16).reshape(TR, epoch_here, 2, panel_width)
    band = lax.all_to_all(panel_raster, "date", split_axis=0, concat_axis=1, tiled=True)
    band_rows = band.shape[0]
    rimmed = extended(band, (("date", 0),), 3)
    first = jnp.take(rimmed, epoch_couples[:, 0], axis=1)
    second = jnp.take(rimmed, epoch_couples[:, 1], axis=1)
    band_result = coherence_of(first, second, band_rows)
    return lax.all_to_all(band_result, "date", split_axis=1, concat_axis=0, tiled=True)


def solution(mesh):
    in_specs = (P("tile", None, "date", None, None), P("tile", None), P("tile"), P())
    out_specs = P("tile", "date", None)
    return jax.shard_map(local, mesh=mesh, in_specs=in_specs, out_specs=out_specs, check_vma=False)
```

profile of v0, /device:TPU:0, one launch (start us, length us, event | category | flops | bytes accessed | tf_op | source)
XLA Modules:
  0.0 314.6 jit_solution(1008597656626741752)
XLA Ops:
  0.0 0.9 convert_reduce_fusion
  0.9 0.7 multiply_add_fusion.2
  1.6 0.8 select_reduce_fusion
  2.3 0.7 all_to_all.35
  3.0 7.3 %all-to-all-start = ((s32[8,12,1]{1,2,0:T(1,128)}), s32[8,12,1]{1,2,0:T(1,128)S(1)}, u32[]{:S(2)}, u32[]{:S(2)}) async-start(s32[8,12,1]{1,2,0:T(1,128)} %bitcast.2), calls=%async_computation | async-start | bytes 8192 | tf_op jit(solution)/shard_map/all_to_all | solution.py:74
  10.3 7.8 %reshape.109 = bf16[64,32768]{1,0:T(8,128)(2,1)} reshape(bf16[64,16,4,2,256]{4,3,2,1,0:T(2,128)(2,1)} %param.6) | data formatting | bytes 8388608 | tf_op jit(solution)/shard_map/reshape | solution.py:64
  18.1 6.7 %convolution_convert_fusion = bf16[96,32768]{1,0:T(8,128)(2,1)} fusion(bf16[64,32768]{1,0:T(8,128)(2,1)} %reshape.109, s32[64]{0:T(128)S(1)} %multiply_add_fusion.2), kind=kOutput, calls=%fused_computation.2 | convolution fusion | flops 405805056 | bytes 10486016 | tf_op jit(solution)/shard_map/dot_general | solution.py:65
  24.8 11.1 %reshape.110 = bf16[96,16,4,2,256]{4,3,2,1,0:T(2,128)(2,1)} reshape(bf16[96,32768]{1,0:T(8,128)(2,1)} %convolution_convert_fusion) | data formatting | bytes 12582912 | tf_op jit(solution)/shard_map/reshape | solution.py:68
  35.9 0.0 all-to-all-done
  35.9 6.0 %all-to-all-start.1 = ((bf16[96,16,4,2,256]{4,3,2,1,0:T(2,128)(2,1)}), bf16[96,16,4,2,256]{4,3,2,1,0:T(2,128)(2,1)}, u32[]{:S(2)}, u32[]{:S(2)}) async-start(bf16[96,16,4,2,256]{4,3,2,1,0:T(2,128)(2,1)} %reshape.110), calls=%async_computation.1 | async-start | bytes 12582912 | tf_op jit(solution)/shard_map/all_to_all | solution.py:73
  41.9 0.1 add.321
  42.0 0.5 broadcast.59
  42.5 0.7 reduce.3
  43.2 0.1 add.317
  43.3 0.1 add.318
  43.3 0.1 add.319
  43.4 136.1 %all-to-all-done.1 = bf16[96,16,4,2,256]{4,3,2,1,0:T(2,128)(2,1)} async-done(((bf16[96,16,4,2,256]{4,3,2,1,0:T(2,128)(2,1)}), bf16[96,16,4,2,256]{4,3,2,1,0:T(2,128)(2,1)}, u32[]{:S(2)}, u32[]{:S(2)}) %all-to-all-start.1) | async-done | bytes 6291488 | tf_op jit(solution)/shard_map/all_to_all | solution.py:73
  179.6 11.1 %reshape.111 = bf16[1536,2048]{1,0:T(8,128)(2,1)} reshape(bf16[96,16,4,2,256]{4,3,2,1,0:T(2,128)(2,1)} %all-to-all-done.1) | data formatting | bytes 12582912 | tf_op jit(solution)/shard_map/reshape | solution.py:82
  190.7 4.6 %convolution_convert_fusion.1 = bf16[256,2048]{1,0:T(8,128)(2,1)S(1)} fusion(bf16[1536,2048]{1,0:T(8,128)(2,1)} %reshape.111, s32[1536]{0:T(1024)S(1)} %add.322), kind=kOutput, calls=%fused_computation.59 | convolution fusion | flops 1611530240 | bytes 7346176 | tf_op jit(solution)/shard_map/dot_general | solution.py:80
  195.3 0.0 copy-start
  195.3 1.6 reshape.112
  196.9 3.5 %all-to-all-start.2 = ((bf16[256,4,2,256]{3,2,1,0:T(2,128)(2,1)}), bf16[256,4,2,256]{3,2,1,0:T(2,128)(2,1)S(1)}, u32[]{:S(2)}, u32[]{:S(2)}) async-start(bf16[256,4,2,256]{3,2,1,0:T(2,128)(2,1)} %reshape.112), calls=%async_computation.2 | async-start | bytes 2097152 | tf_op jit(solution)/shard_map/all_to_all | solution.py:86
  200.4 0.0 copy-done
  200.4 14.4 %all-to-all-done.2 = bf16[256,4,2,256]{3,2,1,0:T(2,128)(2,1)S(1)} async-done(((bf16[256,4,2,256]{3,2,1,0:T(2,128)(2,1)}), bf16[256,4,2,256]{3,2,1,0:T(2,128)(2,1)S(1)}, u32[]{:S(2)}, u32[]{:S(2)}) %all-to-all-start.2) | async-done | bytes 1048608 | tf_op jit(solution)/shard_map/all_to_all | solution.py:86
  214.8 0.2 copy.68
  215.0 0.1 fusion.67
  215.2 1.5 collective-permute-start
  216.7 0.1 copy.70
  216.8 1.3 collective-permute-start.1
  218.1 0.0 collective-permute-done
  218.2 1.1 copy_dynamic-update-slice_fusion
  219.4 1.0 collective-permute-done.1
  220.4 8.1 %gather_fusion = bf16[32,70,2,256]{3,2,1,0:T(2,128)(2,1)S(1)} fusion(bf16[70,16,2,256]{3,2,1,0:T(2,128)(2,1)S(1)} %constant_dynamic-update-slice_fusion, s32[1024]{0:T(1024)S(1)} %pad_clamp_fusion.1), kind=kCustom, calls=%fused_computation.clone | custom fusion | bytes 4587648 | tf_op jit(solution)/shard_map/jit(_take)/gather | solution.py:89
  228.5 7.6 %gather_fusion.1 = bf16[32,70,2,256]{3,2,1,0:T(2,128)(2,1)} fusion(bf16[70,16,2,256]{3,2,1,0:T(2,128)(2,1)S(1)} %constant_dynamic-update-slice_fusion, s32[1024]{0:T(1024)S(1)} %pad_clamp_fusion), kind=kCustom, calls=%fused_computation.1.clone | custom fusion | bytes 4587648 | tf_op jit(solution)/shard_map/jit(_take)/gather | solution.py:90
  236.1 2.6 bitcast_convert_fusion
  238.6 0.7 bitcast_add_fusion
  239.4 1.9 multiply_add_fusion.1
  241.3 0.5 fusion.60
  241.8 0.5 fusion.62
  242.4 0.5 fusion.63
  242.9 1.8 fusion.61
  244.7 36.6 %rsqrt_multiply_fusion = f32[64,32,256]{2,1,0:T(8,128)S(1)} fusion(f32[64,32,256]{2,1,0:T(8,128)S(1)} %fusion.60, f32[64,32,256]{2,1,0:T(8,128)} %fusion.61, f32[64,32,256]{2,1,0:T(8,128)S(1)} %fusion.62, f32[64,32,256]{2,1,0:T(8,128)S(1)} %fusion.63), kind=kLoop, calls=%fused_computation.157 | loop fusion | flops 32505856 | bytes 10485760 | tf_op jit(solution)/shard_map/div | solution.py:47
  281.3 1.2 copy.78
  282.5 29.6 %all_to_all.50 = f32[64,32,256]{2,0,1:T(8,128)S(1)} all-to-all(f32[64,32,256]{2,0,1:T(8,128)S(1)} %copy.78), channel_id=1, replica_groups=mesh['date'=4,'tile'=8] {'date'}, dimensions={1} | all-to-all | bytes 4194304 | tf_op jit(solution)/shard_map/all_to_all | solution.py:92
  312.0 2.5 copy.80
  (9 shorter events, 0.2 us)
Async XLA Ops:
  3.0 32.9 %all-to-all-start = ((s32[8,12,1]{1,2,0:T(1,128)}), s32[8,12,1]{1,2,0:T(1,128)S(1)}, u32[]{:S(2)}, u32[]{:S(2)}) async-start(s32[8,12,1]{1,2,0:T(1,128)} %bitcast.2), calls=%async_computation | async-start | bytes 8192 | tf_op jit(solution)/shard_map/all_to_all | solution.py:74
  35.9 143.7 %all-to-all-start.1 = ((bf16[96,16,4,2,256]{4,3,2,1,0:T(2,128)(2,1)}), bf16[96,16,4,2,256]{4,3,2,1,0:T(2,128)(2,1)}, u32[]{:S(2)}, u32[]{:S(2)}) async-start(bf16[96,16,4,2,256]{4,3,2,1,0:T(2,128)(2,1)} %reshape.110), calls=%async_computation.1 | async-start | bytes 12582912 | tf_op jit(solution)/shard_map/all_to_all | solution.py:73
  195.3 5.1 %copy-start = (s32[32,2]{0,1:T(2,128)S(1)}, s32[32,2]{0,1:T(2,128)}, u32[]{:S(2)}) copy-start(s32[32,2]{0,1:T(2,128)} %param.9) | copy-start | bytes 772
  196.9 18.0 %all-to-all-start.2 = ((bf16[256,4,2,256]{3,2,1,0:T(2,128)(2,1)}), bf16[256,4,2,256]{3,2,1,0:T(2,128)(2,1)S(1)}, u32[]{:S(2)}, u32[]{:S(2)}) async-start(bf16[256,4,2,256]{3,2,1,0:T(2,128)(2,1)} %reshape.112), calls=%async_computation.2 | async-start | bytes 2097152 | tf_op jit(solution)/shard_map/all_to_all | solution.py:86
  215.2 3.0 collective-permute-start
  216.8 3.5 %collective-permute-start.1 = (bf16[3,16,2,256]{3,2,1,0:T(2,128)(2,1)S(1)}, bf16[3,16,2,256]{3,2,1,0:T(2,128)(2,1)S(1)}, u32[]{:S(2)}, u32[]{:S(2)}) collective-permute-start(bf16[3,16,2,256]{3,2,1,0:T(2,128)(2,1)S(1)} %bitcast.48), channel_id=1, source_target_pairs={{8,0},{16,8},{24,16},{9,1},{17,9},{25,17},{10,2},{18,10},{26,18},{... | collective-permute-start | bytes 147464 | tf_op jit(solution)/shard_map/ppermute | solution.py:17
where the time goes:
time: 316 us; the launch traced here: 315 us
  waiting for transfers between devices  151 us (48%)
  local copies, waits for them, and re-layouts  54.3 us (17%)
  other arithmetic  48.1 us (15%)
  blocking collectives  29.6 us (9%)
  starting transfers between devices  19.6 us (6%)
  matrix products  11.3 us (4%)
    all_to_all x1, waiting for transfers between devices, local(): lax.all_to_all(send_blocks, 'tile', split_axis=0, concat_axis=0, tiled=True)  136 us
    div x1, other arithmetic, coherence_of(): jnp.sqrt(box_re * box_re + box_im * box_im)  36.6 us
    all_to_all x1, blocking collectives, local(): lax.all_to_all(band_result, 'date', split_axis=1, concat_axis=0, tiled=True)  29.6 us
    all_to_all x1, waiting for transfers between devices, local(): lax.all_to_all(panel_raster, 'date', split_axis=0, concat_axis=1, tiled=T...  14.4 us
    reshape x1, local copies, waits for them, and re-layouts, local(): send_blocks.astype(jnp.bfloat16)  11.1 us
    reshape x1, local copies, waits for them, and re-layouts, local(): got_blocks.reshape(slot_count * patch_height, -1)  11.1 us
    gather x1, local copies, waits for them, and re-layouts, local(): first = jnp.take(rimmed, epoch_couples[:, 0], axis=1)  8.1 us
    reshape x1, local copies, waits for them, and re-layouts, local(): serial_patches = radar_echoes.reshape(patch_number, -1)  7.8 us
  transfers between devices with their start and end apart: 5, of which 3 were waited for; matrix products, arithmetic and copies ran while one was open for 9% of the time, Pallas kernels for 0%

commit v1 on v0

v1 whole, which is shorter than its diff:
```python
import functools

import jax
import jax.numpy as jnp
from jax import lax
from jax.experimental import pallas as pl
from jax.experimental.pallas import tpu as pltpu
from jax.sharding import PartitionSpec as P

TR = 256
LANES = 128
ROW_SPACE = 1 << 16
VMEM_BYTES = 48 * 1024 * 1024


def flip_pairs(axis, mask):
    return [(i, i ^ mask) for i in range(lax.axis_size(axis))]


def swap(value, axis, mask):
    return lax.ppermute(value, axis, flip_pairs(axis, mask))


def pick_kernel(code_ref, blocks_ref, out_ref, meta_ref):
    def body(b, count):
        code = code_ref[b]
        crosses = (code // ROW_SPACE) % 2

        @pl.when(crosses == 1)
        def _():
            out_ref[count] = blocks_ref[b, :, 0]
            meta_ref[count] = code

        return count + crosses

    count = lax.fori_loop(0, blocks_ref.shape[0], body, jnp.int32(0))
    meta_ref[meta_ref.shape[0] - 1] = count


def pick(code, view, date, slots):
    blocks, height, _, parts, lanes = view.shape
    return pl.pallas_call(
        pick_kernel,
        grid=(1,),
        in_specs=[
            pl.BlockSpec(memory_space=pltpu.SMEM),
            pl.BlockSpec((blocks, height, 1, parts, lanes), lambda i: (0, 0, date, 0, 0)),
        ],
        out_specs=[
            pl.BlockSpec((slots, height, parts, lanes), lambda i: (0, 0, 0, 0)),
            pl.BlockSpec(memory_space=pltpu.SMEM),
        ],
        out_shape=[
            jax.ShapeDtypeStruct((slots, height, parts, lanes), view.dtype),
            jax.ShapeDtypeStruct((slots + 1,), jnp.int32),
        ],
        compiler_params=pltpu.CompilerParams(vmem_limit_bytes=VMEM_BYTES),
    )(code, view)


def deposit_kernel(code_ref, meta_ref, blocks_ref, got_ref, send_ref, keep_ref, acc_ref):
    height = blocks_ref.shape[1]
    tiles, rows, parts, lanes = acc_ref.shape

    def clear(t, _):
        acc_ref[t] = jnp.zeros((rows, parts, lanes), jnp.float32)
        return 0

    lax.fori_loop(0, tiles, clear, 0)

    def add(code, block):
        tile = code // (2 * ROW_SPACE)
        row = code % ROW_SPACE
        span = pl.ds(row, height)
        acc_ref[tile, span] = acc_ref[tile, span] + block.astype(jnp.float32)

    def own(b, _):
        code = code_ref[b]

        @pl.when((code // ROW_SPACE) % 2 == 0)
        def _():
            add(code, blocks_ref[b, :, 0])

        return 0

    lax.fori_loop(0, blocks_ref.shape[0], own, 0)

    def received(k, _):
        add(meta_ref[k], got_ref[k])
        return 0

    lax.fori_loop(0, meta_ref[meta_ref.shape[0] - 1], received, 0)

    flat = acc_ref.reshape(tiles, rows * parts, lanes)

    def hand_over(i, _):
        for part in range(parts):
            keep_ref[i, part] = flat[2 * i, pl.ds(part, rows, stride=parts)]
            send_ref[i, part] = flat[2 * i + 1, pl.ds(part, rows, stride=parts)].astype(send_ref.dtype)
        return 0

    lax.fori_loop(0, tiles // 2, hand_over, 0)


def deposit(code, meta, view, got, date, tiles):
    blocks, height, _, parts, lanes = view.shape
    dense = (tiles // 2, parts, TR, lanes)
    return pl.pallas_call(
        deposit_kernel,
        grid=(1,),
        in_specs=[
            pl.BlockSpec(memory_space=pltpu.SMEM),
            pl.BlockSpec(memory_space=pltpu.SMEM),
            pl.BlockSpec((blocks, height, 1, parts, lanes), lambda i: (0, 0, date, 0, 0)),
            pl.BlockSpec(got.shape, lambda i: (0, 0, 0, 0)),
        ],
        out_specs=[
            pl.BlockSpec(dense, lambda i: (0, 0, 0, 0)),
            pl.BlockSpec(dense, lambda i: (0, 0, 0, 0)),
        ],
        out_shape=[
            jax.ShapeDtypeStruct(dense, view.dtype),
            jax.ShapeDtypeStruct(dense, jnp.float32),
        ],
        scratch_shapes=[pltpu.VMEM((tiles, TR, parts, lanes), jnp.float32)],
        compiler_params=pltpu.CompilerParams(vmem_limit_bytes=VMEM_BYTES),
    )(code, meta, view, got)


def split(value):
    high = value.astype(jnp.bfloat16)
    low = (value - high.astype(jnp.float32)).astype(jnp.bfloat16)
    return high, low


def band(size, reach):
    row = lax.broadcasted_iota(jnp.int32, (size, size), 0)
    col = lax.broadcasted_iota(jnp.int32, (size, size), 1)
    return (jnp.abs(row - col) <= reach).astype(jnp.bfloat16)


def coherence_kernel(pairs_ref, *refs):
    *field_refs, out_ref, held, done, sems, out_sems = refs
    copies = [
        pltpu.make_async_copy(ref, held.at[k], sems.at[k]) for k, ref in enumerate(field_refs)
    ]
    for copy in copies:
        copy.start()
    rows, pairs, cols = out_ref.shape
    row_band = band(rows, 3)
    col_band = band(cols, 7)
    halves = cols // held.shape[-1]
    for copy in copies:
        copy.wait()

    def box(value):
        high, low = split(value)
        wide = jnp.dot(high, col_band, preferred_element_type=jnp.float32)
        wide = wide + jnp.dot(low, col_band, preferred_element_type=jnp.float32)
        high, low = split(wide)
        total = jnp.dot(row_band, high, preferred_element_type=jnp.float32)
        return total + jnp.dot(row_band, low, preferred_element_type=jnp.float32)

    def field(index, component):
        sides = [held[index, 2 * half + component] for half in range(halves)]
        return jnp.concatenate(sides, axis=-1).astype(jnp.float32)

    for p in range(pairs):
        first, second = pairs_ref[2 * p], pairs_ref[2 * p + 1]
        u0, u1 = field(first, 0), field(first, 1)
        v0, v1 = field(second, 0), field(second, 1)
        box_re = box(u0 * v0 + u1 * v1)
        box_im = box(u1 * v0 - u0 * v1)
        box_a = box(u0 * u0 + u1 * u1)
        box_e = box(v0 * v0 + v1 * v1)
        value = jnp.sqrt(box_re * box_re + box_im * box_im) * lax.rsqrt(
            jnp.maximum(box_a * box_e, 1.0)
        )
        for half in range(halves):
            side = value[:, half * LANES : (half + 1) * LANES]
            done.at[half].reshape(rows * pairs, LANES)[pl.ds(p, rows, stride=pairs)] = side
    leaving = [
        pltpu.make_async_copy(
            done.at[half], out_ref.at[:, :, pl.ds(half * LANES, LANES)], out_sems.at[half]
        )
        for half in range(halves)
    ]
    for copy in leaving:
        copy.start()
    for copy in leaving:
        copy.wait()


def coherence(pairs, fields, out_shape):
    parts, rows, lanes = fields[0].shape
    return pl.pallas_call(
        coherence_kernel,
        in_specs=[pl.BlockSpec(memory_space=pltpu.SMEM)]
        + [pl.BlockSpec(memory_space=pl.ANY)] * len(fields),
        out_specs=pl.BlockSpec(memory_space=pl.ANY),
        out_shape=jax.ShapeDtypeStruct(out_shape, jnp.float32),
        scratch_shapes=[
            pltpu.VMEM((len(fields), parts, rows, lanes), fields[0].dtype),
            pltpu.VMEM((out_shape[2] // lanes, rows, out_shape[1], lanes), jnp.float32),
            pltpu.SemaphoreType.DMA((len(fields),)),
            pltpu.SemaphoreType.DMA((out_shape[2] // lanes,)),
        ],
        compiler_params=pltpu.CompilerParams(vmem_limit_bytes=VMEM_BYTES),
    )(pairs, *fields)


def local(radar_echoes, destination_panel, panel_line_shift, epoch_couples):
    blocks, height, dates_here, components, cols = radar_echoes.shape
    tile_count = lax.axis_size("tile")
    group_count = lax.axis_size("date")
    here = lax.axis_index("tile")
    group = lax.axis_index("date")
    capacity = max(2, blocks // tile_count + max(1, blocks // (2 * tile_count)))
    slots = min(blocks, tile_count // 2 * capacity)

    halves = cols // LANES
    view = radar_echoes.reshape(blocks, height, dates_here, components, halves, LANES)
    view = view.transpose(0, 1, 2, 4, 3, 5)
    view = view.reshape(blocks, height, dates_here, halves * components, LANES)

    relative = jnp.bitwise_xor(destination_panel[:, 0], here)
    code = relative * ROW_SPACE + panel_line_shift

    groups = {}
    meta = None
    for date in range(dates_here):
        packed, own_meta = pick(code, view, date, slots)
        if meta is None:
            meta = swap(own_meta, "tile", 1)
        got = swap(packed, "tile", 1)
        send, keep = deposit(code, meta, view, got, date, tile_count // 2)
        mask = 2
        while True:
            total = keep + swap(send, "tile", mask).astype(jnp.float32)
            if total.shape[0] == 1:
                break
            keep, send = total[0::2], total[1::2].astype(view.dtype)
            mask *= 2
        field = total[0].astype(view.dtype)
        known = {0: field}
        mask = group_count // 2
        while mask:
            known.update({g ^ mask: swap(f, "date", mask) for g, f in list(known.items())})
            mask //= 2
        for g, f in known.items():
            groups[g * dates_here + date] = f
    fields = [groups[k] for k in range(group_count * dates_here)]

    pairs_here = epoch_couples.shape[0] // group_count
    mine = lax.dynamic_slice_in_dim(epoch_couples, group * pairs_here, pairs_here, axis=0)
    place = jnp.bitwise_xor(mine // dates_here, group) * dates_here + mine % dates_here
    return coherence(place.reshape(-1), fields, (TR, pairs_here, cols))


def solution(mesh):
    in_specs = (P("tile", None, "date", None, None), P("tile", None), P("tile"), P())
    out_specs = P("tile", "date", None)
    return jax.shard_map(local, mesh=mesh, in_specs=in_specs, out_specs=out_specs, check_vma=False)
```

time: 316 us -> 185 us (0.59)
  local copies, waits for them, and re-layouts: 54.3 us -> 2.51 us
  other arithmetic: 48.1 us -> 1.41 us
  Pallas kernels: 0 us -> 34.6 us
  waiting for transfers between devices: 151 us -> 119 us
  blocking collectives: 29.6 us -> 0 us
  matrix products: 11.3 us -> 0 us
  starting transfers between devices: 19.6 us -> 27.6 us
    all_to_all x3 -> x0, waiting for transfers between devices: 151 us -> none  [the longest x1 136 us: local(): lax.all_to_all(send_blocks, 'tile', split_axis=0, concat_axis=0, tiled=True)]
    ppermute x2 -> x25, waiting for transfers between devices: 0.96 us -> 119 us  [swap(): return lax.ppermute(value, axis, flip_pairs(axis, mask))]
    div x1 -> x0, other arithmetic: 36.6 us -> none  [coherence_of(): jnp.sqrt(box_re * box_re + box_im * box_im)]
    pallas_call x0 -> x9, Pallas kernels: none -> 34.6 us  [the longest x4 15.7 us: deposit(): pl.pallas_call(deposit_kernel, grid=(1,), in_specs=[pl.BlockSpec(memory_s...]
    reshape x4 -> x1, local copies, waits for them, and re-layouts: 31.6 us -> 0.08 us  [local(): return coherence(place.reshape(-1), fields, (TR, pairs_here, cols))]
    all_to_all x1 -> x0, blocking collectives: 29.6 us -> none  [local(): lax.all_to_all(band_result, 'date', split_axis=1, concat_axis=0, tiled=True)]
    ppermute x2 -> x25, starting transfers between devices: 2.84 us -> 27.6 us  [swap(): return lax.ppermute(value, axis, flip_pairs(axis, mask))]
    all_to_all x3 -> x0, starting transfers between devices: 16.8 us -> none  [the longest x1 7.25 us: local(): lax.all_to_all(send_offset, 'tile', split_axis=0, concat_axis=0, tiled=True)]
  transfers between devices with their start and end apart: 5 -> 25, of which waited for: 3 -> 9; matrix products, arithmetic and copies ran while one was open for 9% -> 1% of each run, Pallas kernels for 0% -> 13%
where the time goes in v1:
time: 185 us
  waiting for transfers between devices  119 us (64%)
  Pallas kernels  34.6 us (19%)
  starting transfers between devices  27.6 us (15%)
  local copies, waits for them, and re-layouts  2.51 us (1%)
    ppermute x25, waiting for transfers between devices, swap(): return lax.ppermute(value, axis, flip_pairs(axis, mask))  119 us
    ppermute x25, starting transfers between devices, swap(): return lax.ppermute(value, axis, flip_pairs(axis, mask))  27.6 us
    pallas_call x4, Pallas kernels, deposit(): pl.pallas_call(deposit_kernel, grid=(1,), in_specs=[pl.BlockSpec(memory_s...  15.7 us
    pallas_call x4, Pallas kernels, pick(): pl.pallas_call(pick_kernel, grid=(1,), in_specs=[pl.BlockSpec(memory_spac...  10.4 us
    pallas_call x1, Pallas kernels, coherence(): pl.pallas_call(coherence_kernel, in_specs=[pl.BlockSpec(memory_space=pltp...  8.47 us
  transfers between devices with their start and end apart: 25, of which 9 were waited for; matrix products, arithmetic and copies ran while one was open for 1% of the time, Pallas kernels for 13%

profile of v1, /device:TPU:0, one launch (start us, length us, event | category | flops | bytes accessed | tf_op | source)
XLA Modules:
  0.0 184.9 jit_solution(17977211762932495989)
XLA Ops:
  0.0 0.7 bitcast_add_fusion.code_ref
  0.7 2.2 %copy-done = bf16[64,16,4,2,256]{4,3,2,1,0:T(2,128)(2,1)S(1)} copy-done((bf16[64,16,4,2,256]{4,3,2,1,0:T(2,128)(2,1)S(1)}, bf16[64,16,4,2,256]{4,3,2,1,0:T(2,128)(2,1)}, u32[]{:S(2)}) %copy-start) | copy-done | bytes 4194328
  2.9 2.6 %shard_map.48 = (bf16[48,16,4,128]{3,2,1,0:T(4,128)(2,1)S(1)}, s32[49]{0:T(128)}) custom-call(s32[64]{0:T(128)S(1)} %bitcast_add_fusion.code_ref, bf16[64,16,4,4,128]{4,3,2,1,0:T(4,128)(2,1)S(1)} %bitcast.19), custom_call_target="tpu_custom_call" | custom-call | tf_op jit(solution)/shard_map/pallas_call | solution.py:42
  5.5 3.0 %collective-permute-start.4 = (bf16[48,16,4,128]{3,2,1,0:T(4,128)(2,1)S(1)}, bf16[48,16,4,128]{3,2,1,0:T(4,128)(2,1)S(1)}, u32[]{:S(2)}, u32[]{:S(2)}) collective-permute-start(bf16[48,16,4,128]{3,2,1,0:T(4,128)(2,1)S(1)} %get-tuple-element.22), channel_id=1, source_target_pairs={{0,1},{1,0},{2,3},{3,2},{4,5},{5,4},{6,7},{7,6},{8,9},{9,8},{10,11... | collective-permute-start | bytes 2359304 | tf_op jit(solution)/shard_map/ppermute | solution.py:21
  8.5 2.6 %shard_map.50 = (bf16[48,16,4,128]{3,2,1,0:T(4,128)(2,1)S(1)}, s32[49]{0:T(128)}) custom-call(s32[64]{0:T(128)S(1)} %bitcast_add_fusion.code_ref, bf16[64,16,4,4,128]{4,3,2,1,0:T(4,128)(2,1)S(1)} %bitcast.20), custom_call_target="tpu_custom_call" | custom-call | tf_op jit(solution)/shard_map/pallas_call | solution.py:42
  11.1 0.1 collective-permute-start.7
  11.1 2.6 %shard_map.52 = (bf16[48,16,4,128]{3,2,1,0:T(4,128)(2,1)S(1)}, s32[49]{0:T(128)}) custom-call(s32[64]{0:T(128)S(1)} %bitcast_add_fusion.code_ref, bf16[64,16,4,4,128]{4,3,2,1,0:T(4,128)(2,1)S(1)} %bitcast.21), custom_call_target="tpu_custom_call" | custom-call | tf_op jit(solution)/shard_map/pallas_call | solution.py:42
  13.7 2.1 %collective-permute-start.10 = (bf16[48,16,4,128]{3,2,1,0:T(4,128)(2,1)S(1)}, bf16[48,16,4,128]{3,2,1,0:T(4,128)(2,1)S(1)}, u32[]{:S(2)}, u32[]{:S(2)}) collective-permute-start(bf16[48,16,4,128]{3,2,1,0:T(4,128)(2,1)S(1)} %get-tuple-element.28), channel_id=1, source_target_pairs={{0,1},{1,0},{2,3},{3,2},{4,5},{5,4},{6,7},{7,6},{8,9},{9,8},{10,11... | collective-permute-start | bytes 2359304 | tf_op jit(solution)/shard_map/ppermute | solution.py:21
  15.8 2.7 %shard_map.46 = (bf16[48,16,4,128]{3,2,1,0:T(4,128)(2,1)S(1)}, s32[49]{0:T(128)S(1)}) custom-call(s32[64]{0:T(128)S(1)} %bitcast_add_fusion.code_ref, bf16[64,16,4,4,128]{4,3,2,1,0:T(4,128)(2,1)S(1)} %bitcast.22), custom_call_target="tpu_custom_call" | custom-call | tf_op jit(solution)/shard_map/pallas_call | solution.py:42
  18.5 0.1 collective-permute-start.1
  18.6 2.0 %collective-permute-start = (s32[49]{0:T(128)S(1)}, s32[49]{0:T(128)S(1)}, u32[]{:S(2)}, u32[]{:S(2)}) collective-permute-start(s32[49]{0:T(128)S(1)} %get-tuple-element.18), channel_id=1, source_target_pairs={{0,1},{1,0},{2,3},{3,2},{4,5},{5,4},{6,7},{7,6},{8,9},{9,8},{10,11... | collective-permute-start | bytes 596 | tf_op jit(solution)/shard_map/ppermute | solution.py:21
  20.6 56.1 %collective-permute-done.meta_ref = s32[49]{0:T(128)S(1)} collective-permute-done((s32[49]{0:T(128)S(1)}, s32[49]{0:T(128)S(1)}, u32[]{:S(2)}, u32[]{:S(2)}) %collective-permute-start) | collective-permute-done | bytes 228 | tf_op jit(solution)/shard_map/ppermute | solution.py:21
  76.6 3.9 %shard_map.49 = (bf16[2,4,256,128]{3,2,1,0:T(8,128)(2,1)S(1)}, f32[2,4,256,128]{3,2,1,0:T(8,128)S(1)}) custom-call(s32[64]{0:T(128)S(1)} %bitcast_add_fusion.code_ref, s32[49]{0:T(128)S(1)} %collective-permute-done.meta_ref, bf16[64,16,4,4,128]{4,3,2,1,0:T(4,128)(2,1)} %bitcast.15, bf16[48,16,4,128]{3,2,1,0:T(4,128)(2,1)S(1)} %collective-permute-done.4.got_ref), custom_call_target="tpu_custom_call" | custom-call | tf_op jit(solution)/shard_map/pallas_call | solution.py:108
  80.6 1.9 %collective-permute-start.5 = (bf16[2,4,256,128]{3,2,1,0:T(8,128)(2,1)S(1)}, bf16[2,4,256,128]{3,2,1,0:T(8,128)(2,1)S(1)}, u32[]{:S(2)}, u32[]{:S(2)}) collective-permute-start(bf16[2,4,256,128]{3,2,1,0:T(8,128)(2,1)S(1)} %get-tuple-element.24), channel_id=1, source_target_pairs={{0,2},{1,3},{2,0},{3,1},{4,6},{5,7},{6,4},{7,5},{8,10},{9,11},{10,... | collective-permute-start | bytes 1572872 | tf_op jit(solution)/shard_map/ppermute | solution.py:21
  82.5 3.9 %shard_map.51 = (bf16[2,4,256,128]{3,2,1,0:T(8,128)(2,1)S(1)}, f32[2,4,256,128]{3,2,1,0:T(8,128)S(1)}) custom-call(s32[64]{0:T(128)S(1)} %bitcast_add_fusion.code_ref, s32[49]{0:T(128)S(1)} %collective-permute-done.meta_ref, bf16[64,16,4,4,128]{4,3,2,1,0:T(4,128)(2,1)} %bitcast.16, bf16[48,16,4,128]{3,2,1,0:T(4,128)(2,1)S(1)} %collective-permute-done.7.got_ref), custom_call_target="tpu_custom_call" | custom-call | tf_op jit(solution)/shard_map/pallas_call | solution.py:108
  86.4 0.3 collective-permute-start.8
  86.7 0.0 collective-permute-done.10.got_ref
  86.7 3.9 %shard_map.53 = (bf16[2,4,256,128]{3,2,1,0:T(8,128)(2,1)S(1)}, f32[2,4,256,128]{3,2,1,0:T(8,128)S(1)}) custom-call(s32[64]{0:T(128)S(1)} %bitcast_add_fusion.code_ref, s32[49]{0:T(128)S(1)} %collective-permute-done.meta_ref, bf16[64,16,4,4,128]{4,3,2,1,0:T(4,128)(2,1)} %bitcast.17, bf16[48,16,4,128]{3,2,1,0:T(4,128)(2,1)S(1)} %collective-permute-done.10.got_ref), custom_call_target="tpu_custom_call" | custom-call | tf_op jit(solution)/shard_map/pallas_call | solution.py:108
  90.6 1.9 %collective-permute-start.11 = (bf16[2,4,256,128]{3,2,1,0:T(8,128)(2,1)S(1)}, bf16[2,4,256,128]{3,2,1,0:T(8,128)(2,1)S(1)}, u32[]{:S(2)}, u32[]{:S(2)}) collective-permute-start(bf16[2,4,256,128]{3,2,1,0:T(8,128)(2,1)S(1)} %get-tuple-element.30), channel_id=1, source_target_pairs={{0,2},{1,3},{2,0},{3,1},{4,6},{5,7},{6,4},{7,5},{8,10},{9,11},{10,... | collective-permute-start | bytes 1572872 | tf_op jit(solution)/shard_map/ppermute | solution.py:21
  92.5 0.0 collective-permute-done.1.got_ref
  92.5 3.9 %shard_map.47 = (bf16[2,4,256,128]{3,2,1,0:T(8,128)(2,1)S(1)}, f32[2,4,256,128]{3,2,1,0:T(8,128)S(1)}) custom-call(s32[64]{0:T(128)S(1)} %bitcast_add_fusion.code_ref, s32[49]{0:T(128)S(1)} %collective-permute-done.meta_ref, bf16[64,16,4,4,128]{4,3,2,1,0:T(4,128)(2,1)} %bitcast.18, bf16[48,16,4,128]{3,2,1,0:T(4,128)(2,1)S(1)} %collective-permute-done.1.got_ref), custom_call_target="tpu_custom_call" | custom-call | tf_op jit(solution)/shard_map/pallas_call | solution.py:108
  96.4 0.3 collective-permute-start.2
  96.7 0.1 convert_add_fusion.2
  96.9 3.1 %collective-permute-start.6 = (bf16[1,4,256,128]{3,2,1,0:T(8,128)(2,1)S(1)}, bf16[1,4,256,128]{3,2,1,0:T(8,128)(2,1)S(1)}, u32[]{:S(2)}, u32[]{:S(2)}) collective-permute-start(bf16[1,4,256,128]{3,2,1,0:T(8,128)(2,1)S(1)} %slice.78), channel_id=1, source_target_pairs={{0,4},{1,5},{2,6},{3,7},{4,0},{5,1},{6,2},{7,3},{8,12},{9,13},{10,... | collective-permute-start | bytes 786440 | tf_op jit(solution)/shard_map/ppermute | solution.py:21
  100.0 12.3 %collective-permute-done.8 = bf16[2,4,256,128]{3,2,1,0:T(8,128)(2,1)S(1)} collective-permute-done((bf16[2,4,256,128]{3,2,1,0:T(8,128)(2,1)S(1)}, bf16[2,4,256,128]{3,2,1,0:T(8,128)(2,1)S(1)}, u32[]{:S(2)}, u32[]{:S(2)}) %collective-permute-start.8) | collective-permute-done | bytes 524320 | tf_op jit(solution)/shard_map/ppermute | solution.py:21
  112.4 0.1 convert_add_fusion.1
  112.5 4.8 %collective-permute-start.9 = (bf16[1,4,256,128]{3,2,1,0:T(8,128)(2,1)S(1)}, bf16[1,4,256,128]{3,2,1,0:T(8,128)(2,1)S(1)}, u32[]{:S(2)}, u32[]{:S(2)}) collective-permute-start(bf16[1,4,256,128]{3,2,1,0:T(8,128)(2,1)S(1)} %slice.77), channel_id=1, source_target_pairs={{0,4},{1,5},{2,6},{3,7},{4,0},{5,1},{6,2},{7,3},{8,12},{9,13},{10,... | collective-permute-start | bytes 786440 | tf_op jit(solution)/shard_map/ppermute | solution.py:21
  117.2 12.0 %collective-permute-done.11 = bf16[2,4,256,128]{3,2,1,0:T(8,128)(2,1)S(1)} collective-permute-done((bf16[2,4,256,128]{3,2,1,0:T(8,128)(2,1)S(1)}, bf16[2,4,256,128]{3,2,1,0:T(8,128)(2,1)S(1)}, u32[]{:S(2)}, u32[]{:S(2)}) %collective-permute-start.11) | collective-permute-done | bytes 524320 | tf_op jit(solution)/shard_map/ppermute | solution.py:21
  129.2 0.1 convert_add_fusion
  129.3 0.0 copy-start.1
  129.4 2.0 %collective-permute-start.12 = (bf16[1,4,256,128]{3,2,1,0:T(8,128)(2,1)S(1)}, bf16[1,4,256,128]{3,2,1,0:T(8,128)(2,1)S(1)}, u32[]{:S(2)}, u32[]{:S(2)}) collective-permute-start(bf16[1,4,256,128]{3,2,1,0:T(8,128)(2,1)S(1)} %slice.76), channel_id=1, source_target_pairs={{0,4},{1,5},{2,6},{3,7},{4,0},{5,1},{6,2},{7,3},{8,12},{9,13},{10,... | collective-permute-start | bytes 786440 | tf_op jit(solution)/shard_map/ppermute | solution.py:21
  131.4 8.4 %collective-permute-done.2 = bf16[2,4,256,128]{3,2,1,0:T(8,128)(2,1)S(1)} collective-permute-done((bf16[2,4,256,128]{3,2,1,0:T(8,128)(2,1)S(1)}, bf16[2,4,256,128]{3,2,1,0:T(8,128)(2,1)S(1)}, u32[]{:S(2)}, u32[]{:S(2)}) %collective-permute-start.2) | collective-permute-done | bytes 524320 | tf_op jit(solution)/shard_map/ppermute | solution.py:21
  139.8 0.1 convert_add_fusion.3
  139.9 0.8 collective-permute-start.3
  140.7 0.0 collective-permute-done.6
  140.7 0.1 fusion.5.refs_1_
  140.8 1.6 collective-permute-start.18
  142.4 0.0 collective-permute-start.14
  142.4 0.1 fusion.6.refs_2_
  142.4 0.6 collective-permute-start.19
  143.0 14.6 %collective-permute-done.12 = bf16[1,4,256,128]{3,2,1,0:T(8,128)(2,1)S(1)} collective-permute-done((bf16[1,4,256,128]{3,2,1,0:T(8,128)(2,1)S(1)}, bf16[1,4,256,128]{3,2,1,0:T(8,128)(2,1)S(1)}, u32[]{:S(2)}, u32[]{:S(2)}) %collective-permute-start.12) | collective-permute-done | bytes 262176 | tf_op jit(solution)/shard_map/ppermute | solution.py:21
  157.6 0.0 collective-permute-start.15
  157.6 0.1 fusion.7.refs_3_
  157.7 4.3 %collective-permute-done.3 = bf16[1,4,256,128]{3,2,1,0:T(8,128)(2,1)S(1)} collective-permute-done((bf16[1,4,256,128]{3,2,1,0:T(8,128)(2,1)S(1)}, bf16[1,4,256,128]{3,2,1,0:T(8,128)(2,1)S(1)}, u32[]{:S(2)}, u32[]{:S(2)}) %collective-permute-start.3) | collective-permute-done | bytes 262176 | tf_op jit(solution)/shard_map/ppermute | solution.py:21
  162.0 1.3 collective-permute-start.20
  163.3 0.1 fusion.4.refs_0_
  163.4 0.1 collective-permute-start.16
  163.5 0.0 collective-permute-done.14.refs_5_
  163.5 0.8 collective-permute-start.17
  164.3 0.0 collective-permute-done.19.refs_10_
  164.3 0.2 collective-permute-start.13
  164.4 0.0 collective-permute-done.15.refs_6_
  164.4 0.4 collective-permute-start.22
  164.8 6.5 %collective-permute-done.20.refs_11_ = bf16[4,256,128]{2,1,0:T(8,128)(2,1)S(1)} collective-permute-done((bf16[4,256,128]{2,1,0:T(8,128)(2,1)S(1)}, bf16[4,256,128]{2,1,0:T(8,128)(2,1)S(1)}, u32[]{:S(2)}, u32[]{:S(2)}) %collective-permute-start.20) | collective-permute-done | bytes 262176 | tf_op jit(solution)/shard_map/ppermute | solution.py:21
  171.3 0.0 collective-permute-start.23
  171.3 0.0 collective-permute-done.16.refs_7_
  171.3 0.5 collective-permute-start.24
  171.8 3.0 %collective-permute-done.17.refs_8_ = bf16[4,256,128]{2,1,0:T(8,128)(2,1)S(1)} collective-permute-done((bf16[4,256,128]{2,1,0:T(8,128)(2,1)S(1)}, bf16[4,256,128]{2,1,0:T(8,128)(2,1)S(1)}, u32[]{:S(2)}, u32[]{:S(2)}) %collective-permute-start.17) | collective-permute-done | bytes 262176 | tf_op jit(solution)/shard_map/ppermute | solution.py:21
  174.7 0.0 collective-permute-start.21
  174.8 0.1 fusion.8
  174.8 0.1 copy.7
  174.9 0.1 reshape.17.pairs_ref
  175.0 1.4 collective-permute-done.21.refs_12_
  176.4 8.5 %shard_map.54 = f32[256,8,256]{2,1,0:T(8,128)} custom-call(s32[16]{0:T(128)S(1)} %reshape.17.pairs_ref, bf16[4,256,128]{2,1,0:T(8,128)(2,1)S(1)} %fusion.4.refs_0_, bf16[4,256,128]{2,1,0:T(8,128)(2,1)S(1)} %fusion.5.refs_1_, bf16[4,256,128]{2,1,0:T(8,128)(2,1)S(1)} %fusion.6.refs_2_, bf16[4,256,128]{2,1,0:T(8,128)(2,1)S(1)} %fusion.7.refs_3_, ...), custom_call_target="tpu_custom_call" | custom-call | tf_op jit(solution)/shard_map/pallas_call | solution.py:196
  (15 shorter events, 0.2 us)
Async XLA Ops:
  0.7 2.2 %copy-start = (bf16[64,16,4,2,256]{4,3,2,1,0:T(2,128)(2,1)S(1)}, bf16[64,16,4,2,256]{4,3,2,1,0:T(2,128)(2,1)}, u32[]{:S(2)}) copy-start(bf16[64,16,4,2,256]{4,3,2,1,0:T(2,128)(2,1)} %param.4) | copy-start | bytes 12582916
  5.5 71.2 %collective-permute-start.4 = (bf16[48,16,4,128]{3,2,1,0:T(4,128)(2,1)S(1)}, bf16[48,16,4,128]{3,2,1,0:T(4,128)(2,1)S(1)}, u32[]{:S(2)}, u32[]{:S(2)}) collective-permute-start(bf16[48,16,4,128]{3,2,1,0:T(4,128)(2,1)S(1)} %get-tuple-element.22), channel_id=1, source_target_pairs={{0,1},{1,0},{2,3},{3,2},{4,5},{5,4},{6,7},{7,6},{8,9},{9,8},{10,11... | collective-permute-start | bytes 2359304 | tf_op jit(solution)/shard_map/ppermute | solution.py:21
  11.1 71.4 %collective-permute-start.7 = (bf16[48,16,4,128]{3,2,1,0:T(4,128)(2,1)S(1)}, bf16[48,16,4,128]{3,2,1,0:T(4,128)(2,1)S(1)}, u32[]{:S(2)}, u32[]{:S(2)}) collective-permute-start(bf16[48,16,4,128]{3,2,1,0:T(4,128)(2,1)S(1)} %get-tuple-element.25), channel_id=1, source_target_pairs={{0,1},{1,0},{2,3},{3,2},{4,5},{5,4},{6,7},{7,6},{8,9},{9,8},{10,11... | collective-permute-start | bytes 2359304 | tf_op jit(solution)/shard_map/ppermute | solution.py:21
  13.7 72.9 %collective-permute-start.10 = (bf16[48,16,4,128]{3,2,1,0:T(4,128)(2,1)S(1)}, bf16[48,16,4,128]{3,2,1,0:T(4,128)(2,1)S(1)}, u32[]{:S(2)}, u32[]{:S(2)}) collective-permute-start(bf16[48,16,4,128]{3,2,1,0:T(4,128)(2,1)S(1)} %get-tuple-element.28), channel_id=1, source_target_pairs={{0,1},{1,0},{2,3},{3,2},{4,5},{5,4},{6,7},{7,6},{8,9},{9,8},{10,11... | collective-permute-start | bytes 2359304 | tf_op jit(solution)/shard_map/ppermute | solution.py:21
  18.5 74.0 %collective-permute-start.1 = (bf16[48,16,4,128]{3,2,1,0:T(4,128)(2,1)S(1)}, bf16[48,16,4,128]{3,2,1,0:T(4,128)(2,1)S(1)}, u32[]{:S(2)}, u32[]{:S(2)}) collective-permute-start(bf16[48,16,4,128]{3,2,1,0:T(4,128)(2,1)S(1)} %get-tuple-element.19), channel_id=1, source_target_pairs={{0,1},{1,0},{2,3},{3,2},{4,5},{5,4},{6,7},{7,6},{8,9},{9,8},{10,11... | collective-permute-start | bytes 2359304 | tf_op jit(solution)/shard_map/ppermute | solution.py:21
  18.6 58.1 %collective-permute-start = (s32[49]{0:T(128)S(1)}, s32[49]{0:T(128)S(1)}, u32[]{:S(2)}, u32[]{:S(2)}) collective-permute-start(s32[49]{0:T(128)S(1)} %get-tuple-element.18), channel_id=1, source_target_pairs={{0,1},{1,0},{2,3},{3,2},{4,5},{5,4},{6,7},{7,6},{8,9},{9,8},{10,11... | collective-permute-start | bytes 596 | tf_op jit(solution)/shard_map/ppermute | solution.py:21
  80.6 16.1 %collective-permute-start.5 = (bf16[2,4,256,128]{3,2,1,0:T(8,128)(2,1)S(1)}, bf16[2,4,256,128]{3,2,1,0:T(8,128)(2,1)S(1)}, u32[]{:S(2)}, u32[]{:S(2)}) collective-permute-start(bf16[2,4,256,128]{3,2,1,0:T(8,128)(2,1)S(1)} %get-tuple-element.24), channel_id=1, source_target_pairs={{0,2},{1,3},{2,0},{3,1},{4,6},{5,7},{6,4},{7,5},{8,10},{9,11},{10,... | collective-permute-start | bytes 1572872 | tf_op jit(solution)/shard_map/ppermute | solution.py:21
  86.4 26.0 %collective-permute-start.8 = (bf16[2,4,256,128]{3,2,1,0:T(8,128)(2,1)S(1)}, bf16[2,4,256,128]{3,2,1,0:T(8,128)(2,1)S(1)}, u32[]{:S(2)}, u32[]{:S(2)}) collective-permute-start(bf16[2,4,256,128]{3,2,1,0:T(8,128)(2,1)S(1)} %get-tuple-element.27), channel_id=1, source_target_pairs={{0,2},{1,3},{2,0},{3,1},{4,6},{5,7},{6,4},{7,5},{8,10},{9,11},{10,... | collective-permute-start | bytes 1572872 | tf_op jit(solution)/shard_map/ppermute | solution.py:21
  90.6 38.6 %collective-permute-start.11 = (bf16[2,4,256,128]{3,2,1,0:T(8,128)(2,1)S(1)}, bf16[2,4,256,128]{3,2,1,0:T(8,128)(2,1)S(1)}, u32[]{:S(2)}, u32[]{:S(2)}) collective-permute-start(bf16[2,4,256,128]{3,2,1,0:T(8,128)(2,1)S(1)} %get-tuple-element.30), channel_id=1, source_target_pairs={{0,2},{1,3},{2,0},{3,1},{4,6},{5,7},{6,4},{7,5},{8,10},{9,11},{10,... | collective-permute-start | bytes 1572872 | tf_op jit(solution)/shard_map/ppermute | solution.py:21
  96.4 43.3 %collective-permute-start.2 = (bf16[2,4,256,128]{3,2,1,0:T(8,128)(2,1)S(1)}, bf16[2,4,256,128]{3,2,1,0:T(8,128)(2,1)S(1)}, u32[]{:S(2)}, u32[]{:S(2)}) collective-permute-start(bf16[2,4,256,128]{3,2,1,0:T(8,128)(2,1)S(1)} %get-tuple-element.21), channel_id=1, source_target_pairs={{0,2},{1,3},{2,0},{3,1},{4,6},{5,7},{6,4},{7,5},{8,10},{9,11},{10,... | collective-permute-start | bytes 1572872 | tf_op jit(solution)/shard_map/ppermute | solution.py:21
  96.9 43.8 %collective-permute-start.6 = (bf16[1,4,256,128]{3,2,1,0:T(8,128)(2,1)S(1)}, bf16[1,4,256,128]{3,2,1,0:T(8,128)(2,1)S(1)}, u32[]{:S(2)}, u32[]{:S(2)}) collective-permute-start(bf16[1,4,256,128]{3,2,1,0:T(8,128)(2,1)S(1)} %slice.78), channel_id=1, source_target_pairs={{0,4},{1,5},{2,6},{3,7},{4,0},{5,1},{6,2},{7,3},{8,12},{9,13},{10,... | collective-permute-start | bytes 786440 | tf_op jit(solution)/shard_map/ppermute | solution.py:21
  112.5 29.9 %collective-permute-start.9 = (bf16[1,4,256,128]{3,2,1,0:T(8,128)(2,1)S(1)}, bf16[1,4,256,128]{3,2,1,0:T(8,128)(2,1)S(1)}, u32[]{:S(2)}, u32[]{:S(2)}) collective-permute-start(bf16[1,4,256,128]{3,2,1,0:T(8,128)(2,1)S(1)} %slice.77), channel_id=1, source_target_pairs={{0,4},{1,5},{2,6},{3,7},{4,0},{5,1},{6,2},{7,3},{8,12},{9,13},{10,... | collective-permute-start | bytes 786440 | tf_op jit(solution)/shard_map/ppermute | solution.py:21
  129.3 45.4 %copy-start.1 = (s32[32,2]{0,1:T(2,128)S(1)}, s32[32,2]{0,1:T(2,128)}, u32[]{:S(2)}) copy-start(s32[32,2]{0,1:T(2,128)} %param.7) | copy-start | bytes 772
  129.4 28.2 %collective-permute-start.12 = (bf16[1,4,256,128]{3,2,1,0:T(8,128)(2,1)S(1)}, bf16[1,4,256,128]{3,2,1,0:T(8,128)(2,1)S(1)}, u32[]{:S(2)}, u32[]{:S(2)}) collective-permute-start(bf16[1,4,256,128]{3,2,1,0:T(8,128)(2,1)S(1)} %slice.76), channel_id=1, source_target_pairs={{0,4},{1,5},{2,6},{3,7},{4,0},{5,1},{6,2},{7,3},{8,12},{9,13},{10,... | collective-permute-start | bytes 786440 | tf_op jit(solution)/shard_map/ppermute | solution.py:21
  139.9 22.1 %collective-permute-start.3 = (bf16[1,4,256,128]{3,2,1,0:T(8,128)(2,1)S(1)}, bf16[1,4,256,128]{3,2,1,0:T(8,128)(2,1)S(1)}, u32[]{:S(2)}, u32[]{:S(2)}) collective-permute-start(bf16[1,4,256,128]{3,2,1,0:T(8,128)(2,1)S(1)} %slice.79), channel_id=1, source_target_pairs={{0,4},{1,5},{2,6},{3,7},{4,0},{5,1},{6,2},{7,3},{8,12},{9,13},{10,... | collective-permute-start | bytes 786440 | tf_op jit(solution)/shard_map/ppermute | solution.py:21
  140.8 22.6 %collective-permute-start.18 = (bf16[4,256,128]{2,1,0:T(8,128)(2,1)S(1)}, bf16[4,256,128]{2,1,0:T(8,128)(2,1)S(1)}, u32[]{:S(2)}, u32[]{:S(2)}) collective-permute-start(bf16[4,256,128]{2,1,0:T(8,128)(2,1)S(1)} %fusion.5.refs_1_), channel_id=1, source_target_pairs={{0,16},{8,24},{16,0},{24,8},{1,17},{9,25},{17,1},{25,9},{2,18},{10... | collective-permute-start | bytes 786440 | tf_op jit(solution)/shard_map/ppermute | solution.py:21
  142.4 21.1 %collective-permute-start.14 = (bf16[4,256,128]{2,1,0:T(8,128)(2,1)S(1)}, bf16[4,256,128]{2,1,0:T(8,128)(2,1)S(1)}, u32[]{:S(2)}, u32[]{:S(2)}) collective-permute-start(bf16[4,256,128]{2,1,0:T(8,128)(2,1)S(1)} %fusion.5.refs_1_), channel_id=1, source_target_pairs={{0,8},{8,0},{16,24},{24,16},{1,9},{9,1},{17,25},{25,17},{2,10},{10... | collective-permute-start | bytes 786440 | tf_op jit(solution)/shard_map/ppermute | solution.py:21
  142.4 21.8 %collective-permute-start.19 = (bf16[4,256,128]{2,1,0:T(8,128)(2,1)S(1)}, bf16[4,256,128]{2,1,0:T(8,128)(2,1)S(1)}, u32[]{:S(2)}, u32[]{:S(2)}) collective-permute-start(bf16[4,256,128]{2,1,0:T(8,128)(2,1)S(1)} %fusion.6.refs_2_), channel_id=1, source_target_pairs={{0,16},{8,24},{16,0},{24,8},{1,17},{9,25},{17,1},{25,9},{2,18},{10... | collective-permute-start | bytes 786440 | tf_op jit(solution)/shard_map/ppermute | solution.py:21
  157.6 6.8 %collective-permute-start.15 = (bf16[4,256,128]{2,1,0:T(8,128)(2,1)S(1)}, bf16[4,256,128]{2,1,0:T(8,128)(2,1)S(1)}, u32[]{:S(2)}, u32[]{:S(2)}) collective-permute-start(bf16[4,256,128]{2,1,0:T(8,128)(2,1)S(1)} %fusion.6.refs_2_), channel_id=1, source_target_pairs={{0,8},{8,0},{16,24},{24,16},{1,9},{9,1},{17,25},{25,17},{2,10},{10... | collective-permute-start | bytes 786440 | tf_op jit(solution)/shard_map/ppermute | solution.py:21
  162.0 9.2 %collective-permute-start.20 = (bf16[4,256,128]{2,1,0:T(8,128)(2,1)S(1)}, bf16[4,256,128]{2,1,0:T(8,128)(2,1)S(1)}, u32[]{:S(2)}, u32[]{:S(2)}) collective-permute-start(bf16[4,256,128]{2,1,0:T(8,128)(2,1)S(1)} %fusion.7.refs_3_), channel_id=1, source_target_pairs={{0,16},{8,24},{16,0},{24,8},{1,17},{9,25},{17,1},{25,9},{2,18},{10... | collective-permute-start | bytes 786440 | tf_op jit(solution)/shard_map/ppermute | solution.py:21
  163.4 7.9 %collective-permute-start.16 = (bf16[4,256,128]{2,1,0:T(8,128)(2,1)S(1)}, bf16[4,256,128]{2,1,0:T(8,128)(2,1)S(1)}, u32[]{:S(2)}, u32[]{:S(2)}) collective-permute-start(bf16[4,256,128]{2,1,0:T(8,128)(2,1)S(1)} %fusion.7.refs_3_), channel_id=1, source_target_pairs={{0,8},{8,0},{16,24},{24,16},{1,9},{9,1},{17,25},{25,17},{2,10},{10... | collective-permute-start | bytes 786440 | tf_op jit(solution)/shard_map/ppermute | solution.py:21
  163.5 11.2 %collective-permute-start.17 = (bf16[4,256,128]{2,1,0:T(8,128)(2,1)S(1)}, bf16[4,256,128]{2,1,0:T(8,128)(2,1)S(1)}, u32[]{:S(2)}, u32[]{:S(2)}) collective-permute-start(bf16[4,256,128]{2,1,0:T(8,128)(2,1)S(1)} %fusion.4.refs_0_), channel_id=1, source_target_pairs={{0,16},{8,24},{16,0},{24,8},{1,17},{9,25},{17,1},{25,9},{2,18},{10... | collective-permute-start | bytes 786440 | tf_op jit(solution)/shard_map/ppermute | solution.py:21
  164.3 10.7 %collective-permute-start.13 = (bf16[4,256,128]{2,1,0:T(8,128)(2,1)S(1)}, bf16[4,256,128]{2,1,0:T(8,128)(2,1)S(1)}, u32[]{:S(2)}, u32[]{:S(2)}) collective-permute-start(bf16[4,256,128]{2,1,0:T(8,128)(2,1)S(1)} %fusion.4.refs_0_), channel_id=1, source_target_pairs={{0,8},{8,0},{16,24},{24,16},{1,9},{9,1},{17,25},{25,17},{2,10},{10... | collective-permute-start | bytes 786440 | tf_op jit(solution)/shard_map/ppermute | solution.py:21
  164.4 10.6 %collective-permute-start.22 = (bf16[4,256,128]{2,1,0:T(8,128)(2,1)S(1)}, bf16[4,256,128]{2,1,0:T(8,128)(2,1)S(1)}, u32[]{:S(2)}, u32[]{:S(2)}) collective-permute-start(bf16[4,256,128]{2,1,0:T(8,128)(2,1)S(1)} %collective-permute-done.18.refs_9_), channel_id=1, source_target_pairs={{0,8},{8,0},{16,24},{24,16},{1,9},{9,1},{17,25},{25,17},{2,10},{10... | collective-permute-start | bytes 786440 | tf_op jit(solution)/shard_map/ppermute | solution.py:21
  171.3 3.8 %collective-permute-start.23 = (bf16[4,256,128]{2,1,0:T(8,128)(2,1)S(1)}, bf16[4,256,128]{2,1,0:T(8,128)(2,1)}, u32[]{:S(2)}, u32[]{:S(2)}) collective-permute-start(bf16[4,256,128]{2,1,0:T(8,128)(2,1)S(1)} %collective-permute-done.19.refs_10_), channel_id=1, source_target_pairs={{0,8},{8,0},{16,24},{24,16},{1,9},{9,1},{17,25},{25,17},{2,10},{10... | collective-permute-start | bytes 786440 | tf_op jit(solution)/shard_map/ppermute | solution.py:21
  171.3 3.8 %collective-permute-start.24 = (bf16[4,256,128]{2,1,0:T(8,128)(2,1)S(1)}, bf16[4,256,128]{2,1,0:T(8,128)(2,1)}, u32[]{:S(2)}, u32[]{:S(2)}) collective-permute-start(bf16[4,256,128]{2,1,0:T(8,128)(2,1)S(1)} %collective-permute-done.20.refs_11_), channel_id=1, source_target_pairs={{0,8},{8,0},{16,24},{24,16},{1,9},{9,1},{17,25},{25,17},{2,10},{10... | collective-permute-start | bytes 786440 | tf_op jit(solution)/shard_map/ppermute | solution.py:21
  174.7 1.7 collective-permute-start.21

commit v2 on v1

v2 whole, which is shorter than its diff:
```python
import functools

import jax
import jax.numpy as jnp
from jax import lax
from jax.experimental import pallas as pl
from jax.experimental.pallas import tpu as pltpu
from jax.sharding import PartitionSpec as P

TR = 256
LANES = 128
SUBLANES = 8
ROW_SPACE = 1 << 16
CROSS = 1 << 24
MIB = 1024 * 1024
CHEAP = pl.CostEstimate(flops=1, bytes_accessed=1, transcendentals=0)
SMEM = pl.BlockSpec(memory_space=pltpu.SMEM)
VMEM = pl.BlockSpec(memory_space=pltpu.VMEM)
ANY = pl.BlockSpec(memory_space=pl.ANY)


def params(mib):
    return pltpu.CompilerParams(vmem_limit_bytes=mib * MIB)


def swap(value, axis, mask):
    pairs = [(i, i ^ mask) for i in range(lax.axis_size(axis))]
    return lax.ppermute(value, axis, pairs)


def block_codes(target, row, here, order):
    relative = jnp.bitwise_xor(target, here)
    first, *others = [(relative // (1 << bit)) % 2 for bit in order]
    place = sum([bit * (1 << k) for k, bit in enumerate(others)], jnp.zeros_like(relative))
    return first * CROSS + place * ROW_SPACE + row


def unpack(code):
    place = jnp.bitwise_and(lax.shift_right_logical(code, 16), CROSS // ROW_SPACE - 1)
    return lax.shift_right_logical(code, 24), place, jnp.bitwise_and(code, ROW_SPACE - 1)


def pick_kernel(code_ref, blocks_ref, *refs):
    out_ref, count_ref = refs[-2:]
    step = pl.program_id(0)
    share = blocks_ref.shape[0]

    @pl.when(step == 0)
    def _():
        count_ref[0] = 0

    def body(b, count):
        crosses = lax.shift_right_logical(code_ref[step * share + b], 24)

        @pl.when(crosses == 1)
        def _():
            out_ref[count] = blocks_ref[b, :, 0]

        return count + crosses

    count_ref[0] = lax.fori_loop(0, share, body, count_ref[0])


def pick(codes, view, date, slots, tokens):
    blocks, height, _, parts, lanes = view.shape
    steps = PICK_STEPS if blocks % PICK_STEPS == 0 else 1
    return pl.pallas_call(
        pick_kernel,
        grid=(steps,),
        in_specs=[
            SMEM,
            pl.BlockSpec((blocks // steps, height, 1, parts, lanes), lambda i: (i, 0, date, 0, 0)),
        ]
        + [ANY if token.ndim > 1 else SMEM for token in tokens],
        out_specs=VMEM,
        out_shape=jax.ShapeDtypeStruct((slots, height, parts, lanes), view.dtype),
        scratch_shapes=[pltpu.SMEM((1,), jnp.int32)],
        cost_estimate=CHEAP,
        compiler_params=params(PICK_MIB),
        name="pick",
    )(codes, view, *tokens)


def deposit_kernel(
    date, code_ref, partner_ref, view_ref, got_ref, token_ref, far_ref, near_ref, keep_ref, acc_ref, own_ref, sem
):
    del token_ref
    count, height = own_ref.shape[:2]
    tiles, rows, parts, lanes = acc_ref.shape
    fetch = pltpu.make_async_copy(view_ref.at[:, :, date], own_ref, sem)
    fetch.start()
    flat = acc_ref.reshape(tiles, rows * parts, lanes)

    def clear(t, _):
        flat[t] = jnp.zeros((rows * parts, lanes), jnp.float32)
        return 0

    lax.fori_loop(0, tiles, clear, 0)

    def add(tile, row, block):
        span = pl.ds(row, height)
        acc_ref[tile, span] = acc_ref[tile, span] + block.astype(jnp.float32)

    def received(b, slot):
        crosses, tile, row = unpack(partner_ref[b])

        @pl.when(crosses == 1)
        def _():
            add(tile, row, got_ref[slot])

        return slot + crosses

    lax.fori_loop(0, count, received, jnp.int32(0))
    fetch.wait()

    def own(b, _):
        crosses, tile, row = unpack(code_ref[b])

        @pl.when(crosses == 0)
        def _():
            add(tile, row, own_ref[b])

        return 0

    lax.fori_loop(0, count, own, 0)

    strips = rows // SUBLANES

    def dense(tile, part):
        return jnp.concatenate(
            [
                flat[tile, pl.ds(k * parts + part, SUBLANES, stride=strips * parts)]
                for k in range(strips)
            ],
            axis=0,
        )

    def hand_over(i, _):
        for part in range(parts):
            near_ref[i, part] = dense(4 * i + 1, part).astype(near_ref.dtype)
            far_ref[i, part] = dense(4 * i + 3, part).astype(far_ref.dtype)
            keep_ref[2 * i, part] = dense(4 * i, part)
            keep_ref[2 * i + 1, part] = dense(4 * i + 2, part)
        return 0

    lax.fori_loop(0, tiles // 4, hand_over, 0)


def deposit(codes, partner_codes, view, got, date, tiles, token):
    blocks, height, _, parts, lanes = view.shape
    half = (tiles // 4, parts, TR, lanes)
    return pl.pallas_call(
        functools.partial(deposit_kernel, date),
        in_specs=[SMEM, SMEM, ANY, VMEM, ANY],
        out_specs=[VMEM, VMEM, VMEM],
        out_shape=[
            jax.ShapeDtypeStruct(half, view.dtype),
            jax.ShapeDtypeStruct(half, view.dtype),
            jax.ShapeDtypeStruct((tiles // 2,) + half[1:], jnp.float32),
        ],
        scratch_shapes=[
            pltpu.VMEM((tiles, TR, parts, lanes), jnp.float32),
            pltpu.VMEM((blocks, height, parts, lanes), view.dtype),
            pltpu.SemaphoreType.DMA,
        ],
        cost_estimate=CHEAP,
        compiler_params=params(DEPOSIT_MIB),
        name="deposit",
    )(codes, partner_codes, view, got, token)


def merge_kernel(places, *refs):
    *addend_refs, token_ref, out_ref = refs
    del token_ref
    for k, row in enumerate(zip(*places)):
        total = sum(ref[place].astype(jnp.float32) for ref, place in zip(addend_refs, row))
        out_ref[k] = total.astype(out_ref.dtype)


def merge(addends, dtype, token):
    arrays = [array for array, _ in addends]
    places = [tuple(place) for _, place in addends]
    return pl.pallas_call(
        functools.partial(merge_kernel, places),
        in_specs=[VMEM] * len(arrays) + [ANY],
        out_specs=VMEM,
        out_shape=jax.ShapeDtypeStruct((len(places[0]),) + arrays[0].shape[1:], dtype),
        cost_estimate=CHEAP,
        compiler_params=params(DEPOSIT_MIB),
        name="merge",
    )(*arrays, token)


def split(value):
    high = value.astype(jnp.bfloat16)
    return high, (value - high.astype(jnp.float32)).astype(jnp.bfloat16)


def band(size, reach):
    row = lax.broadcasted_iota(jnp.int32, (size, size), 0)
    col = lax.broadcasted_iota(jnp.int32, (size, size), 1)
    return (jnp.abs(row - col) <= reach).astype(jnp.bfloat16)


def shifted(strip, by):
    row = lax.broadcasted_iota(jnp.int32, strip.shape, 0)
    edge = 0 if by > 0 else SUBLANES - 1
    return jnp.where(row == edge, 0.0, pltpu.roll(strip, by % SUBLANES, axis=0))


def boxes(cols):
    col_band = band(cols, 7)

    def box(value):
        strips = [value[k : k + SUBLANES] for k in range(0, value.shape[0], SUBLANES)]
        strips = [shifted(s, 1) for s in strips[-3:]] + strips + [shifted(s, -1) for s in strips[:3]]
        two = [a + b for a, b in zip(strips, strips[1:])]
        four = [a + b for a, b in zip(two, two[2:])]
        seven = [a + b + c for a, b, c in zip(four, two[4:], strips[6:])]
        high, low = split(jnp.concatenate(seven, axis=0))
        wide = jnp.dot(high, col_band, preferred_element_type=jnp.float32)
        return wide + jnp.dot(low, col_band, preferred_element_type=jnp.float32)

    return box


def component(ref, part, halves):
    sides = [ref[2 * half + part] for half in range(halves)]
    return jnp.concatenate(sides, axis=-1).astype(jnp.float32)


def coherence_kernel(pairs_ref, *refs):
    *field_refs, out_ref, stack, done, sems = refs
    rows, pairs, cols = out_ref.shape
    halves = cols // LANES
    strips = rows // SUBLANES
    box = boxes(cols)
    for k, ref in enumerate(field_refs):
        stack[k] = ref[...]
    for p in range(pairs):
        u, v = stack.at[pairs_ref[2 * p]], stack.at[pairs_ref[2 * p + 1]]
        u0, u1 = component(u, 0, halves), component(u, 1, halves)
        v0, v1 = component(v, 0, halves), component(v, 1, halves)
        box_re = box(u0 * v0 + u1 * v1)
        box_im = box(u1 * v0 - u0 * v1)
        box_a = box(u0 * u0 + u1 * u1)
        box_e = box(v0 * v0 + v1 * v1)
        value = jnp.sqrt(box_re * box_re + box_im * box_im) * lax.rsqrt(
            jnp.maximum(box_a * box_e, 1.0)
        )
        for half in range(halves):
            side = done.at[half].reshape(rows * pairs, LANES)
            for k in range(strips):
                place = pl.ds(p + pairs * k, SUBLANES, stride=pairs * strips)
                side[place] = value[k * SUBLANES : (k + 1) * SUBLANES, half * LANES : (half + 1) * LANES]
    leaving = [
        pltpu.make_async_copy(done.at[half], out_ref.at[:, :, pl.ds(half * LANES, LANES)], sems.at[half])
        for half in range(halves)
    ]
    for copy in leaving:
        copy.start()
    for copy in leaving:
        copy.wait()


def coherence(pairs, fields, out_shape):
    rows, pair_count, cols = out_shape
    return pl.pallas_call(
        coherence_kernel,
        in_specs=[SMEM] + [VMEM] * len(fields),
        out_specs=ANY,
        out_shape=jax.ShapeDtypeStruct(out_shape, jnp.float32),
        scratch_shapes=[
            pltpu.VMEM((len(fields),) + fields[0].shape, fields[0].dtype),
            pltpu.VMEM((cols // LANES, rows, pair_count, LANES), jnp.float32),
            pltpu.SemaphoreType.DMA((cols // LANES,)),
        ],
        compiler_params=params(DEPOSIT_MIB),
        name="coherence",
    )(pairs, *fields)


def chunk_plan(dates, bits):
    straight = tuple(range(bits))
    return [(0, straight[1:2] + straight[:1] + straight[2:])] + [(date, straight) for date in range(1, dates)]


PICK_MIB = 60
PICK_STEPS = 4
DEPOSIT_MIB = 48
ORDER = (1, 0, 2, 1, 3, 1, 0, 2, 1, 2, 3, 2, 0, 3, 0, 3)


def local(radar_echoes, destination_panel, panel_line_shift, epoch_couples):
    blocks, height, dates_here, components, cols = radar_echoes.shape
    tile_count = lax.axis_size("tile")
    group_count = lax.axis_size("date")
    here = lax.axis_index("tile")
    group = lax.axis_index("date")
    capacity = max(2, blocks // tile_count + max(1, blocks // (2 * tile_count)))
    slots = min(blocks, tile_count // 2 * capacity)
    bits = tile_count.bit_length() - 1
    stages = bits + 1

    halves = cols // LANES
    view = radar_echoes.reshape(blocks, height, dates_here, components, halves, LANES)
    view = view.transpose(0, 1, 2, 4, 3, 5)
    view = view.reshape(blocks, height, dates_here, halves * components, LANES)

    chunks = chunk_plan(dates_here, bits)
    codes = {}
    partner_codes = {}
    for _, bit_order in chunks:
        if bit_order not in codes:
            codes[bit_order] = block_codes(destination_panel[:, 0], panel_line_shift, here, bit_order)
            partner_codes[bit_order] = swap(codes[bit_order], "tile", 1 << bit_order[0])

    order = ORDER
    if len(order) != len(chunks) * stages:
        order = [c for _, c in sorted((2 * k + c, c) for c in range(len(chunks)) for k in range(stages))]
    state = [None] * len(chunks)
    step = [0] * len(chunks)
    fields = [None] * (group_count * dates_here)
    tokens = list(partner_codes.values())
    for c in order:
        date, bit_order = chunks[c]
        k = step[c]
        step[c] += 1
        flip = [lambda value, bit=bit: swap(value, "tile", 1 << bit) for bit in bit_order]
        if k == 0:
            token = pick(codes[bit_order], view, date, slots, tokens)
            tokens = [token]
            state[c] = flip[0](token)
            continue
        if k == 1:
            far, near, keep = deposit(
                codes[bit_order], partner_codes[bit_order], view, state[c], date, tile_count // 2, token
            )
            token = far
            state[c] = [(keep, range(keep.shape[0]))], flip[1](near), flip[1](far)
            continue
        addends, near, far = state[c]
        if k < bits:
            onward = [(array, places[1::2]) for array, places in addends]
            sent = merge(onward + [(far, range(far.shape[0]))], view.dtype, token)
            token = sent
            addends = [(array, places[0::2]) for array, places in addends]
            addends = addends + [(near, range(near.shape[0]))]
            if sent.shape[0] == 1:
                state[c] = addends, None, flip[k](sent)
            else:
                state[c] = addends, flip[k](sent[0::2]), flip[k](sent[1::2])
            continue
        token = merge(addends + [(far, range(1))], view.dtype, token)
        known = {0: token[0]}
        mask = group_count // 2
        while mask:
            known.update({g ^ mask: swap(f, "date", mask) for g, f in list(known.items())})
            mask //= 2
        for g, f in known.items():
            fields[g * dates_here + date] = f

    pairs_here = epoch_couples.shape[0] // group_count
    mine = lax.dynamic_slice_in_dim(epoch_couples, group * pairs_here, pairs_here, axis=0)
    place = jnp.bitwise_xor(mine // dates_here, group) * dates_here + mine % dates_here
    return coherence(place.reshape(-1), fields, (TR, pairs_here, cols))


def solution(mesh):
    in_specs = (P("tile", None, "date", None, None), P("tile", None), P("tile"), P())
    out_specs = P("tile", "date", None)
    return jax.shard_map(local, mesh=mesh, in_specs=in_specs, out_specs=out_specs, check_vma=False)
```

time: 185 us -> 124 us (0.67)
  waiting for transfers between devices: 119 us -> 55.9 us
  Pallas kernels: 34.6 us -> 40.4 us
  starting transfers between devices: 27.6 us -> 24.7 us
    ppermute x25 -> x30, waiting for transfers between devices: 119 us -> 55.9 us  [swap(): return lax.ppermute(value, axis, pairs)]
    pallas_call x9 -> x17, Pallas kernels: 34.6 us -> 40.4 us  [the longest x4 17 us: deposit(): pl.pallas_call(functools.partial(deposit_kernel, date), in_specs=[SMEM, S...]
    ppermute x25 -> x30, starting transfers between devices: 27.6 us -> 24.7 us  [swap(): return lax.ppermute(value, axis, pairs)]
  transfers between devices with their start and end apart: 25 -> 30, of which waited for: 9 -> 12; matrix products, arithmetic and copies ran while one was open for 1% -> 0% of each run, Pallas kernels for 13% -> 23%
where the time goes in v2:
time: 124 us
  waiting for transfers between devices  55.9 us (45%)
  Pallas kernels  40.4 us (33%)
  starting transfers between devices  24.7 us (20%)
  other arithmetic  1.44 us (1%)
    ppermute x30, waiting for transfers between devices, swap(): return lax.ppermute(value, axis, pairs)  55.9 us
    ppermute x30, starting transfers between devices, swap(): return lax.ppermute(value, axis, pairs)  24.7 us
    pallas_call x4, Pallas kernels, deposit(): pl.pallas_call(functools.partial(deposit_kernel, date), in_specs=[SMEM, S...  17 us
    pallas_call x4, Pallas kernels, pick(): pl.pallas_call(pick_kernel, grid=(steps,), in_specs=[SMEM, pl.BlockSpec((...  14.4 us
    pallas_call x1, Pallas kernels, coherence(): pl.pallas_call(coherence_kernel, in_specs=[SMEM] + [VMEM] * len(fields),...  8.45 us
  transfers between devices with their start and end apart: 30, of which 12 were waited for; matrix products, arithmetic and copies ran while one was open for 0% of the time, Pallas kernels for 23%

profile of v2, /device:TPU:0, one launch (start us, length us, event | category | flops | bytes accessed | tf_op | source)
XLA Modules:
  0.0 123.6 jit_solution(9019079855485903659)
XLA Ops:
  0.0 0.7 add_add_fusion
  0.7 0.7 add_add_fusion.1.code_ref
  1.4 3.0 %collective-permute-start = (s32[64]{0:T(128)S(1)}, s32[64]{0:T(128)S(1)}, u32[]{:S(2)}, u32[]{:S(2)}) collective-permute-start(s32[64]{0:T(128)S(1)} %add_add_fusion.1.code_ref), channel_id=1, source_target_pairs={{0,2},{1,3},{2,0},{3,1},{4,6},{5,7},{6,4},{7,5},{8,10},{9,11},{10,... | collective-permute-start | bytes 776 | tf_op jit(solution)/shard_map/ppermute | solution.py:28
  4.4 1.5 %collective-permute-start.1 = (s32[64]{0:T(128)S(1)}, s32[64]{0:T(128)S(1)}, u32[]{:S(2)}, u32[]{:S(2)}) collective-permute-start(s32[64]{0:T(128)S(1)} %get-tuple-element.29.code_ref), channel_id=1, source_target_pairs={{0,1},{1,0},{2,3},{3,2},{4,5},{5,4},{6,7},{7,6},{8,9},{9,8},{10,11... | collective-permute-start | bytes 776 | tf_op jit(solution)/shard_map/ppermute | solution.py:28
  5.9 0.0 collective-permute-done.refs_0_.partner_ref
  5.9 2.0 %collective-permute-done.1.refs_1_.partner_ref = s32[64]{0:T(128)S(1)} collective-permute-done((s32[64]{0:T(128)S(1)}, s32[64]{0:T(128)S(1)}, u32[]{:S(2)}, u32[]{:S(2)}) %collective-permute-start.1) | collective-permute-done | bytes 288 | tf_op jit(solution)/shard_map/ppermute | solution.py:28
  7.9 0.5 copy-done.4
  8.5 3.6 %pick.4.refs_0_ = bf16[48,16,4,128]{3,2,1,0:T(4,128)(2,1)} custom-call(s32[64]{0:T(128)} %copy-done.2, bf16[64,16,4,4,128]{4,3,2,1,0:T(4,128)(2,1)} %bitcast.46, s32[64]{0:T(128)} %copy-done.8, s32[64]{0:T(128)} %copy-done.4), custom_call_target="tpu_custom_call" | custom-call | flops 1 | bytes 1 | tf_op jit(solution)/shard_map/pick/pallas_call | solution.py:67
  12.1 1.5 %collective-permute-start.3 = (bf16[48,16,4,128]{3,2,1,0:T(4,128)(2,1)}, bf16[48,16,4,128]{3,2,1,0:T(4,128)(2,1)S(1)}, u32[]{:S(2)}, u32[]{:S(2)}) collective-permute-start(bf16[48,16,4,128]{3,2,1,0:T(4,128)(2,1)} %pick.4.refs_0_), channel_id=1, source_target_pairs={{0,1},{1,0},{2,3},{3,2},{4,5},{5,4},{6,7},{7,6},{8,9},{9,8},{10,11... | collective-permute-start | bytes 2359304 | tf_op jit(solution)/shard_map/ppermute | solution.py:28
  13.6 3.6 %pick.5.refs_0_ = bf16[48,16,4,128]{3,2,1,0:T(4,128)(2,1)} custom-call(s32[64]{0:T(128)} %copy-done.6, bf16[64,16,4,4,128]{4,3,2,1,0:T(4,128)(2,1)} %bitcast.47, bf16[48,16,4,128]{3,2,1,0:T(4,128)(2,1)} %pick.4.refs_0_), custom_call_target="tpu_custom_call" | custom-call | flops 1 | bytes 1 | tf_op jit(solution)/shard_map/pick/pallas_call | solution.py:67
  17.2 0.4 collective-permute-start.2
  17.6 3.6 %pick.6.token_ref.refs_0_ = bf16[48,16,4,128]{3,2,1,0:T(4,128)(2,1)} custom-call(s32[64]{0:T(128)} %copy-done.2, bf16[64,16,4,4,128]{4,3,2,1,0:T(4,128)(2,1)} %bitcast.48, bf16[48,16,4,128]{3,2,1,0:T(4,128)(2,1)} %pick.5.refs_0_), custom_call_target="tpu_custom_call" | custom-call | flops 1 | bytes 1 | tf_op jit(solution)/shard_map/pick/pallas_call | solution.py:67
  21.2 0.2 collective-permute-start.7
  21.4 3.6 %pick.7.refs_2_ = bf16[48,16,4,128]{3,2,1,0:T(4,128)(2,1)} custom-call(s32[64]{0:T(128)} %copy-done.2, bf16[64,16,4,4,128]{4,3,2,1,0:T(4,128)(2,1)} %bitcast.49, bf16[48,16,4,128]{3,2,1,0:T(4,128)(2,1)} %pick.6.token_ref.refs_0_), custom_call_target="tpu_custom_call" | custom-call | flops 1 | bytes 1 | tf_op jit(solution)/shard_map/pick/pallas_call | solution.py:67
  25.1 1.9 %collective-permute-start.13 = (bf16[48,16,4,128]{3,2,1,0:T(4,128)(2,1)}, bf16[48,16,4,128]{3,2,1,0:T(4,128)(2,1)S(1)}, u32[]{:S(2)}, u32[]{:S(2)}) collective-permute-start(bf16[48,16,4,128]{3,2,1,0:T(4,128)(2,1)} %pick.7.refs_2_), channel_id=1, source_target_pairs={{0,1},{1,0},{2,3},{3,2},{4,5},{5,4},{6,7},{7,6},{8,9},{9,8},{10,11... | collective-permute-start | bytes 2359304 | tf_op jit(solution)/shard_map/ppermute | solution.py:28
  27.0 5.8 %collective-permute-done.3.got_ref = bf16[48,16,4,128]{3,2,1,0:T(4,128)(2,1)S(1)} collective-permute-done((bf16[48,16,4,128]{3,2,1,0:T(4,128)(2,1)}, bf16[48,16,4,128]{3,2,1,0:T(4,128)(2,1)S(1)}, u32[]{:S(2)}, u32[]{:S(2)}) %collective-permute-start.3) | collective-permute-done | bytes 786464 | tf_op jit(solution)/shard_map/ppermute | solution.py:28
  32.8 4.2 %deposit.4 = (bf16[1,4,256,128]{3,2,1,0:T(8,128)(2,1)S(1)}, bf16[1,4,256,128]{3,2,1,0:T(8,128)(2,1)S(1)}, f32[2,4,256,128]{3,2,1,0:T(8,128)S(1)}) custom-call(s32[64]{0:T(128)S(1)} %copy-done.3, s32[64]{0:T(128)S(1)} %copy-done.5, bf16[64,16,4,4,128]{4,3,2,1,0:T(4,128)(2,1)} %bitcast.50, bf16[48,16,4,128]{3,2,1,0:T(4,128)(2,1)S(1)} %collective-permute-done.3.got_ref, ...), custom_call_target="tpu_custom_call" | custom-call | flops 1 | bytes 1 | tf_op jit(solution)/shard_map/deposit/pallas_call | solution.py:152
  37.0 0.1 collective-permute-start.4
  37.1 2.0 %collective-permute-start.10 = (bf16[1,4,256,128]{3,2,1,0:T(8,128)(2,1)S(1)}, bf16[1,4,256,128]{3,2,1,0:T(8,128)(2,1)S(1)}, u32[]{:S(2)}, u32[]{:S(2)}) collective-permute-start(bf16[1,4,256,128]{3,2,1,0:T(8,128)(2,1)S(1)} %get-tuple-element.25), channel_id=1, source_target_pairs={{0,2},{1,3},{2,0},{3,1},{4,6},{5,7},{6,4},{7,5},{8,10},{9,11},{10,... | collective-permute-start | bytes 786440 | tf_op jit(solution)/shard_map/ppermute | solution.py:28
  39.1 7.1 %collective-permute-done.4.refs_1_ = bf16[1,4,256,128]{3,2,1,0:T(8,128)(2,1)S(1)} collective-permute-done((bf16[1,4,256,128]{3,2,1,0:T(8,128)(2,1)S(1)}, bf16[1,4,256,128]{3,2,1,0:T(8,128)(2,1)S(1)}, u32[]{:S(2)}, u32[]{:S(2)}) %collective-permute-start.4) | collective-permute-done | bytes 262176 | tf_op jit(solution)/shard_map/ppermute | solution.py:28
  46.2 0.1 merge.8.token_ref
  46.3 2.6 %collective-permute-start.11 = (bf16[1,4,256,128]{3,2,1,0:T(8,128)(2,1)S(1)}, bf16[1,4,256,128]{3,2,1,0:T(8,128)(2,1)S(1)}, u32[]{:S(2)}, u32[]{:S(2)}) collective-permute-start(bf16[1,4,256,128]{3,2,1,0:T(8,128)(2,1)S(1)} %merge.8.token_ref), channel_id=1, source_target_pairs={{0,4},{1,5},{2,6},{3,7},{4,0},{5,1},{6,2},{7,3},{8,12},{9,13},{10,... | collective-permute-start | bytes 786440 | tf_op jit(solution)/shard_map/ppermute | solution.py:28
  48.9 0.0 collective-permute-done.2.got_ref
  48.9 4.2 %deposit.5 = (bf16[1,4,256,128]{3,2,1,0:T(8,128)(2,1)S(1)}, bf16[1,4,256,128]{3,2,1,0:T(8,128)(2,1)S(1)}, f32[2,4,256,128]{3,2,1,0:T(8,128)S(1)}) custom-call(s32[64]{0:T(128)S(1)} %copy-done.7, s32[64]{0:T(128)S(1)} %copy-done.9, bf16[64,16,4,4,128]{4,3,2,1,0:T(4,128)(2,1)} %bitcast.51, bf16[48,16,4,128]{3,2,1,0:T(4,128)(2,1)S(1)} %collective-permute-done.2.got_ref, ...), custom_call_target="tpu_custom_call" | custom-call | flops 1 | bytes 1 | tf_op jit(solution)/shard_map/deposit/pallas_call | solution.py:152
  53.1 4.2 %deposit.6 = (bf16[1,4,256,128]{3,2,1,0:T(8,128)(2,1)S(1)}, bf16[1,4,256,128]{3,2,1,0:T(8,128)(2,1)S(1)}, f32[2,4,256,128]{3,2,1,0:T(8,128)S(1)}) custom-call(s32[64]{0:T(128)S(1)} %copy-done.3, s32[64]{0:T(128)S(1)} %copy-done.5, bf16[64,16,4,4,128]{4,3,2,1,0:T(4,128)(2,1)} %bitcast.52, bf16[48,16,4,128]{3,2,1,0:T(4,128)(2,1)S(1)} %collective-permute-done.7.got_ref, ...), custom_call_target="tpu_custom_call" | custom-call | flops 1 | bytes 1 | tf_op jit(solution)/shard_map/deposit/pallas_call | solution.py:152
  57.4 0.5 collective-permute-start.9
  57.9 1.6 %collective-permute-start.8 = (bf16[1,4,256,128]{3,2,1,0:T(8,128)(2,1)S(1)}, bf16[1,4,256,128]{3,2,1,0:T(8,128)(2,1)S(1)}, u32[]{:S(2)}, u32[]{:S(2)}) collective-permute-start(bf16[1,4,256,128]{3,2,1,0:T(8,128)(2,1)S(1)} %get-tuple-element.23), channel_id=1, source_target_pairs={{0,2},{1,3},{2,0},{3,1},{4,6},{5,7},{6,4},{7,5},{8,10},{9,11},{10,... | collective-permute-start | bytes 786440 | tf_op jit(solution)/shard_map/ppermute | solution.py:28
  59.4 0.0 collective-permute-done.10.refs_1_
  59.5 0.1 merge.9.refs_2_
  59.5 6.9 %collective-permute-done.9.refs_1_ = bf16[1,4,256,128]{3,2,1,0:T(8,128)(2,1)S(1)} collective-permute-done((bf16[1,4,256,128]{3,2,1,0:T(8,128)(2,1)S(1)}, bf16[1,4,256,128]{3,2,1,0:T(8,128)(2,1)S(1)}, u32[]{:S(2)}, u32[]{:S(2)}) %collective-permute-start.9) | collective-permute-done | bytes 262176 | tf_op jit(solution)/shard_map/ppermute | solution.py:28
  66.5 0.1 collective-permute-start.12
  66.6 1.6 %collective-permute-start.6 = (bf16[1,4,256,128]{3,2,1,0:T(8,128)(2,1)S(1)}, bf16[1,4,256,128]{3,2,1,0:T(8,128)(2,1)S(1)}, u32[]{:S(2)}, u32[]{:S(2)}) collective-permute-start(bf16[1,4,256,128]{3,2,1,0:T(8,128)(2,1)S(1)} %get-tuple-element.21.token_ref), channel_id=1, source_target_pairs={{0,1},{1,0},{2,3},{3,2},{4,5},{5,4},{6,7},{7,6},{8,9},{9,8},{10,11... | collective-permute-start | bytes 786440 | tf_op jit(solution)/shard_map/ppermute | solution.py:28
  68.2 4.4 %deposit.7 = (bf16[1,4,256,128]{3,2,1,0:T(8,128)(2,1)S(1)}, bf16[1,4,256,128]{3,2,1,0:T(8,128)(2,1)S(1)}, f32[2,4,256,128]{3,2,1,0:T(8,128)S(1)}) custom-call(s32[64]{0:T(128)S(1)} %copy-done.3, s32[64]{0:T(128)S(1)} %copy-done.5, bf16[64,16,4,4,128]{4,3,2,1,0:T(4,128)(2,1)} %bitcast.53, bf16[48,16,4,128]{3,2,1,0:T(4,128)(2,1)S(1)} %collective-permute-done.13.got_ref, ...), custom_call_target="tpu_custom_call" | custom-call | flops 1 | bytes 1 | tf_op jit(solution)/shard_map/deposit/pallas_call | solution.py:152
  72.6 0.1 collective-permute-start.15
  72.7 0.6 collective-permute-start.5
  73.3 0.0 collective-permute-done.8.refs_1_
  73.3 8.5 %collective-permute-done.12.refs_2_ = bf16[1,4,256,128]{3,2,1,0:T(8,128)(2,1)S(1)} collective-permute-done((bf16[1,4,256,128]{3,2,1,0:T(8,128)(2,1)S(1)}, bf16[1,4,256,128]{3,2,1,0:T(8,128)(2,1)S(1)}, u32[]{:S(2)}, u32[]{:S(2)}) %collective-permute-start.12) | collective-permute-done | bytes 262176 | tf_op jit(solution)/shard_map/ppermute | solution.py:28
  81.7 0.1 merge.11.refs_2_
  81.8 0.0 copy-start.10
  81.8 0.0 collective-permute-done.6.refs_1_
  81.9 0.1 collective-permute-start.14
  82.0 0.1 collective-permute-start.16
  82.1 1.6 %collective-permute-start.23 = (bf16[4,256,128]{2,1,0:T(8,128)(2,1)S(1)}, bf16[4,256,128]{2,1,0:T(8,128)(2,1)S(1)}, u32[]{:S(2)}, u32[]{:S(2)}) collective-permute-start(bf16[4,256,128]{2,1,0:T(8,128)(2,1)S(1)} %bitcast.34), channel_id=1, source_target_pairs={{0,16},{8,24},{16,0},{24,8},{1,17},{9,25},{17,1},{25,9},{2,18},{10... | collective-permute-start | bytes 786440 | tf_op jit(solution)/shard_map/ppermute | solution.py:28
  83.6 2.3 %collective-permute-done.15.refs_1_ = bf16[1,4,256,128]{3,2,1,0:T(8,128)(2,1)S(1)} collective-permute-done((bf16[1,4,256,128]{3,2,1,0:T(8,128)(2,1)S(1)}, bf16[1,4,256,128]{3,2,1,0:T(8,128)(2,1)S(1)}, u32[]{:S(2)}, u32[]{:S(2)}) %collective-permute-start.15) | collective-permute-done | bytes 262176 | tf_op jit(solution)/shard_map/ppermute | solution.py:28
  86.0 0.5 collective-permute-start.17
  86.5 9.1 %collective-permute-done.14.refs_2_ = bf16[1,4,256,128]{3,2,1,0:T(8,128)(2,1)S(1)} collective-permute-done((bf16[1,4,256,128]{3,2,1,0:T(8,128)(2,1)S(1)}, bf16[1,4,256,128]{3,2,1,0:T(8,128)(2,1)S(1)}, u32[]{:S(2)}, u32[]{:S(2)}) %collective-permute-start.14) | collective-permute-done | bytes 262176 | tf_op jit(solution)/shard_map/ppermute | solution.py:28
  95.7 1.5 %collective-permute-start.24 = (bf16[4,256,128]{2,1,0:T(8,128)(2,1)S(1)}, bf16[4,256,128]{2,1,0:T(8,128)(2,1)S(1)}, u32[]{:S(2)}, u32[]{:S(2)}) collective-permute-start(bf16[4,256,128]{2,1,0:T(8,128)(2,1)S(1)} %bitcast.37), channel_id=1, source_target_pairs={{0,16},{8,24},{16,0},{24,8},{1,17},{9,25},{17,1},{25,9},{2,18},{10... | collective-permute-start | bytes 786440 | tf_op jit(solution)/shard_map/ppermute | solution.py:28
  97.2 0.1 merge.14.refs_3_
  97.3 0.1 collective-permute-start.20
  97.3 0.5 collective-permute-start.27
  97.8 0.6 collective-permute-done.17.refs_2_
  98.5 0.1 merge.15
  98.6 1.6 %collective-permute-start.25 = (bf16[4,256,128]{2,1,0:T(8,128)(2,1)S(1)}, bf16[4,256,128]{2,1,0:T(8,128)(2,1)S(1)}, u32[]{:S(2)}, u32[]{:S(2)}) collective-permute-start(bf16[4,256,128]{2,1,0:T(8,128)(2,1)S(1)} %bitcast.43), channel_id=1, source_target_pairs={{0,16},{8,24},{16,0},{24,8},{1,17},{9,25},{17,1},{25,9},{2,18},{10... | collective-permute-start | bytes 786440 | tf_op jit(solution)/shard_map/ppermute | solution.py:28
  100.1 0.5 collective-permute-start.22
  100.7 2.8 %collective-permute-done.24.refs_10_ = bf16[4,256,128]{2,1,0:T(8,128)(2,1)S(1)} collective-permute-done((bf16[4,256,128]{2,1,0:T(8,128)(2,1)S(1)}, bf16[4,256,128]{2,1,0:T(8,128)(2,1)S(1)}, u32[]{:S(2)}, u32[]{:S(2)}) %collective-permute-start.24) | collective-permute-done | bytes 262176 | tf_op jit(solution)/shard_map/ppermute | solution.py:28
  103.5 0.5 collective-permute-start.18
  104.0 0.1 collective-permute-start.28
  104.1 5.0 %collective-permute-done.25.refs_11_ = bf16[4,256,128]{2,1,0:T(8,128)(2,1)S(1)} collective-permute-done((bf16[4,256,128]{2,1,0:T(8,128)(2,1)S(1)}, bf16[4,256,128]{2,1,0:T(8,128)(2,1)S(1)}, u32[]{:S(2)}, u32[]{:S(2)}) %collective-permute-start.25) | collective-permute-done | bytes 262176 | tf_op jit(solution)/shard_map/ppermute | solution.py:28
  109.1 4.2 %collective-permute-done.22.refs_8_ = bf16[4,256,128]{2,1,0:T(8,128)(2,1)S(1)} collective-permute-done((bf16[4,256,128]{2,1,0:T(8,128)(2,1)S(1)}, bf16[4,256,128]{2,1,0:T(8,128)(2,1)S(1)}, u32[]{:S(2)}, u32[]{:S(2)}) %collective-permute-start.22) | collective-permute-done | bytes 262176 | tf_op jit(solution)/shard_map/ppermute | solution.py:28
  113.3 0.1 fusion
  113.4 0.1 copy.7
  113.4 0.1 reshape.11.pairs_ref
  113.6 1.4 %collective-permute-done.26.refs_12_ = bf16[4,256,128]{2,1,0:T(8,128)(2,1)} collective-permute-done((bf16[4,256,128]{2,1,0:T(8,128)(2,1)S(1)}, bf16[4,256,128]{2,1,0:T(8,128)(2,1)}, u32[]{:S(2)}, u32[]{:S(2)}) %collective-permute-start.26) | collective-permute-done | bytes 262176 | tf_op jit(solution)/shard_map/ppermute | solution.py:28
  114.9 8.5 %coherence.1 = f32[256,8,256]{2,1,0:T(8,128)} custom-call(s32[16]{0:T(128)S(1)} %reshape.11.pairs_ref, bf16[4,256,128]{2,1,0:T(8,128)(2,1)S(1)} %bitcast.42, bf16[4,256,128]{2,1,0:T(8,128)(2,1)S(1)} %bitcast.36, bf16[4,256,128]{2,1,0:T(8,128)(2,1)S(1)} %bitcast.39, bf16[4,256,128]{2,1,0:T(8,128)(2,1)S(1)} %bitcast.45, ...), custom_call_target="tpu_custom_call" | custom-call | tf_op jit(solution)/shard_map/coherence/pallas_call | solution.py:268
  (40 shorter events, 0.2 us)
Async XLA Ops:
  0.7 7.2 %copy-start.2 = (s32[64]{0:T(128)}, s32[64]{0:T(128)S(1)}, u32[]{:S(2)}) copy-start(s32[64]{0:T(128)S(1)} %get-tuple-element.29.code_ref) | copy-start | bytes 772
  1.4 12.2 %copy-start.6 = (s32[64]{0:T(128)}, s32[64]{0:T(128)S(1)}, u32[]{:S(2)}) copy-start(s32[64]{0:T(128)S(1)} %add_add_fusion.1.code_ref) | copy-start | bytes 772
  1.4 4.5 %collective-permute-start = (s32[64]{0:T(128)S(1)}, s32[64]{0:T(128)S(1)}, u32[]{:S(2)}, u32[]{:S(2)}) collective-permute-start(s32[64]{0:T(128)S(1)} %add_add_fusion.1.code_ref), channel_id=1, source_target_pairs={{0,2},{1,3},{2,0},{3,1},{4,6},{5,7},{6,4},{7,5},{8,10},{9,11},{10,... | collective-permute-start | bytes 776 | tf_op jit(solution)/shard_map/ppermute | solution.py:28
  4.4 3.5 %collective-permute-start.1 = (s32[64]{0:T(128)S(1)}, s32[64]{0:T(128)S(1)}, u32[]{:S(2)}, u32[]{:S(2)}) collective-permute-start(s32[64]{0:T(128)S(1)} %get-tuple-element.29.code_ref), channel_id=1, source_target_pairs={{0,1},{1,0},{2,3},{3,2},{4,5},{5,4},{6,7},{7,6},{8,9},{9,8},{10,11... | collective-permute-start | bytes 776 | tf_op jit(solution)/shard_map/ppermute | solution.py:28
  5.9 2.0 %copy-start.8 = (s32[64]{0:T(128)}, s32[64]{0:T(128)S(1)}, u32[]{:S(2)}) copy-start(s32[64]{0:T(128)S(1)} %collective-permute-done.refs_0_.partner_ref) | copy-start | bytes 772
  7.9 0.5 copy-start.4
  12.1 20.7 %collective-permute-start.3 = (bf16[48,16,4,128]{3,2,1,0:T(4,128)(2,1)}, bf16[48,16,4,128]{3,2,1,0:T(4,128)(2,1)S(1)}, u32[]{:S(2)}, u32[]{:S(2)}) collective-permute-start(bf16[48,16,4,128]{3,2,1,0:T(4,128)(2,1)} %pick.4.refs_0_), channel_id=1, source_target_pairs={{0,1},{1,0},{2,3},{3,2},{4,5},{5,4},{6,7},{7,6},{8,9},{9,8},{10,11... | collective-permute-start | bytes 2359304 | tf_op jit(solution)/shard_map/ppermute | solution.py:28
  17.2 31.7 %collective-permute-start.2 = (bf16[48,16,4,128]{3,2,1,0:T(4,128)(2,1)}, bf16[48,16,4,128]{3,2,1,0:T(4,128)(2,1)S(1)}, u32[]{:S(2)}, u32[]{:S(2)}) collective-permute-start(bf16[48,16,4,128]{3,2,1,0:T(4,128)(2,1)} %pick.5.refs_0_), channel_id=1, source_target_pairs={{0,2},{1,3},{2,0},{3,1},{4,6},{5,7},{6,4},{7,5},{8,10},{9,11},{10,... | collective-permute-start | bytes 2359304 | tf_op jit(solution)/shard_map/ppermute | solution.py:28
  21.2 11.5 %copy-start = (bf16[48,16,4,128]{3,2,1,0:T(4,128)(2,1)S(1)}, bf16[48,16,4,128]{3,2,1,0:T(4,128)(2,1)}, u32[]{:S(2)}) copy-start(bf16[48,16,4,128]{3,2,1,0:T(4,128)(2,1)} %pick.6.token_ref.refs_0_) | copy-start | bytes 2359300
  21.2 11.5 %copy-start.3 = (s32[64]{0:T(128)S(1)}, s32[64]{0:T(128)}, u32[]{:S(2)}) copy-start(s32[64]{0:T(128)} %copy-done.2) | copy-start | bytes 772
  21.2 11.5 %copy-start.5 = (s32[64]{0:T(128)S(1)}, s32[64]{0:T(128)}, u32[]{:S(2)}) copy-start(s32[64]{0:T(128)} %copy-done.4) | copy-start | bytes 772
  21.2 31.9 %collective-permute-start.7 = (bf16[48,16,4,128]{3,2,1,0:T(4,128)(2,1)}, bf16[48,16,4,128]{3,2,1,0:T(4,128)(2,1)S(1)}, u32[]{:S(2)}, u32[]{:S(2)}) collective-permute-start(bf16[48,16,4,128]{3,2,1,0:T(4,128)(2,1)} %pick.6.token_ref.refs_0_), channel_id=1, source_target_pairs={{0,1},{1,0},{2,3},{3,2},{4,5},{5,4},{6,7},{7,6},{8,9},{9,8},{10,11... | collective-permute-start | bytes 2359304 | tf_op jit(solution)/shard_map/ppermute | solution.py:28
  25.0 21.1 %copy-start.1 = (bf16[48,16,4,128]{3,2,1,0:T(4,128)(2,1)S(1)}, bf16[48,16,4,128]{3,2,1,0:T(4,128)(2,1)}, u32[]{:S(2)}) copy-start(bf16[48,16,4,128]{3,2,1,0:T(4,128)(2,1)} %pick.7.refs_2_) | copy-start | bytes 2359300
  25.1 23.8 %copy-start.7 = (s32[64]{0:T(128)S(1)}, s32[64]{0:T(128)}, u32[]{:S(2)}) copy-start(s32[64]{0:T(128)} %copy-done.6) | copy-start | bytes 772
  25.1 23.8 %copy-start.9 = (s32[64]{0:T(128)S(1)}, s32[64]{0:T(128)}, u32[]{:S(2)}) copy-start(s32[64]{0:T(128)} %copy-done.8) | copy-start | bytes 772
  25.1 43.1 %collective-permute-start.13 = (bf16[48,16,4,128]{3,2,1,0:T(4,128)(2,1)}, bf16[48,16,4,128]{3,2,1,0:T(4,128)(2,1)S(1)}, u32[]{:S(2)}, u32[]{:S(2)}) collective-permute-start(bf16[48,16,4,128]{3,2,1,0:T(4,128)(2,1)} %pick.7.refs_2_), channel_id=1, source_target_pairs={{0,1},{1,0},{2,3},{3,2},{4,5},{5,4},{6,7},{7,6},{8,9},{9,8},{10,11... | collective-permute-start | bytes 2359304 | tf_op jit(solution)/shard_map/ppermute | solution.py:28
  37.0 9.2 %collective-permute-start.4 = (bf16[1,4,256,128]{3,2,1,0:T(8,128)(2,1)S(1)}, bf16[1,4,256,128]{3,2,1,0:T(8,128)(2,1)S(1)}, u32[]{:S(2)}, u32[]{:S(2)}) collective-permute-start(bf16[1,4,256,128]{3,2,1,0:T(8,128)(2,1)S(1)} %get-tuple-element.18), channel_id=1, source_target_pairs={{0,2},{1,3},{2,0},{3,1},{4,6},{5,7},{6,4},{7,5},{8,10},{9,11},{10,... | collective-permute-start | bytes 786440 | tf_op jit(solution)/shard_map/ppermute | solution.py:28
  37.1 22.4 %collective-permute-start.10 = (bf16[1,4,256,128]{3,2,1,0:T(8,128)(2,1)S(1)}, bf16[1,4,256,128]{3,2,1,0:T(8,128)(2,1)S(1)}, u32[]{:S(2)}, u32[]{:S(2)}) collective-permute-start(bf16[1,4,256,128]{3,2,1,0:T(8,128)(2,1)S(1)} %get-tuple-element.25), channel_id=1, source_target_pairs={{0,2},{1,3},{2,0},{3,1},{4,6},{5,7},{6,4},{7,5},{8,10},{9,11},{10,... | collective-permute-start | bytes 786440 | tf_op jit(solution)/shard_map/ppermute | solution.py:28
  46.3 13.2 %collective-permute-start.11 = (bf16[1,4,256,128]{3,2,1,0:T(8,128)(2,1)S(1)}, bf16[1,4,256,128]{3,2,1,0:T(8,128)(2,1)S(1)}, u32[]{:S(2)}, u32[]{:S(2)}) collective-permute-start(bf16[1,4,256,128]{3,2,1,0:T(8,128)(2,1)S(1)} %merge.8.token_ref), channel_id=1, source_target_pairs={{0,4},{1,5},{2,6},{3,7},{4,0},{5,1},{6,2},{7,3},{8,12},{9,13},{10,... | collective-permute-start | bytes 786440 | tf_op jit(solution)/shard_map/ppermute | solution.py:28
  57.4 9.1 %collective-permute-start.9 = (bf16[1,4,256,128]{3,2,1,0:T(8,128)(2,1)S(1)}, bf16[1,4,256,128]{3,2,1,0:T(8,128)(2,1)S(1)}, u32[]{:S(2)}, u32[]{:S(2)}) collective-permute-start(bf16[1,4,256,128]{3,2,1,0:T(8,128)(2,1)S(1)} %get-tuple-element.24.refs_3_), channel_id=1, source_target_pairs={{0,2},{1,3},{2,0},{3,1},{4,6},{5,7},{6,4},{7,5},{8,10},{9,11},{10,... | collective-permute-start | bytes 786440 | tf_op jit(solution)/shard_map/ppermute | solution.py:28
  57.9 15.4 %collective-permute-start.8 = (bf16[1,4,256,128]{3,2,1,0:T(8,128)(2,1)S(1)}, bf16[1,4,256,128]{3,2,1,0:T(8,128)(2,1)S(1)}, u32[]{:S(2)}, u32[]{:S(2)}) collective-permute-start(bf16[1,4,256,128]{3,2,1,0:T(8,128)(2,1)S(1)} %get-tuple-element.23), channel_id=1, source_target_pairs={{0,2},{1,3},{2,0},{3,1},{4,6},{5,7},{6,4},{7,5},{8,10},{9,11},{10,... | collective-permute-start | bytes 786440 | tf_op jit(solution)/shard_map/ppermute | solution.py:28
  66.5 15.2 %collective-permute-start.12 = (bf16[1,4,256,128]{3,2,1,0:T(8,128)(2,1)S(1)}, bf16[1,4,256,128]{3,2,1,0:T(8,128)(2,1)S(1)}, u32[]{:S(2)}, u32[]{:S(2)}) collective-permute-start(bf16[1,4,256,128]{3,2,1,0:T(8,128)(2,1)S(1)} %merge.10.token_ref), channel_id=1, source_target_pairs={{0,4},{1,5},{2,6},{3,7},{4,0},{5,1},{6,2},{7,3},{8,12},{9,13},{10,... | collective-permute-start | bytes 786440 | tf_op jit(solution)/shard_map/ppermute | solution.py:28
  66.6 15.2 %collective-permute-start.6 = (bf16[1,4,256,128]{3,2,1,0:T(8,128)(2,1)S(1)}, bf16[1,4,256,128]{3,2,1,0:T(8,128)(2,1)S(1)}, u32[]{:S(2)}, u32[]{:S(2)}) collective-permute-start(bf16[1,4,256,128]{3,2,1,0:T(8,128)(2,1)S(1)} %get-tuple-element.21.token_ref), channel_id=1, source_target_pairs={{0,1},{1,0},{2,3},{3,2},{4,5},{5,4},{6,7},{7,6},{8,9},{9,8},{10,11... | collective-permute-start | bytes 786440 | tf_op jit(solution)/shard_map/ppermute | solution.py:28
  72.6 13.4 %collective-permute-start.15 = (bf16[1,4,256,128]{3,2,1,0:T(8,128)(2,1)S(1)}, bf16[1,4,256,128]{3,2,1,0:T(8,128)(2,1)S(1)}, u32[]{:S(2)}, u32[]{:S(2)}) collective-permute-start(bf16[1,4,256,128]{3,2,1,0:T(8,128)(2,1)S(1)} %get-tuple-element.26.refs_3_), channel_id=1, source_target_pairs={{0,2},{1,3},{2,0},{3,1},{4,6},{5,7},{6,4},{7,5},{8,10},{9,11},{10,... | collective-permute-start | bytes 786440 | tf_op jit(solution)/shard_map/ppermute | solution.py:28
  72.7 13.9 %collective-permute-start.5 = (bf16[1,4,256,128]{3,2,1,0:T(8,128)(2,1)S(1)}, bf16[1,4,256,128]{3,2,1,0:T(8,128)(2,1)S(1)}, u32[]{:S(2)}, u32[]{:S(2)}) collective-permute-start(bf16[1,4,256,128]{3,2,1,0:T(8,128)(2,1)S(1)} %get-tuple-element.20), channel_id=1, source_target_pairs={{0,1},{1,0},{2,3},{3,2},{4,5},{5,4},{6,7},{7,6},{8,9},{9,8},{10,11... | collective-permute-start | bytes 786440 | tf_op jit(solution)/shard_map/ppermute | solution.py:28
  81.8 31.4 %copy-start.10 = (s32[32,2]{0,1:T(2,128)S(1)}, s32[32,2]{0,1:T(2,128)}, u32[]{:S(2)}) copy-start(s32[32,2]{0,1:T(2,128)} %param.7) | copy-start | bytes 772
  81.9 13.8 %collective-permute-start.14 = (bf16[1,4,256,128]{3,2,1,0:T(8,128)(2,1)S(1)}, bf16[1,4,256,128]{3,2,1,0:T(8,128)(2,1)S(1)}, u32[]{:S(2)}, u32[]{:S(2)}) collective-permute-start(bf16[1,4,256,128]{3,2,1,0:T(8,128)(2,1)S(1)} %merge.12.refs_2_), channel_id=1, source_target_pairs={{0,4},{1,5},{2,6},{3,7},{4,0},{5,1},{6,2},{7,3},{8,12},{9,13},{10,... | collective-permute-start | bytes 786440 | tf_op jit(solution)/shard_map/ppermute | solution.py:28
  82.0 15.3 %collective-permute-start.16 = (bf16[1,4,256,128]{3,2,1,0:T(8,128)(2,1)S(1)}, bf16[1,4,256,128]{3,2,1,0:T(8,128)(2,1)S(1)}, u32[]{:S(2)}, u32[]{:S(2)}) collective-permute-start(bf16[1,4,256,128]{3,2,1,0:T(8,128)(2,1)S(1)} %get-tuple-element.28), channel_id=1, source_target_pairs={{0,2},{1,3},{2,0},{3,1},{4,6},{5,7},{6,4},{7,5},{8,10},{9,11},{10,... | collective-permute-start | bytes 786440 | tf_op jit(solution)/shard_map/ppermute | solution.py:28
  82.1 15.3 %collective-permute-start.23 = (bf16[4,256,128]{2,1,0:T(8,128)(2,1)S(1)}, bf16[4,256,128]{2,1,0:T(8,128)(2,1)S(1)}, u32[]{:S(2)}, u32[]{:S(2)}) collective-permute-start(bf16[4,256,128]{2,1,0:T(8,128)(2,1)S(1)} %bitcast.34), channel_id=1, source_target_pairs={{0,16},{8,24},{16,0},{24,8},{1,17},{9,25},{17,1},{25,9},{2,18},{10... | collective-permute-start | bytes 786440 | tf_op jit(solution)/shard_map/ppermute | solution.py:28
  86.0 12.4 %collective-permute-start.17 = (bf16[1,4,256,128]{3,2,1,0:T(8,128)(2,1)S(1)}, bf16[1,4,256,128]{3,2,1,0:T(8,128)(2,1)S(1)}, u32[]{:S(2)}, u32[]{:S(2)}) collective-permute-start(bf16[1,4,256,128]{3,2,1,0:T(8,128)(2,1)S(1)} %merge.13.refs_3_), channel_id=1, source_target_pairs={{0,4},{1,5},{2,6},{3,7},{4,0},{5,1},{6,2},{7,3},{8,12},{9,13},{10,... | collective-permute-start | bytes 786440 | tf_op jit(solution)/shard_map/ppermute | solution.py:28
  86.5 13.6 %collective-permute-start.19 = (bf16[4,256,128]{2,1,0:T(8,128)(2,1)S(1)}, bf16[4,256,128]{2,1,0:T(8,128)(2,1)S(1)}, u32[]{:S(2)}, u32[]{:S(2)}) collective-permute-start(bf16[4,256,128]{2,1,0:T(8,128)(2,1)S(1)} %bitcast.35), channel_id=1, source_target_pairs={{0,8},{8,0},{16,24},{24,16},{1,9},{9,1},{17,25},{25,17},{2,10},{10... | collective-permute-start | bytes 786440 | tf_op jit(solution)/shard_map/ppermute | solution.py:28
  95.7 7.8 %collective-permute-start.24 = (bf16[4,256,128]{2,1,0:T(8,128)(2,1)S(1)}, bf16[4,256,128]{2,1,0:T(8,128)(2,1)S(1)}, u32[]{:S(2)}, u32[]{:S(2)}) collective-permute-start(bf16[4,256,128]{2,1,0:T(8,128)(2,1)S(1)} %bitcast.37), channel_id=1, source_target_pairs={{0,16},{8,24},{16,0},{24,8},{1,17},{9,25},{17,1},{25,9},{2,18},{10... | collective-permute-start | bytes 786440 | tf_op jit(solution)/shard_map/ppermute | solution.py:28
  97.3 6.2 %collective-permute-start.20 = (bf16[4,256,128]{2,1,0:T(8,128)(2,1)S(1)}, bf16[4,256,128]{2,1,0:T(8,128)(2,1)S(1)}, u32[]{:S(2)}, u32[]{:S(2)}) collective-permute-start(bf16[4,256,128]{2,1,0:T(8,128)(2,1)S(1)} %bitcast.38), channel_id=1, source_target_pairs={{0,8},{8,0},{16,24},{24,16},{1,9},{9,1},{17,25},{25,17},{2,10},{10... | collective-permute-start | bytes 786440 | tf_op jit(solution)/shard_map/ppermute | solution.py:28
  97.3 6.6 %collective-permute-start.27 = (bf16[4,256,128]{2,1,0:T(8,128)(2,1)S(1)}, bf16[4,256,128]{2,1,0:T(8,128)(2,1)S(1)}, u32[]{:S(2)}, u32[]{:S(2)}) collective-permute-start(bf16[4,256,128]{2,1,0:T(8,128)(2,1)S(1)} %collective-permute-done.23.refs_9_), channel_id=1, source_target_pairs={{0,8},{8,0},{16,24},{24,16},{1,9},{9,1},{17,25},{25,17},{2,10},{10... | collective-permute-start | bytes 786440 | tf_op jit(solution)/shard_map/ppermute | solution.py:28
  98.6 10.5 %collective-permute-start.25 = (bf16[4,256,128]{2,1,0:T(8,128)(2,1)S(1)}, bf16[4,256,128]{2,1,0:T(8,128)(2,1)S(1)}, u32[]{:S(2)}, u32[]{:S(2)}) collective-permute-start(bf16[4,256,128]{2,1,0:T(8,128)(2,1)S(1)} %bitcast.43), channel_id=1, source_target_pairs={{0,16},{8,24},{16,0},{24,8},{1,17},{9,25},{17,1},{25,9},{2,18},{10... | collective-permute-start | bytes 786440 | tf_op jit(solution)/shard_map/ppermute | solution.py:28
  100.1 13.1 %collective-permute-start.22 = (bf16[4,256,128]{2,1,0:T(8,128)(2,1)S(1)}, bf16[4,256,128]{2,1,0:T(8,128)(2,1)S(1)}, u32[]{:S(2)}, u32[]{:S(2)}) collective-permute-start(bf16[4,256,128]{2,1,0:T(8,128)(2,1)S(1)} %bitcast.40), channel_id=1, source_target_pairs={{0,16},{8,24},{16,0},{24,8},{1,17},{9,25},{17,1},{25,9},{2,18},{10... | collective-permute-start | bytes 786440 | tf_op jit(solution)/shard_map/ppermute | solution.py:28
  103.5 10.1 %collective-permute-start.21 = (bf16[4,256,128]{2,1,0:T(8,128)(2,1)S(1)}, bf16[4,256,128]{2,1,0:T(8,128)(2,1)S(1)}, u32[]{:S(2)}, u32[]{:S(2)}) collective-permute-start(bf16[4,256,128]{2,1,0:T(8,128)(2,1)S(1)} %bitcast.44), channel_id=1, source_target_pairs={{0,8},{8,0},{16,24},{24,16},{1,9},{9,1},{17,25},{25,17},{2,10},{10... | collective-permute-start | bytes 786440 | tf_op jit(solution)/shard_map/ppermute | solution.py:28
  103.5 10.1 %collective-permute-start.18 = (bf16[4,256,128]{2,1,0:T(8,128)(2,1)S(1)}, bf16[4,256,128]{2,1,0:T(8,128)(2,1)S(1)}, u32[]{:S(2)}, u32[]{:S(2)}) collective-permute-start(bf16[4,256,128]{2,1,0:T(8,128)(2,1)S(1)} %bitcast.41), channel_id=1, source_target_pairs={{0,8},{8,0},{16,24},{24,16},{1,9},{9,1},{17,25},{25,17},{2,10},{10... | collective-permute-start | bytes 786440 | tf_op jit(solution)/shard_map/ppermute | solution.py:28
  104.0 9.6 %collective-permute-start.28 = (bf16[4,256,128]{2,1,0:T(8,128)(2,1)S(1)}, bf16[4,256,128]{2,1,0:T(8,128)(2,1)}, u32[]{:S(2)}, u32[]{:S(2)}) collective-permute-start(bf16[4,256,128]{2,1,0:T(8,128)(2,1)S(1)} %collective-permute-done.24.refs_10_), channel_id=1, source_target_pairs={{0,8},{8,0},{16,24},{24,16},{1,9},{9,1},{17,25},{25,17},{2,10},{10... | collective-permute-start | bytes 786440 | tf_op jit(solution)/shard_map/ppermute | solution.py:28
  109.1 4.5 %collective-permute-start.29 = (bf16[4,256,128]{2,1,0:T(8,128)(2,1)S(1)}, bf16[4,256,128]{2,1,0:T(8,128)(2,1)}, u32[]{:S(2)}, u32[]{:S(2)}) collective-permute-start(bf16[4,256,128]{2,1,0:T(8,128)(2,1)S(1)} %collective-permute-done.25.refs_11_), channel_id=1, source_target_pairs={{0,8},{8,0},{16,24},{24,16},{1,9},{9,1},{17,25},{25,17},{2,10},{10... | collective-permute-start | bytes 786440 | tf_op jit(solution)/shard_map/ppermute | solution.py:28
  113.3 1.7 %collective-permute-start.26 = (bf16[4,256,128]{2,1,0:T(8,128)(2,1)S(1)}, bf16[4,256,128]{2,1,0:T(8,128)(2,1)}, u32[]{:S(2)}, u32[]{:S(2)}) collective-permute-start(bf16[4,256,128]{2,1,0:T(8,128)(2,1)S(1)} %collective-permute-done.22.refs_8_), channel_id=1, source_target_pairs={{0,8},{8,0},{16,24},{24,16},{1,9},{9,1},{17,25},{25,17},{2,10},{10... | collective-permute-start | bytes 786440 | tf_op jit(solution)/shard_map/ppermute | solution.py:28

commit v3 on v2

v3 whole, which is shorter than its diff:
```python
import functools

import jax
import jax.numpy as jnp
from jax import lax
from jax.experimental import pallas as pl
from jax.experimental.pallas import tpu as pltpu
from jax.sharding import PartitionSpec as P

TR = 256
LANES = 128
SUBLANES = 8
MIB = 1024 * 1024
CHEAP = pl.CostEstimate(flops=1, bytes_accessed=1, transcendentals=0)
SMEM = pl.BlockSpec(memory_space=pltpu.SMEM)
VMEM = pl.BlockSpec(memory_space=pltpu.VMEM)
ANY = pl.BlockSpec(memory_space=pl.ANY)


def params(mib):
    return pltpu.CompilerParams(vmem_limit_bytes=mib * MIB)


def swap(value, axis, mask):
    pairs = [(i, i ^ mask) for i in range(lax.axis_size(axis))]
    return lax.ppermute(value, axis, pairs)


def placed(target, here, order):
    relative = jnp.bitwise_xor(target, here)
    first, *others = [
        jnp.bitwise_and(lax.shift_right_logical(relative, bit), 1) for bit in order
    ]
    return first, sum(bit * (1 << k) for k, bit in enumerate(others))


def pick_kernel(order, target_ref, table_ref, blocks_ref, *refs):
    out_ref = refs[-1]
    here = lax.axis_index("tile")

    def body(b, count):
        crosses, _ = placed(target_ref[b], here, order)

        @pl.when(crosses == 1)
        def _():
            out_ref[count] = blocks_ref[b, :, 0]

        return count + crosses

    lax.fori_loop(0, blocks_ref.shape[0], body, jnp.int32(0))
    blocks = table_ref.shape[1]
    last = out_ref.shape[0] - 1
    parts, lanes = out_ref.shape[2:]
    table = jnp.zeros((parts, lanes), jnp.float32)
    wide = jnp.concatenate(
        [table_ref[...].astype(jnp.float32), jnp.zeros((2, lanes - blocks), jnp.float32)], axis=1
    )
    row = lax.broadcasted_iota(jnp.int32, (parts, lanes), 0)
    for k in range(2):
        table = jnp.where(row == k, wide[k : k + 1], table)
    out_ref[last, 0] = table.astype(out_ref.dtype)


def pick(targets, table, view, chunk, slots, tokens):
    date, order = chunk
    blocks, height, _, parts, lanes = view.shape
    return pl.pallas_call(
        functools.partial(pick_kernel, order),
        grid=(1,),
        in_specs=[
            SMEM,
            VMEM,
            pl.BlockSpec((blocks, height, 1, parts, lanes), lambda i: (0, 0, date, 0, 0)),
        ]
        + [ANY] * len(tokens),
        out_specs=VMEM,
        out_shape=jax.ShapeDtypeStruct((slots + 1, height, parts, lanes), view.dtype),
        cost_estimate=CHEAP,
        compiler_params=params(PICK_MIB),
        name="pick",
    )(targets, table, view, *tokens)


def own_kernel(date, order, target_ref, row_ref, view_ref, token_ref, acc_ref, own_ref, sem):
    del token_ref
    count, height = own_ref.shape[:2]
    tiles, rows, parts, lanes = acc_ref.shape
    here = lax.axis_index("tile")
    fetch = pltpu.make_async_copy(view_ref.at[:, :, date], own_ref, sem)
    fetch.start()
    flat = acc_ref.reshape(tiles, rows * parts, lanes)

    def clear(t, _):
        flat[t] = jnp.zeros((rows * parts, lanes), jnp.float32)
        return 0

    lax.fori_loop(0, tiles, clear, 0)
    fetch.wait()

    def own(b, _):
        crosses, tile = placed(target_ref[b], here, order)

        @pl.when(crosses == 0)
        def _():
            span = pl.ds(row_ref[b], height)
            acc_ref[tile, span] = acc_ref[tile, span] + own_ref[b].astype(jnp.float32)

        return 0

    lax.fori_loop(0, count, own, 0)


def own_sums(targets, first_rows, view, chunk, tiles, token):
    date, order = chunk
    blocks, height, _, parts, lanes = view.shape
    return pl.pallas_call(
        functools.partial(own_kernel, date, order),
        in_specs=[SMEM, SMEM, ANY, ANY],
        out_specs=VMEM,
        out_shape=jax.ShapeDtypeStruct((tiles, TR, parts, lanes), jnp.float32),
        scratch_shapes=[
            pltpu.VMEM((blocks, height, parts, lanes), view.dtype),
            pltpu.SemaphoreType.DMA,
        ],
        cost_estimate=CHEAP,
        compiler_params=params(DEPOSIT_MIB),
        name="own",
    )(targets, first_rows, view, token)


def deposit_kernel(
    order, count, sums_ref, got_ref, token_ref, far_ref, near_ref, keep_ref, acc_ref, table_ref, code_ref, sem
):
    del token_ref
    height = got_ref.shape[1]
    tiles, rows, parts, lanes = acc_ref.shape
    here = lax.axis_index("tile")
    table = got_ref[got_ref.shape[0] - 1, 0].astype(jnp.float32).astype(jnp.int32)
    table_ref[0:2] = table[0:2]
    inform = pltpu.make_async_copy(table_ref, code_ref, sem)
    inform.start()
    flat = acc_ref.reshape(tiles, rows * parts, lanes)
    flat_sums = sums_ref.reshape(tiles, rows * parts, lanes)

    def begin(t, _):
        flat[t] = flat_sums[t]
        return 0

    lax.fori_loop(0, tiles, begin, 0)
    inform.wait()

    def received(b, slot):
        away, tile = placed(code_ref[0, b], here, order)

        @pl.when(away == 0)
        def _():
            span = pl.ds(code_ref[1, b], height)
            acc_ref[tile, span] = acc_ref[tile, span] + got_ref[slot].astype(jnp.float32)

        return slot + 1 - away

    lax.fori_loop(0, count, received, jnp.int32(0))
    strips = rows // SUBLANES

    def dense(tile, part):
        return jnp.concatenate(
            [
                flat[tile, pl.ds(k * parts + part, SUBLANES, stride=strips * parts)]
                for k in range(strips)
            ],
            axis=0,
        )

    def hand_over(i, _):
        for part in range(parts):
            near_ref[i, part] = dense(4 * i + 1, part).astype(near_ref.dtype)
            far_ref[i, part] = dense(4 * i + 3, part).astype(far_ref.dtype)
            keep_ref[2 * i, part] = dense(4 * i, part)
            keep_ref[2 * i + 1, part] = dense(4 * i + 2, part)
        return 0

    lax.fori_loop(0, tiles // 4, hand_over, 0)


def deposit(sums, got, chunk, blocks, token):
    _, order = chunk
    tiles, rows, parts, lanes = sums.shape
    half = (tiles // 4, parts, rows, lanes)
    return pl.pallas_call(
        functools.partial(deposit_kernel, order, blocks),
        in_specs=[VMEM, VMEM, ANY],
        out_specs=[VMEM, VMEM, VMEM],
        out_shape=[
            jax.ShapeDtypeStruct(half, got.dtype),
            jax.ShapeDtypeStruct(half, got.dtype),
            jax.ShapeDtypeStruct((tiles // 2,) + half[1:], jnp.float32),
        ],
        scratch_shapes=[
            pltpu.VMEM(sums.shape, jnp.float32),
            pltpu.VMEM((SUBLANES, lanes), jnp.int32),
            pltpu.SMEM((SUBLANES, lanes), jnp.int32),
            pltpu.SemaphoreType.DMA,
        ],
        cost_estimate=CHEAP,
        compiler_params=params(DEPOSIT_MIB),
        name="deposit",
    )(sums, got, token)


def merge_kernel(places, *refs):
    *addend_refs, token_ref, out_ref = refs
    del token_ref
    for k, row in enumerate(zip(*places)):
        total = sum(ref[place].astype(jnp.float32) for ref, place in zip(addend_refs, row))
        out_ref[k] = total.astype(out_ref.dtype)


def merge(addends, dtype, token):
    arrays = [array for array, _ in addends]
    places = [tuple(place) for _, place in addends]
    return pl.pallas_call(
        functools.partial(merge_kernel, places),
        in_specs=[VMEM] * len(arrays) + [SMEM if token.ndim == 1 else ANY],
        out_specs=VMEM,
        out_shape=jax.ShapeDtypeStruct((len(places[0]),) + arrays[0].shape[1:], dtype),
        cost_estimate=CHEAP,
        compiler_params=params(DEPOSIT_MIB),
        name="merge",
    )(*arrays, token)


def split(value):
    high = value.astype(jnp.bfloat16)
    return high, (value - high.astype(jnp.float32)).astype(jnp.bfloat16)


def band(size, reach):
    row = lax.broadcasted_iota(jnp.int32, (size, size), 0)
    col = lax.broadcasted_iota(jnp.int32, (size, size), 1)
    return (jnp.abs(row - col) <= reach).astype(jnp.bfloat16)


def shifted(strip, by):
    row = lax.broadcasted_iota(jnp.int32, strip.shape, 0)
    edge = 0 if by > 0 else SUBLANES - 1
    return jnp.where(row == edge, 0.0, pltpu.roll(strip, by % SUBLANES, axis=0))


def boxes(cols):
    col_band = band(cols, 7)

    def box(value):
        strips = [value[k : k + SUBLANES] for k in range(0, value.shape[0], SUBLANES)]
        strips = [shifted(s, 1) for s in strips[-3:]] + strips + [shifted(s, -1) for s in strips[:3]]
        two = [a + b for a, b in zip(strips, strips[1:])]
        four = [a + b for a, b in zip(two, two[2:])]
        seven = [a + b + c for a, b, c in zip(four, two[4:], strips[6:])]
        high, low = split(jnp.concatenate(seven, axis=0))
        wide = jnp.dot(high, col_band, preferred_element_type=jnp.float32)
        return wide + jnp.dot(low, col_band, preferred_element_type=jnp.float32)

    return box


def component(ref, part, halves):
    sides = [ref[2 * half + part] for half in range(halves)]
    return jnp.concatenate(sides, axis=-1).astype(jnp.float32)


def power_box(box, ref, cols):
    halves = cols // LANES
    u0, u1 = component(ref, 0, halves), component(ref, 1, halves)
    return box(u0 * u0 + u1 * u1)


def early_kernel(*refs):
    *field_refs, token_ref, stack_ref, power_ref, end_ref = refs
    del token_ref
    end_ref[0] = 0
    cols = power_ref.shape[2]
    box = boxes(cols)
    for k, ref in enumerate(field_refs):
        stack_ref[k] = ref[...]
        power_ref[k] = power_box(box, ref, cols)


def collect(fields, rows, cols, token):
    return pl.pallas_call(
        early_kernel,
        in_specs=[VMEM] * len(fields) + [ANY],
        out_specs=[VMEM, VMEM, SMEM],
        out_shape=[
            jax.ShapeDtypeStruct((len(fields),) + fields[0].shape, fields[0].dtype),
            jax.ShapeDtypeStruct((len(fields), rows, cols), jnp.float32),
            jax.ShapeDtypeStruct((1,), jnp.int32),
        ],
        cost_estimate=CHEAP,
        compiler_params=params(DEPOSIT_MIB),
        name="collect",
    )(*fields, token)


def coherence_kernel(pairs_ref, *refs):
    *field_refs, stack_ref, power_ref, out_ref, stack, power, done, sems = refs
    rows, pairs, cols = out_ref.shape
    halves = cols // LANES
    strips = rows // SUBLANES
    box = boxes(cols)
    early = stack_ref.shape[0]
    for k in range(early):
        stack[k] = stack_ref[k]
        power[k] = power_ref[k]
    for k, ref in enumerate(field_refs):
        stack[early + k] = ref[...]
        power[early + k] = power_box(box, ref, cols)
    for p in range(pairs):
        first, second = pairs_ref[2 * p], pairs_ref[2 * p + 1]
        u, v = stack.at[first], stack.at[second]
        u0, u1 = component(u, 0, halves), component(u, 1, halves)
        v0, v1 = component(v, 0, halves), component(v, 1, halves)
        box_re = box(u0 * v0 + u1 * v1)
        box_im = box(u1 * v0 - u0 * v1)
        value = jnp.sqrt(box_re * box_re + box_im * box_im) * lax.rsqrt(
            jnp.maximum(power[first] * power[second], 1.0)
        )
        for half in range(halves):
            side = done.at[half].reshape(rows * pairs, LANES)
            for k in range(strips):
                place = pl.ds(p + pairs * k, SUBLANES, stride=pairs * strips)
                side[place] = value[k * SUBLANES : (k + 1) * SUBLANES, half * LANES : (half + 1) * LANES]
    leaving = [
        pltpu.make_async_copy(done.at[half], out_ref.at[:, :, pl.ds(half * LANES, LANES)], sems.at[half])
        for half in range(halves)
    ]
    for copy in leaving:
        copy.start()
    for copy in leaving:
        copy.wait()


def coherence(pairs, fields, stack, power, out_shape):
    rows, pair_count, cols = out_shape
    total = len(fields) + stack.shape[0]
    return pl.pallas_call(
        coherence_kernel,
        in_specs=[SMEM] + [VMEM] * (len(fields) + 2),
        out_specs=ANY,
        out_shape=jax.ShapeDtypeStruct(out_shape, jnp.float32),
        scratch_shapes=[
            pltpu.VMEM((total,) + fields[0].shape, fields[0].dtype),
            pltpu.VMEM((total, rows, cols), jnp.float32),
            pltpu.VMEM((cols // LANES, rows, pair_count, LANES), jnp.float32),
            pltpu.SemaphoreType.DMA((cols // LANES,)),
        ],
        compiler_params=params(LAST_MIB),
        name="coherence",
    )(pairs, *fields, stack, power)


def chunk_plan(dates, bits):
    straight = tuple(range(bits))
    crossed = straight[1:2] + straight[:1] + straight[2:]
    return [(date, crossed if date < CROSSED else straight) for date in range(dates)]


CROSSED = 1
PICK_MIB = 60
DEPOSIT_MIB = 16
LAST_MIB = 32
ORDER = (1, 0, 2, 3, 1, 0, 1, 0, 2, 1, 2, 1, 2, 3, 3, 0, 2, 3, 0, 3)


def local(radar_echoes, destination_panel, panel_line_shift, epoch_couples):
    blocks, height, dates_here, components, cols = radar_echoes.shape
    tile_count = lax.axis_size("tile")
    group_count = lax.axis_size("date")
    group = lax.axis_index("date")
    capacity = max(2, blocks // tile_count + max(1, blocks // (2 * tile_count)))
    slots = min(blocks, tile_count // 2 * capacity)
    bits = tile_count.bit_length() - 1
    stages = bits + 2

    halves = cols // LANES
    view = radar_echoes.reshape(blocks, height, dates_here, components, halves, LANES)
    view = view.transpose(0, 1, 2, 4, 3, 5)
    view = view.reshape(blocks, height, dates_here, halves * components, LANES)

    chunks = chunk_plan(dates_here, bits)
    targets = destination_panel[:, 0]
    table = jnp.stack([targets, panel_line_shift])
    order = ORDER
    if len(order) != len(chunks) * stages:
        order = [c for _, c in sorted((2 * k + c, c) for c in range(len(chunks)) for k in range(stages))]
    state = [None] * len(chunks)
    step = [0] * len(chunks)
    fields = [None] * dates_here
    finished = []
    tokens = []
    for c in order:
        date, bit_order = chunks[c]
        k = step[c]
        step[c] += 1
        flip = [lambda value, bit=bit: swap(value, "tile", 1 << bit) for bit in bit_order]
        if k == 0:
            token = pick(targets, table, view, chunks[c], slots, tokens)
            tokens = [token]
            state[c] = flip[0](token)
            continue
        if k == 1:
            token = own_sums(targets, panel_line_shift, view, chunks[c], tile_count // 2, token)
            state[c] = token, state[c]
            continue
        k -= 1
        if k == 1:
            far, near, keep = deposit(*state[c], chunks[c], blocks, token)
            token = far
            state[c] = [(keep, range(keep.shape[0]))], flip[1](near), flip[1](far)
            continue
        addends, near, far = state[c]
        if k < bits:
            onward = [(array, places[1::2]) for array, places in addends]
            sent = merge(onward + [(far, range(far.shape[0]))], view.dtype, token)
            token = sent
            addends = [(array, places[0::2]) for array, places in addends]
            addends = addends + [(near, range(near.shape[0]))]
            if sent.shape[0] == 1:
                state[c] = addends, None, flip[k](sent)
            else:
                state[c] = addends, flip[k](sent[0::2]), flip[k](sent[1::2])
            continue
        if len(finished) == len(chunks) - 1:
            held = [fields[chunks[e][0]][g] for e in finished[:-1] for g in range(group_count)]
            stack, power, token = collect(held, TR, cols, token)
        finished.append(c)
        token = merge(addends + [(far, range(1))], view.dtype, token)
        known = {0: token[0]}
        mask = group_count // 2
        while mask:
            known.update({g ^ mask: swap(f, "date", mask) for g, f in list(known.items())})
            mask //= 2
        fields[date] = known

    late = [fields[chunks[e][0]][g] for e in finished[-2:] for g in range(group_count)]
    slot_of = [0] * dates_here
    for k, e in enumerate(finished):
        slot_of[chunks[e][0]] = k * group_count
    pairs_here = epoch_couples.shape[0] // group_count
    mine = lax.dynamic_slice_in_dim(epoch_couples, group * pairs_here, pairs_here, axis=0)
    date = mine % dates_here
    slot = sum([jnp.where(date == k, first, 0) for k, first in enumerate(slot_of)], jnp.zeros_like(date))
    place = slot + jnp.bitwise_xor(mine // dates_here, group)
    return coherence(place.reshape(-1), late, stack, power, (TR, pairs_here, cols))


def solution(mesh):
    in_specs = (P("tile", None, "date", None, None), P("tile", None), P("tile"), P())
    out_specs = P("tile", "date", None)
    return jax.shard_map(local, mesh=mesh, in_specs=in_specs, out_specs=out_specs, check_vma=False)
```

time: 124 us -> 114 us (0.919)
  waiting for transfers between devices: 55.9 us -> 28.6 us
  starting transfers between devices: 24.7 us -> 32.5 us
  local copies, waits for them, and re-layouts: 0.72 us -> 6.42 us
  Pallas kernels: 40.4 us -> 44.1 us
    ppermute x30 -> x28, waiting for transfers between devices: 55.9 us -> 28.6 us  [swap(): return lax.ppermute(value, axis, pairs)]
    ppermute x30 -> x28, starting transfers between devices: 24.7 us -> 32.5 us  [swap(): return lax.ppermute(value, axis, pairs)]
    unnamed x22 -> x16, local copies, waits for them, and re-layouts: 0.55 us -> 6.25 us
    pallas_call x9 -> x14, Pallas kernels: 39.9 us -> 43 us  [the longest x4 12.6 us: deposit(): pl.pallas_call(functools.partial(deposit_kernel, order, blocks), in_specs...]
    add x3 -> x1, other arithmetic: 1.44 us -> 0.08 us  [local(): place = slot + jnp.bitwise_xor(mine // dates_here, group)]
  transfers between devices with their start and end apart: 30 -> 28, of which waited for: 12 -> 11; matrix products, arithmetic and copies ran while one was open for 0% -> 0% of each run, Pallas kernels for 23% -> 30%
where the time goes in v3:
time: 114 us; the launch traced here: 113 us
  Pallas kernels  44.1 us (39%)
  starting transfers between devices  32.5 us (29%)
  waiting for transfers between devices  28.6 us (25%)
  local copies, waits for them, and re-layouts  6.42 us (6%)
  other arithmetic  1.31 us (1%)
    ppermute x28, starting transfers between devices, swap(): return lax.ppermute(value, axis, pairs)  32.5 us
    ppermute x28, waiting for transfers between devices, swap(): return lax.ppermute(value, axis, pairs)  28.6 us
    pallas_call x4, Pallas kernels, deposit(): pl.pallas_call(functools.partial(deposit_kernel, order, blocks), in_specs...  12.6 us
    pallas_call x4, Pallas kernels, pick(): pl.pallas_call(functools.partial(pick_kernel, order), grid=(1,), in_specs...  12.4 us
    pallas_call x4, Pallas kernels, own_sums(): pl.pallas_call(functools.partial(own_kernel, date, order), in_specs=[SMEM...  9.24 us
    pallas_call x1, Pallas kernels, coherence(): pl.pallas_call(coherence_kernel, in_specs=[SMEM] + [VMEM] * (len(fields)...  7.58 us
    unnamed x16, local copies, waits for them, and re-layouts  6.25 us
  transfers between devices with their start and end apart: 28, of which 11 were waited for; matrix products, arithmetic and copies ran while one was open for 0% of the time, Pallas kernels for 30%

profile of v3, /device:TPU:0, one launch (start us, length us, event | category | flops | bytes accessed | tf_op | source)
XLA Modules:
  0.0 113.3 jit_solution(12225953297098050929)
XLA Ops:
  0.0 1.2 %pad_add_fusion.table_ref = s32[2,64]{1,0:T(2,128)} fusion(s32[1,64]{1,0:T(1,128)} %bitcast.41, s32[1,64]{1,0:T(1,128)} %bitcast.32), kind=kLoop, calls=%fused_computation.11 | loop fusion | flops 128 | bytes 1024 | tf_op jit(solution)/shard_map/stack | solution.py:390
  1.2 3.1 %pick.4.refs_0_ = bf16[49,16,4,128]{3,2,1,0:T(4,128)(2,1)} custom-call(s32[64]{0:T(128)} %bitcast.33, s32[2,64]{1,0:T(2,128)} %pad_add_fusion.table_ref, bf16[64,16,4,4,128]{4,3,2,1,0:T(4,128)(2,1)} %bitcast.12), custom_call_target="tpu_custom_call" | custom-call | flops 1 | bytes 1 | tf_op jit(solution)/shard_map/pick/pallas_call | solution.py:67
  4.3 2.9 %collective-permute-start.1 = (bf16[49,16,4,128]{3,2,1,0:T(4,128)(2,1)}, bf16[49,16,4,128]{3,2,1,0:T(4,128)(2,1)S(1)}, u32[]{:S(2)}, u32[]{:S(2)}) collective-permute-start(bf16[49,16,4,128]{3,2,1,0:T(4,128)(2,1)} %pick.4.refs_0_), channel_id=1, source_target_pairs={{0,1},{1,0},{2,3},{3,2},{4,5},{5,4},{6,7},{7,6},{8,9},{9,8},{10,11... | collective-permute-start | bytes 2408456 | tf_op jit(solution)/shard_map/ppermute | solution.py:26
  7.2 3.1 %pick.5.refs_0_ = bf16[49,16,4,128]{3,2,1,0:T(4,128)(2,1)} custom-call(s32[64]{0:T(128)} %bitcast.34, s32[2,64]{1,0:T(2,128)} %pad_add_fusion.table_ref, bf16[64,16,4,4,128]{4,3,2,1,0:T(4,128)(2,1)} %bitcast.13, bf16[49,16,4,128]{3,2,1,0:T(4,128)(2,1)} %pick.4.refs_0_), custom_call_target="tpu_custom_call" | custom-call | flops 1 | bytes 1 | tf_op jit(solution)/shard_map/pick/pallas_call | solution.py:67
  10.4 1.6 %collective-permute-start = (bf16[49,16,4,128]{3,2,1,0:T(4,128)(2,1)}, bf16[49,16,4,128]{3,2,1,0:T(4,128)(2,1)S(1)}, u32[]{:S(2)}, u32[]{:S(2)}) collective-permute-start(bf16[49,16,4,128]{3,2,1,0:T(4,128)(2,1)} %pick.5.refs_0_), channel_id=1, source_target_pairs={{0,2},{1,3},{2,0},{3,1},{4,6},{5,7},{6,4},{7,5},{8,10},{9,11},{10,... | collective-permute-start | bytes 2408456 | tf_op jit(solution)/shard_map/ppermute | solution.py:26
  11.9 3.1 %pick.6.refs_0_ = bf16[49,16,4,128]{3,2,1,0:T(4,128)(2,1)} custom-call(s32[64]{0:T(128)} %bitcast.35, s32[2,64]{1,0:T(2,128)} %pad_add_fusion.table_ref, bf16[64,16,4,4,128]{4,3,2,1,0:T(4,128)(2,1)} %bitcast.14, bf16[49,16,4,128]{3,2,1,0:T(4,128)(2,1)} %pick.5.refs_0_), custom_call_target="tpu_custom_call" | custom-call | flops 1 | bytes 1 | tf_op jit(solution)/shard_map/pick/pallas_call | solution.py:67
  15.0 0.5 collective-permute-start.4
  15.5 3.1 %pick.7.token_ref = bf16[49,16,4,128]{3,2,1,0:T(4,128)(2,1)} custom-call(s32[64]{0:T(128)} %bitcast.36, s32[2,64]{1,0:T(2,128)} %pad_add_fusion.table_ref, bf16[64,16,4,4,128]{4,3,2,1,0:T(4,128)(2,1)} %bitcast.15, bf16[49,16,4,128]{3,2,1,0:T(4,128)(2,1)} %pick.6.refs_0_), custom_call_target="tpu_custom_call" | custom-call | flops 1 | bytes 1 | tf_op jit(solution)/shard_map/pick/pallas_call | solution.py:67
  18.6 1.5 %collective-permute-start.9 = (bf16[49,16,4,128]{3,2,1,0:T(4,128)(2,1)}, bf16[49,16,4,128]{3,2,1,0:T(4,128)(2,1)S(1)}, u32[]{:S(2)}, u32[]{:S(2)}) collective-permute-start(bf16[49,16,4,128]{3,2,1,0:T(4,128)(2,1)} %pick.7.token_ref), channel_id=1, source_target_pairs={{0,1},{1,0},{2,3},{3,2},{4,5},{5,4},{6,7},{7,6},{8,9},{9,8},{10,11... | collective-permute-start | bytes 2408456 | tf_op jit(solution)/shard_map/ppermute | solution.py:26
  20.1 2.2 %copy-done = bf16[64,16,4,2,256]{4,3,2,1,0:T(2,128)(2,1)S(1)} copy-done((bf16[64,16,4,2,256]{4,3,2,1,0:T(2,128)(2,1)S(1)}, bf16[64,16,4,2,256]{4,3,2,1,0:T(2,128)(2,1)}, u32[]{:S(2)}) %copy-start) | copy-done | bytes 4194328
  22.3 1.1 %copy-done.2 = bf16[49,16,4,128]{3,2,1,0:T(4,128)(2,1)S(1)} copy-done((bf16[49,16,4,128]{3,2,1,0:T(4,128)(2,1)S(1)}, bf16[49,16,4,128]{3,2,1,0:T(4,128)(2,1)}, u32[]{:S(2)}) %copy-start.2) | copy-done | bytes 802840
  23.5 2.3 %own.4.token_ref.sums_ref = f32[4,256,4,128]{3,2,1,0:T(4,128)S(1)} custom-call(s32[64]{0:T(128)S(1)} %bitcast.37, s32[64]{0:T(128)S(1)} %copy-done.6, bf16[64,16,4,4,128]{4,3,2,1,0:T(4,128)(2,1)S(1)} %bitcast.16, bf16[49,16,4,128]{3,2,1,0:T(4,128)(2,1)S(1)} %copy-done.2), custom_call_target="tpu_custom_call" | custom-call | flops 1 | bytes 1 | tf_op jit(solution)/shard_map/own/pallas_call | solution.py:116
  25.8 2.3 %own.5.token_ref.sums_ref = f32[4,256,4,128]{3,2,1,0:T(4,128)S(1)} custom-call(s32[64]{0:T(128)S(1)} %bitcast.38, s32[64]{0:T(128)S(1)} %copy-done.6, bf16[64,16,4,4,128]{4,3,2,1,0:T(4,128)(2,1)S(1)} %bitcast.17, f32[4,256,4,128]{3,2,1,0:T(4,128)S(1)} %own.4.token_ref.sums_ref), custom_call_target="tpu_custom_call" | custom-call | flops 1 | bytes 1 | tf_op jit(solution)/shard_map/own/pallas_call | solution.py:116
  28.1 0.0 collective-permute-done.1.got_ref
  28.1 0.0 copy-start.1
  28.1 3.1 %deposit.4 = (bf16[1,4,256,128]{3,2,1,0:T(8,128)(2,1)S(1)}, bf16[1,4,256,128]{3,2,1,0:T(8,128)(2,1)S(1)}, f32[2,4,256,128]{3,2,1,0:T(8,128)S(1)}) custom-call(f32[4,256,4,128]{3,2,1,0:T(4,128)S(1)} %own.4.token_ref.sums_ref, bf16[49,16,4,128]{3,2,1,0:T(4,128)(2,1)S(1)} %collective-permute-done.1.got_ref, f32[4,256,4,128]{3,2,1,0:T(4,128)S(1)} %own.5.token_ref.sums_ref), custom_call_target="tpu_custom_call" | custom-call | flops 1 | bytes 1 | tf_op jit(solution)/shard_map/deposit/pallas_call | solution.py:189
  31.2 0.5 collective-permute-start.5
  31.7 0.0 collective-permute-done.got_ref
  31.7 3.1 %deposit.5 = (bf16[1,4,256,128]{3,2,1,0:T(8,128)(2,1)S(1)}, bf16[1,4,256,128]{3,2,1,0:T(8,128)(2,1)S(1)}, f32[2,4,256,128]{3,2,1,0:T(8,128)S(1)}) custom-call(f32[4,256,4,128]{3,2,1,0:T(4,128)S(1)} %own.5.token_ref.sums_ref, bf16[49,16,4,128]{3,2,1,0:T(4,128)(2,1)S(1)} %collective-permute-done.got_ref, bf16[1,4,256,128]{3,2,1,0:T(8,128)(2,1)S(1)} %get-tuple-element.20.token_ref), custom_call_target="tpu_custom_call" | custom-call | flops 1 | bytes 1 | tf_op jit(solution)/shard_map/deposit/pallas_call | solution.py:189
  34.8 2.3 %own.6.refs_2_.sums_ref = f32[4,256,4,128]{3,2,1,0:T(4,128)S(1)} custom-call(s32[64]{0:T(128)S(1)} %bitcast.39, s32[64]{0:T(128)S(1)} %copy-done.6, bf16[64,16,4,4,128]{4,3,2,1,0:T(4,128)(2,1)S(1)} %bitcast.18, bf16[1,4,256,128]{3,2,1,0:T(8,128)(2,1)S(1)} %get-tuple-element.23.token_ref), custom_call_target="tpu_custom_call" | custom-call | flops 1 | bytes 1 | tf_op jit(solution)/shard_map/own/pallas_call | solution.py:116
  37.1 1.6 %collective-permute-start.7 = (bf16[1,4,256,128]{3,2,1,0:T(8,128)(2,1)S(1)}, bf16[1,4,256,128]{3,2,1,0:T(8,128)(2,1)S(1)}, u32[]{:S(2)}, u32[]{:S(2)}) collective-permute-start(bf16[1,4,256,128]{3,2,1,0:T(8,128)(2,1)S(1)} %get-tuple-element.27), channel_id=1, source_target_pairs={{0,2},{1,3},{2,0},{3,1},{4,6},{5,7},{6,4},{7,5},{8,10},{9,11},{10,... | collective-permute-start | bytes 786440 | tf_op jit(solution)/shard_map/ppermute | solution.py:26
  38.8 2.6 %collective-permute-start.8 = (bf16[1,4,256,128]{3,2,1,0:T(8,128)(2,1)S(1)}, bf16[1,4,256,128]{3,2,1,0:T(8,128)(2,1)S(1)}, u32[]{:S(2)}, u32[]{:S(2)}) collective-permute-start(bf16[1,4,256,128]{3,2,1,0:T(8,128)(2,1)S(1)} %merge.8.token_ref), channel_id=1, source_target_pairs={{0,4},{1,5},{2,6},{3,7},{4,0},{5,1},{6,2},{7,3},{8,12},{9,13},{10,... | collective-permute-start | bytes 786440 | tf_op jit(solution)/shard_map/ppermute | solution.py:26
  41.4 2.0 %collective-permute-done.4.got_ref = bf16[49,16,4,128]{3,2,1,0:T(4,128)(2,1)S(1)} collective-permute-done((bf16[49,16,4,128]{3,2,1,0:T(4,128)(2,1)}, bf16[49,16,4,128]{3,2,1,0:T(4,128)(2,1)S(1)}, u32[]{:S(2)}, u32[]{:S(2)}) %collective-permute-start.4) | collective-permute-done | bytes 802848 | tf_op jit(solution)/shard_map/ppermute | solution.py:26
  43.4 3.1 %deposit.6 = (bf16[1,4,256,128]{3,2,1,0:T(8,128)(2,1)S(1)}, bf16[1,4,256,128]{3,2,1,0:T(8,128)(2,1)S(1)}, f32[2,4,256,128]{3,2,1,0:T(8,128)S(1)}) custom-call(f32[4,256,4,128]{3,2,1,0:T(4,128)S(1)} %own.6.refs_2_.sums_ref, bf16[49,16,4,128]{3,2,1,0:T(4,128)(2,1)S(1)} %collective-permute-done.4.got_ref, bf16[1,4,256,128]{3,2,1,0:T(8,128)(2,1)S(1)} %merge.8.token_ref), custom_call_target="tpu_custom_call" | custom-call | flops 1 | bytes 1 | tf_op jit(solution)/shard_map/deposit/pallas_call | solution.py:189
  46.5 2.2 %collective-permute-start.6 = (bf16[1,4,256,128]{3,2,1,0:T(8,128)(2,1)S(1)}, bf16[1,4,256,128]{3,2,1,0:T(8,128)(2,1)S(1)}, u32[]{:S(2)}, u32[]{:S(2)}) collective-permute-start(bf16[1,4,256,128]{3,2,1,0:T(8,128)(2,1)S(1)} %get-tuple-element.26.refs_3_), channel_id=1, source_target_pairs={{0,2},{1,3},{2,0},{3,1},{4,6},{5,7},{6,4},{7,5},{8,10},{9,11},{10,... | collective-permute-start | bytes 786440 | tf_op jit(solution)/shard_map/ppermute | solution.py:26
  48.7 1.4 %collective-permute-start.3 = (bf16[1,4,256,128]{3,2,1,0:T(8,128)(2,1)S(1)}, bf16[1,4,256,128]{3,2,1,0:T(8,128)(2,1)S(1)}, u32[]{:S(2)}, u32[]{:S(2)}) collective-permute-start(bf16[1,4,256,128]{3,2,1,0:T(8,128)(2,1)S(1)} %get-tuple-element.23.token_ref), channel_id=1, source_target_pairs={{0,1},{1,0},{2,3},{3,2},{4,5},{5,4},{6,7},{7,6},{8,9},{9,8},{10,11... | collective-permute-start | bytes 786440 | tf_op jit(solution)/shard_map/ppermute | solution.py:26
  50.1 0.4 collective-permute-done.7.refs_1_
  50.5 0.0 collective-permute-start.12
  50.5 0.1 merge.9.refs_2_
  50.6 5.5 %collective-permute-done.6.refs_1_ = bf16[1,4,256,128]{3,2,1,0:T(8,128)(2,1)S(1)} collective-permute-done((bf16[1,4,256,128]{3,2,1,0:T(8,128)(2,1)S(1)}, bf16[1,4,256,128]{3,2,1,0:T(8,128)(2,1)S(1)}, u32[]{:S(2)}, u32[]{:S(2)}) %collective-permute-start.6) | collective-permute-done | bytes 262176 | tf_op jit(solution)/shard_map/ppermute | solution.py:26
  56.2 3.5 %collective-permute-start.13 = (bf16[1,4,256,128]{3,2,1,0:T(8,128)(2,1)S(1)}, bf16[1,4,256,128]{3,2,1,0:T(8,128)(2,1)S(1)}, u32[]{:S(2)}, u32[]{:S(2)}) collective-permute-start(bf16[1,4,256,128]{3,2,1,0:T(8,128)(2,1)S(1)} %merge.10.token_ref), channel_id=1, source_target_pairs={{0,4},{1,5},{2,6},{3,7},{4,0},{5,1},{6,2},{7,3},{8,12},{9,13},{10,... | collective-permute-start | bytes 786440 | tf_op jit(solution)/shard_map/ppermute | solution.py:26
  59.6 2.3 %own.7.sums_ref.token_ref = f32[4,256,4,128]{3,2,1,0:T(4,128)S(1)} custom-call(s32[64]{0:T(128)S(1)} %bitcast.40, s32[64]{0:T(128)S(1)} %copy-done.6, bf16[64,16,4,4,128]{4,3,2,1,0:T(4,128)(2,1)S(1)} %bitcast.19, bf16[1,4,256,128]{3,2,1,0:T(8,128)(2,1)S(1)} %merge.10.token_ref), custom_call_target="tpu_custom_call" | custom-call | flops 1 | bytes 1 | tf_op jit(solution)/shard_map/own/pallas_call | solution.py:116
  62.0 3.3 %deposit.7 = (bf16[1,4,256,128]{3,2,1,0:T(8,128)(2,1)S(1)}, bf16[1,4,256,128]{3,2,1,0:T(8,128)(2,1)S(1)}, f32[2,4,256,128]{3,2,1,0:T(8,128)S(1)}) custom-call(f32[4,256,4,128]{3,2,1,0:T(4,128)S(1)} %own.7.sums_ref.token_ref, bf16[49,16,4,128]{3,2,1,0:T(4,128)(2,1)S(1)} %collective-permute-done.9.got_ref, f32[4,256,4,128]{3,2,1,0:T(4,128)S(1)} %own.7.sums_ref.token_ref), custom_call_target="tpu_custom_call" | custom-call | flops 1 | bytes 1 | tf_op jit(solution)/shard_map/deposit/pallas_call | solution.py:189
  65.3 1.1 collective-permute-start.11
  66.3 1.3 %collective-permute-start.2 = (bf16[1,4,256,128]{3,2,1,0:T(8,128)(2,1)S(1)}, bf16[1,4,256,128]{3,2,1,0:T(8,128)(2,1)S(1)}, u32[]{:S(2)}, u32[]{:S(2)}) collective-permute-start(bf16[1,4,256,128]{3,2,1,0:T(8,128)(2,1)S(1)} %get-tuple-element.22), channel_id=1, source_target_pairs={{0,1},{1,0},{2,3},{3,2},{4,5},{5,4},{6,7},{7,6},{8,9},{9,8},{10,11... | collective-permute-start | bytes 786440 | tf_op jit(solution)/shard_map/ppermute | solution.py:26
  67.6 1.5 %collective-permute-start.20 = (bf16[4,256,128]{2,1,0:T(8,128)(2,1)S(1)}, bf16[4,256,128]{2,1,0:T(8,128)(2,1)S(1)}, u32[]{:S(2)}, u32[]{:S(2)}) collective-permute-start(bf16[4,256,128]{2,1,0:T(8,128)(2,1)S(1)} %bitcast.20), channel_id=1, source_target_pairs={{0,16},{8,24},{16,0},{24,8},{1,17},{9,25},{17,1},{25,9},{2,18},{10... | collective-permute-start | bytes 786440 | tf_op jit(solution)/shard_map/ppermute | solution.py:26
  69.2 0.1 merge.12.refs_2_
  69.3 1.5 %collective-permute-start.23 = (bf16[4,256,128]{2,1,0:T(8,128)(2,1)S(1)}, bf16[4,256,128]{2,1,0:T(8,128)(2,1)S(1)}, u32[]{:S(2)}, u32[]{:S(2)}) collective-permute-start(bf16[4,256,128]{2,1,0:T(8,128)(2,1)S(1)} %bitcast.26), channel_id=1, source_target_pairs={{0,16},{8,24},{16,0},{24,8},{1,17},{9,25},{17,1},{25,9},{2,18},{10... | collective-permute-start | bytes 786440 | tf_op jit(solution)/shard_map/ppermute | solution.py:26
  70.8 1.6 %collective-permute-start.10 = (bf16[1,4,256,128]{3,2,1,0:T(8,128)(2,1)S(1)}, bf16[1,4,256,128]{3,2,1,0:T(8,128)(2,1)S(1)}, u32[]{:S(2)}, u32[]{:S(2)}) collective-permute-start(bf16[1,4,256,128]{3,2,1,0:T(8,128)(2,1)S(1)} %merge.11.refs_3_), channel_id=1, source_target_pairs={{0,4},{1,5},{2,6},{3,7},{4,0},{5,1},{6,2},{7,3},{8,12},{9,13},{10,... | collective-permute-start | bytes 786440 | tf_op jit(solution)/shard_map/ppermute | solution.py:26
  72.3 2.4 %collective-permute-done.11.refs_1_ = bf16[1,4,256,128]{3,2,1,0:T(8,128)(2,1)S(1)} collective-permute-done((bf16[1,4,256,128]{3,2,1,0:T(8,128)(2,1)S(1)}, bf16[1,4,256,128]{3,2,1,0:T(8,128)(2,1)S(1)}, u32[]{:S(2)}, u32[]{:S(2)}) %collective-permute-start.11) | collective-permute-done | bytes 262176 | tf_op jit(solution)/shard_map/ppermute | solution.py:26
  74.8 0.6 collective-permute-start.22
  75.4 0.4 collective-permute-done.20.refs_2_
  75.8 2.8 %collective-permute-done.23.refs_6_ = bf16[4,256,128]{2,1,0:T(8,128)(2,1)S(1)} collective-permute-done((bf16[4,256,128]{2,1,0:T(8,128)(2,1)S(1)}, bf16[4,256,128]{2,1,0:T(8,128)(2,1)S(1)}, u32[]{:S(2)}, u32[]{:S(2)}) %collective-permute-start.23) | collective-permute-done | bytes 262176 | tf_op jit(solution)/shard_map/ppermute | solution.py:26
  78.6 3.6 %collective-permute-done.10.refs_2_ = bf16[1,4,256,128]{3,2,1,0:T(8,128)(2,1)S(1)} collective-permute-done((bf16[1,4,256,128]{3,2,1,0:T(8,128)(2,1)S(1)}, bf16[1,4,256,128]{3,2,1,0:T(8,128)(2,1)S(1)}, u32[]{:S(2)}, u32[]{:S(2)}) %collective-permute-start.10) | collective-permute-done | bytes 262176 | tf_op jit(solution)/shard_map/ppermute | solution.py:26
  82.2 2.9 %collective-permute-start.18 = (bf16[1,4,256,128]{3,2,1,0:T(8,128)(2,1)S(1)}, bf16[1,4,256,128]{3,2,1,0:T(8,128)(2,1)S(1)}, u32[]{:S(2)}, u32[]{:S(2)}) collective-permute-start(bf16[1,4,256,128]{3,2,1,0:T(8,128)(2,1)S(1)} %merge.13.refs_3_), channel_id=1, source_target_pairs={{0,4},{1,5},{2,6},{3,7},{4,0},{5,1},{6,2},{7,3},{8,12},{9,13},{10,... | collective-permute-start | bytes 786440 | tf_op jit(solution)/shard_map/ppermute | solution.py:26
  85.2 0.1 merge.14.refs_8_
  85.3 0.0 copy-start.7
  85.3 1.6 %collective-permute-start.15 = (bf16[4,256,128]{2,1,0:T(8,128)(2,1)S(1)}, bf16[4,256,128]{2,1,0:T(8,128)(2,1)S(1)}, u32[]{:S(2)}, u32[]{:S(2)}) collective-permute-start(bf16[4,256,128]{2,1,0:T(8,128)(2,1)S(1)} %bitcast.23), channel_id=1, source_target_pairs={{0,16},{8,24},{16,0},{24,8},{1,17},{9,25},{17,1},{25,9},{2,18},{10... | collective-permute-start | bytes 786440 | tf_op jit(solution)/shard_map/ppermute | solution.py:26
  86.9 1.2 %collect.1 = (bf16[8,4,256,128]{3,2,1,0:T(8,128)(2,1)S(1)}, f32[8,256,256]{2,1,0:T(8,128)S(1)}, s32[1]{0:T(128)}) custom-call(bf16[4,256,128]{2,1,0:T(8,128)(2,1)S(1)} %bitcast.22, bf16[4,256,128]{2,1,0:T(8,128)(2,1)S(1)} %collective-permute-done.19.refs_1_, bf16[4,256,128]{2,1,0:T(8,128)(2,1)S(1)} %collective-permute-done.20.refs_2_, ...), custom_call_target="tpu_custom_call" | custom-call | flops 1 | bytes 1 | tf_op jit(solution)/shard_map/collect/pallas_call | solution.py:288
  88.1 0.0 copy-start.3
  88.1 1.3 %copy-done.3 = f32[8,256,256]{2,1,0:T(8,128)} copy-done((f32[8,256,256]{2,1,0:T(8,128)}, f32[8,256,256]{2,1,0:T(8,128)S(1)}, u32[]{:S(2)}) %copy-start.3) | copy-done | bytes 2097176
  89.4 4.0 %collective-permute-done.17.refs_1_ = bf16[1,4,256,128]{3,2,1,0:T(8,128)(2,1)S(1)} collective-permute-done((bf16[1,4,256,128]{3,2,1,0:T(8,128)(2,1)S(1)}, bf16[1,4,256,128]{3,2,1,0:T(8,128)(2,1)S(1)}, u32[]{:S(2)}, u32[]{:S(2)}) %collective-permute-start.17) | collective-permute-done | bytes 262176 | tf_op jit(solution)/shard_map/ppermute | solution.py:26
  93.3 1.8 %collective-permute-done.18.refs_2_ = bf16[1,4,256,128]{3,2,1,0:T(8,128)(2,1)S(1)} collective-permute-done((bf16[1,4,256,128]{3,2,1,0:T(8,128)(2,1)S(1)}, bf16[1,4,256,128]{3,2,1,0:T(8,128)(2,1)S(1)}, u32[]{:S(2)}, u32[]{:S(2)}) %collective-permute-start.18) | collective-permute-done | bytes 262176 | tf_op jit(solution)/shard_map/ppermute | solution.py:26
  95.1 0.7 merge.15
  95.8 1.6 %collective-permute-start.26 = (bf16[4,256,128]{2,1,0:T(8,128)(2,1)S(1)}, bf16[4,256,128]{2,1,0:T(8,128)(2,1)S(1)}, u32[]{:S(2)}, u32[]{:S(2)}) collective-permute-start(bf16[4,256,128]{2,1,0:T(8,128)(2,1)S(1)} %bitcast.29), channel_id=1, source_target_pairs={{0,16},{8,24},{16,0},{24,8},{1,17},{9,25},{17,1},{25,9},{2,18},{10... | collective-permute-start | bytes 786440 | tf_op jit(solution)/shard_map/ppermute | solution.py:26
  97.4 0.5 collective-permute-start.16
  97.9 0.0 collective-permute-start.25
  98.0 4.3 %collective-permute-done.26.refs_6_ = bf16[4,256,128]{2,1,0:T(8,128)(2,1)S(1)} collective-permute-done((bf16[4,256,128]{2,1,0:T(8,128)(2,1)S(1)}, bf16[4,256,128]{2,1,0:T(8,128)(2,1)S(1)}, u32[]{:S(2)}, u32[]{:S(2)}) %collective-permute-start.26) | collective-permute-done | bytes 262176 | tf_op jit(solution)/shard_map/ppermute | solution.py:26
  102.3 0.1 fusion.2
  102.4 0.1 copy.7
  102.5 0.1 reshape.9.pairs_ref
  102.6 1.4 %collective-permute-done.27.refs_7_ = bf16[4,256,128]{2,1,0:T(8,128)(2,1)} collective-permute-done((bf16[4,256,128]{2,1,0:T(8,128)(2,1)S(1)}, bf16[4,256,128]{2,1,0:T(8,128)(2,1)}, u32[]{:S(2)}, u32[]{:S(2)}) %collective-permute-start.27) | collective-permute-done | bytes 262176 | tf_op jit(solution)/shard_map/ppermute | solution.py:26
  104.0 1.6 %copy-done.4 = f32[8,256,256]{2,1,0:T(8,128)S(1)} copy-done((f32[8,256,256]{2,1,0:T(8,128)S(1)}, f32[8,256,256]{2,1,0:T(8,128)}, u32[]{:S(2)}) %copy-start.4) | copy-done | bytes 2097176
  105.5 7.6 %coherence.1 = f32[256,8,256]{2,1,0:T(8,128)} custom-call(s32[16]{0:T(128)S(1)} %reshape.9.pairs_ref, bf16[4,256,128]{2,1,0:T(8,128)(2,1)S(1)} %bitcast.25, bf16[4,256,128]{2,1,0:T(8,128)(2,1)S(1)} %collective-permute-done.14.refs_1_, bf16[4,256,128]{2,1,0:T(8,128)(2,1)S(1)} %collective-permute-done.15.refs_2_, ...), custom_call_target="tpu_custom_call" | custom-call | tf_op jit(solution)/shard_map/coherence/pallas_call | solution.py:344
  (34 shorter events, 0.3 us)
Async XLA Ops:
  4.3 23.8 %collective-permute-start.1 = (bf16[49,16,4,128]{3,2,1,0:T(4,128)(2,1)}, bf16[49,16,4,128]{3,2,1,0:T(4,128)(2,1)S(1)}, u32[]{:S(2)}, u32[]{:S(2)}) collective-permute-start(bf16[49,16,4,128]{3,2,1,0:T(4,128)(2,1)} %pick.4.refs_0_), channel_id=1, source_target_pairs={{0,1},{1,0},{2,3},{3,2},{4,5},{5,4},{6,7},{7,6},{8,9},{9,8},{10,11... | collective-permute-start | bytes 2408456 | tf_op jit(solution)/shard_map/ppermute | solution.py:26
  10.4 21.3 %collective-permute-start = (bf16[49,16,4,128]{3,2,1,0:T(4,128)(2,1)}, bf16[49,16,4,128]{3,2,1,0:T(4,128)(2,1)S(1)}, u32[]{:S(2)}, u32[]{:S(2)}) collective-permute-start(bf16[49,16,4,128]{3,2,1,0:T(4,128)(2,1)} %pick.5.refs_0_), channel_id=1, source_target_pairs={{0,2},{1,3},{2,0},{3,1},{4,6},{5,7},{6,4},{7,5},{8,10},{9,11},{10,... | collective-permute-start | bytes 2408456 | tf_op jit(solution)/shard_map/ppermute | solution.py:26
  15.0 5.1 %copy-start.5 = (s32[64,1]{0,1:T(1,128)S(1)}, s32[64,1]{0,1:T(1,128)}, u32[]{:S(2)}) copy-start(s32[64,1]{0,1:T(1,128)} %param.5) | copy-start | bytes 772
  15.0 5.1 %copy-start.6 = (s32[64]{0:T(128)S(1)}, s32[64]{0:T(128)}, u32[]{:S(2)}) copy-start(s32[64]{0:T(128)} %row_ref.7) | copy-start | bytes 772
  15.0 28.3 %collective-permute-start.4 = (bf16[49,16,4,128]{3,2,1,0:T(4,128)(2,1)}, bf16[49,16,4,128]{3,2,1,0:T(4,128)(2,1)S(1)}, u32[]{:S(2)}, u32[]{:S(2)}) collective-permute-start(bf16[49,16,4,128]{3,2,1,0:T(4,128)(2,1)} %pick.6.refs_0_), channel_id=1, source_target_pairs={{0,1},{1,0},{2,3},{3,2},{4,5},{5,4},{6,7},{7,6},{8,9},{9,8},{10,11... | collective-permute-start | bytes 2408456 | tf_op jit(solution)/shard_map/ppermute | solution.py:26
  18.6 43.3 %collective-permute-start.9 = (bf16[49,16,4,128]{3,2,1,0:T(4,128)(2,1)}, bf16[49,16,4,128]{3,2,1,0:T(4,128)(2,1)S(1)}, u32[]{:S(2)}, u32[]{:S(2)}) collective-permute-start(bf16[49,16,4,128]{3,2,1,0:T(4,128)(2,1)} %pick.7.token_ref), channel_id=1, source_target_pairs={{0,1},{1,0},{2,3},{3,2},{4,5},{5,4},{6,7},{7,6},{8,9},{9,8},{10,11... | collective-permute-start | bytes 2408456 | tf_op jit(solution)/shard_map/ppermute | solution.py:26
  20.1 2.2 %copy-start = (bf16[64,16,4,2,256]{4,3,2,1,0:T(2,128)(2,1)S(1)}, bf16[64,16,4,2,256]{4,3,2,1,0:T(2,128)(2,1)}, u32[]{:S(2)}) copy-start(bf16[64,16,4,2,256]{4,3,2,1,0:T(2,128)(2,1)} %param.4) | copy-start | bytes 12582916
  22.3 1.1 %copy-start.2 = (bf16[49,16,4,128]{3,2,1,0:T(4,128)(2,1)S(1)}, bf16[49,16,4,128]{3,2,1,0:T(4,128)(2,1)}, u32[]{:S(2)}) copy-start(bf16[49,16,4,128]{3,2,1,0:T(4,128)(2,1)} %pick.7.token_ref) | copy-start | bytes 2408452
  28.1 6.7 %copy-start.1 = (bf16[64,16,4,2,256]{4,3,2,1,0:T(2,128)(2,1)S(1)}, bf16[64,16,4,2,256]{4,3,2,1,0:T(2,128)(2,1)}, u32[]{:S(2)}) copy-start(bf16[64,16,4,2,256]{4,3,2,1,0:T(2,128)(2,1)} %param.4) | copy-start | bytes 12582916
  31.2 7.5 %collective-permute-start.5 = (bf16[1,4,256,128]{3,2,1,0:T(8,128)(2,1)S(1)}, bf16[1,4,256,128]{3,2,1,0:T(8,128)(2,1)S(1)}, u32[]{:S(2)}, u32[]{:S(2)}) collective-permute-start(bf16[1,4,256,128]{3,2,1,0:T(8,128)(2,1)S(1)} %get-tuple-element.20.token_ref), channel_id=1, source_target_pairs={{0,2},{1,3},{2,0},{3,1},{4,6},{5,7},{6,4},{7,5},{8,10},{9,11},{10,... | collective-permute-start | bytes 786440 | tf_op jit(solution)/shard_map/ppermute | solution.py:26
  37.1 13.4 %collective-permute-start.7 = (bf16[1,4,256,128]{3,2,1,0:T(8,128)(2,1)S(1)}, bf16[1,4,256,128]{3,2,1,0:T(8,128)(2,1)S(1)}, u32[]{:S(2)}, u32[]{:S(2)}) collective-permute-start(bf16[1,4,256,128]{3,2,1,0:T(8,128)(2,1)S(1)} %get-tuple-element.27), channel_id=1, source_target_pairs={{0,2},{1,3},{2,0},{3,1},{4,6},{5,7},{6,4},{7,5},{8,10},{9,11},{10,... | collective-permute-start | bytes 786440 | tf_op jit(solution)/shard_map/ppermute | solution.py:26
  38.8 11.8 %collective-permute-start.8 = (bf16[1,4,256,128]{3,2,1,0:T(8,128)(2,1)S(1)}, bf16[1,4,256,128]{3,2,1,0:T(8,128)(2,1)S(1)}, u32[]{:S(2)}, u32[]{:S(2)}) collective-permute-start(bf16[1,4,256,128]{3,2,1,0:T(8,128)(2,1)S(1)} %merge.8.token_ref), channel_id=1, source_target_pairs={{0,4},{1,5},{2,6},{3,7},{4,0},{5,1},{6,2},{7,3},{8,12},{9,13},{10,... | collective-permute-start | bytes 786440 | tf_op jit(solution)/shard_map/ppermute | solution.py:26
  46.5 9.6 %collective-permute-start.6 = (bf16[1,4,256,128]{3,2,1,0:T(8,128)(2,1)S(1)}, bf16[1,4,256,128]{3,2,1,0:T(8,128)(2,1)S(1)}, u32[]{:S(2)}, u32[]{:S(2)}) collective-permute-start(bf16[1,4,256,128]{3,2,1,0:T(8,128)(2,1)S(1)} %get-tuple-element.26.refs_3_), channel_id=1, source_target_pairs={{0,2},{1,3},{2,0},{3,1},{4,6},{5,7},{6,4},{7,5},{8,10},{9,11},{10,... | collective-permute-start | bytes 786440 | tf_op jit(solution)/shard_map/ppermute | solution.py:26
  48.7 18.9 %collective-permute-start.3 = (bf16[1,4,256,128]{3,2,1,0:T(8,128)(2,1)S(1)}, bf16[1,4,256,128]{3,2,1,0:T(8,128)(2,1)S(1)}, u32[]{:S(2)}, u32[]{:S(2)}) collective-permute-start(bf16[1,4,256,128]{3,2,1,0:T(8,128)(2,1)S(1)} %get-tuple-element.23.token_ref), channel_id=1, source_target_pairs={{0,1},{1,0},{2,3},{3,2},{4,5},{5,4},{6,7},{7,6},{8,9},{9,8},{10,11... | collective-permute-start | bytes 786440 | tf_op jit(solution)/shard_map/ppermute | solution.py:26
  50.5 18.7 %collective-permute-start.12 = (bf16[1,4,256,128]{3,2,1,0:T(8,128)(2,1)S(1)}, bf16[1,4,256,128]{3,2,1,0:T(8,128)(2,1)S(1)}, u32[]{:S(2)}, u32[]{:S(2)}) collective-permute-start(bf16[1,4,256,128]{3,2,1,0:T(8,128)(2,1)S(1)} %get-tuple-element.30), channel_id=1, source_target_pairs={{0,2},{1,3},{2,0},{3,1},{4,6},{5,7},{6,4},{7,5},{8,10},{9,11},{10,... | collective-permute-start | bytes 786440 | tf_op jit(solution)/shard_map/ppermute | solution.py:26
  56.2 13.0 %collective-permute-start.13 = (bf16[1,4,256,128]{3,2,1,0:T(8,128)(2,1)S(1)}, bf16[1,4,256,128]{3,2,1,0:T(8,128)(2,1)S(1)}, u32[]{:S(2)}, u32[]{:S(2)}) collective-permute-start(bf16[1,4,256,128]{3,2,1,0:T(8,128)(2,1)S(1)} %merge.10.token_ref), channel_id=1, source_target_pairs={{0,4},{1,5},{2,6},{3,7},{4,0},{5,1},{6,2},{7,3},{8,12},{9,13},{10,... | collective-permute-start | bytes 786440 | tf_op jit(solution)/shard_map/ppermute | solution.py:26
  65.3 9.5 %collective-permute-start.11 = (bf16[1,4,256,128]{3,2,1,0:T(8,128)(2,1)S(1)}, bf16[1,4,256,128]{3,2,1,0:T(8,128)(2,1)S(1)}, u32[]{:S(2)}, u32[]{:S(2)}) collective-permute-start(bf16[1,4,256,128]{3,2,1,0:T(8,128)(2,1)S(1)} %get-tuple-element.28.refs_2_), channel_id=1, source_target_pairs={{0,2},{1,3},{2,0},{3,1},{4,6},{5,7},{6,4},{7,5},{8,10},{9,11},{10,... | collective-permute-start | bytes 786440 | tf_op jit(solution)/shard_map/ppermute | solution.py:26
  66.3 8.4 %collective-permute-start.2 = (bf16[1,4,256,128]{3,2,1,0:T(8,128)(2,1)S(1)}, bf16[1,4,256,128]{3,2,1,0:T(8,128)(2,1)S(1)}, u32[]{:S(2)}, u32[]{:S(2)}) collective-permute-start(bf16[1,4,256,128]{3,2,1,0:T(8,128)(2,1)S(1)} %get-tuple-element.22), channel_id=1, source_target_pairs={{0,1},{1,0},{2,3},{3,2},{4,5},{5,4},{6,7},{7,6},{8,9},{9,8},{10,11... | collective-permute-start | bytes 786440 | tf_op jit(solution)/shard_map/ppermute | solution.py:26
  67.6 8.2 %collective-permute-start.20 = (bf16[4,256,128]{2,1,0:T(8,128)(2,1)S(1)}, bf16[4,256,128]{2,1,0:T(8,128)(2,1)S(1)}, u32[]{:S(2)}, u32[]{:S(2)}) collective-permute-start(bf16[4,256,128]{2,1,0:T(8,128)(2,1)S(1)} %bitcast.20), channel_id=1, source_target_pairs={{0,16},{8,24},{16,0},{24,8},{1,17},{9,25},{17,1},{25,9},{2,18},{10... | collective-permute-start | bytes 786440 | tf_op jit(solution)/shard_map/ppermute | solution.py:26
  69.3 9.3 %collective-permute-start.23 = (bf16[4,256,128]{2,1,0:T(8,128)(2,1)S(1)}, bf16[4,256,128]{2,1,0:T(8,128)(2,1)S(1)}, u32[]{:S(2)}, u32[]{:S(2)}) collective-permute-start(bf16[4,256,128]{2,1,0:T(8,128)(2,1)S(1)} %bitcast.26), channel_id=1, source_target_pairs={{0,16},{8,24},{16,0},{24,8},{1,17},{9,25},{17,1},{25,9},{2,18},{10... | collective-permute-start | bytes 786440 | tf_op jit(solution)/shard_map/ppermute | solution.py:26
  70.8 11.4 %collective-permute-start.10 = (bf16[1,4,256,128]{3,2,1,0:T(8,128)(2,1)S(1)}, bf16[1,4,256,128]{3,2,1,0:T(8,128)(2,1)S(1)}, u32[]{:S(2)}, u32[]{:S(2)}) collective-permute-start(bf16[1,4,256,128]{3,2,1,0:T(8,128)(2,1)S(1)} %merge.11.refs_3_), channel_id=1, source_target_pairs={{0,4},{1,5},{2,6},{3,7},{4,0},{5,1},{6,2},{7,3},{8,12},{9,13},{10,... | collective-permute-start | bytes 786440 | tf_op jit(solution)/shard_map/ppermute | solution.py:26
  74.7 7.5 %collective-permute-start.19 = (bf16[4,256,128]{2,1,0:T(8,128)(2,1)S(1)}, bf16[4,256,128]{2,1,0:T(8,128)(2,1)S(1)}, u32[]{:S(2)}, u32[]{:S(2)}) collective-permute-start(bf16[4,256,128]{2,1,0:T(8,128)(2,1)S(1)} %bitcast.21), channel_id=1, source_target_pairs={{0,8},{8,0},{16,24},{24,16},{1,9},{9,1},{17,25},{25,17},{2,10},{10... | collective-permute-start | bytes 786440 | tf_op jit(solution)/shard_map/ppermute | solution.py:26
  74.8 10.5 %collective-permute-start.22 = (bf16[4,256,128]{2,1,0:T(8,128)(2,1)S(1)}, bf16[4,256,128]{2,1,0:T(8,128)(2,1)S(1)}, u32[]{:S(2)}, u32[]{:S(2)}) collective-permute-start(bf16[4,256,128]{2,1,0:T(8,128)(2,1)S(1)} %bitcast.27), channel_id=1, source_target_pairs={{0,8},{8,0},{16,24},{24,16},{1,9},{9,1},{17,25},{25,17},{2,10},{10... | collective-permute-start | bytes 786440 | tf_op jit(solution)/shard_map/ppermute | solution.py:26
  75.8 11.1 %collective-permute-start.21 = (bf16[4,256,128]{2,1,0:T(8,128)(2,1)S(1)}, bf16[4,256,128]{2,1,0:T(8,128)(2,1)S(1)}, u32[]{:S(2)}, u32[]{:S(2)}) collective-permute-start(bf16[4,256,128]{2,1,0:T(8,128)(2,1)S(1)} %collective-permute-done.20.refs_2_), channel_id=1, source_target_pairs={{0,8},{8,0},{16,24},{24,16},{1,9},{9,1},{17,25},{25,17},{2,10},{10... | collective-permute-start | bytes 786440 | tf_op jit(solution)/shard_map/ppermute | solution.py:26
  78.6 8.3 %collective-permute-start.24 = (bf16[4,256,128]{2,1,0:T(8,128)(2,1)S(1)}, bf16[4,256,128]{2,1,0:T(8,128)(2,1)S(1)}, u32[]{:S(2)}, u32[]{:S(2)}) collective-permute-start(bf16[4,256,128]{2,1,0:T(8,128)(2,1)S(1)} %collective-permute-done.23.refs_6_), channel_id=1, source_target_pairs={{0,8},{8,0},{16,24},{24,16},{1,9},{9,1},{17,25},{25,17},{2,10},{10... | collective-permute-start | bytes 786440 | tf_op jit(solution)/shard_map/ppermute | solution.py:26
  82.2 11.1 %collective-permute-start.17 = (bf16[1,4,256,128]{3,2,1,0:T(8,128)(2,1)S(1)}, bf16[1,4,256,128]{3,2,1,0:T(8,128)(2,1)S(1)}, u32[]{:S(2)}, u32[]{:S(2)}) collective-permute-start(bf16[1,4,256,128]{3,2,1,0:T(8,128)(2,1)S(1)} %get-tuple-element.31), channel_id=1, source_target_pairs={{0,2},{1,3},{2,0},{3,1},{4,6},{5,7},{6,4},{7,5},{8,10},{9,11},{10,... | collective-permute-start | bytes 786440 | tf_op jit(solution)/shard_map/ppermute | solution.py:26
  82.2 12.9 %collective-permute-start.18 = (bf16[1,4,256,128]{3,2,1,0:T(8,128)(2,1)S(1)}, bf16[1,4,256,128]{3,2,1,0:T(8,128)(2,1)S(1)}, u32[]{:S(2)}, u32[]{:S(2)}) collective-permute-start(bf16[1,4,256,128]{3,2,1,0:T(8,128)(2,1)S(1)} %merge.13.refs_3_), channel_id=1, source_target_pairs={{0,4},{1,5},{2,6},{3,7},{4,0},{5,1},{6,2},{7,3},{8,12},{9,13},{10,... | collective-permute-start | bytes 786440 | tf_op jit(solution)/shard_map/ppermute | solution.py:26
  85.3 17.0 %copy-start.7 = (s32[32,2]{0,1:T(2,128)S(1)}, s32[32,2]{0,1:T(2,128)}, u32[]{:S(2)}) copy-start(s32[32,2]{0,1:T(2,128)} %param.7) | copy-start | bytes 772
  85.3 12.2 %collective-permute-start.15 = (bf16[4,256,128]{2,1,0:T(8,128)(2,1)S(1)}, bf16[4,256,128]{2,1,0:T(8,128)(2,1)S(1)}, u32[]{:S(2)}, u32[]{:S(2)}) collective-permute-start(bf16[4,256,128]{2,1,0:T(8,128)(2,1)S(1)} %bitcast.23), channel_id=1, source_target_pairs={{0,16},{8,24},{16,0},{24,8},{1,17},{9,25},{17,1},{25,9},{2,18},{10... | collective-permute-start | bytes 786440 | tf_op jit(solution)/shard_map/ppermute | solution.py:26
  88.1 1.3 %copy-start.3 = (f32[8,256,256]{2,1,0:T(8,128)}, f32[8,256,256]{2,1,0:T(8,128)S(1)}, u32[]{:S(2)}) copy-start(f32[8,256,256]{2,1,0:T(8,128)S(1)} %get-tuple-element.34.refs_9_) | copy-start | bytes 6291460
  95.8 6.4 %collective-permute-start.26 = (bf16[4,256,128]{2,1,0:T(8,128)(2,1)S(1)}, bf16[4,256,128]{2,1,0:T(8,128)(2,1)S(1)}, u32[]{:S(2)}, u32[]{:S(2)}) collective-permute-start(bf16[4,256,128]{2,1,0:T(8,128)(2,1)S(1)} %bitcast.29), channel_id=1, source_target_pairs={{0,16},{8,24},{16,0},{24,8},{1,17},{9,25},{17,1},{25,9},{2,18},{10... | collective-permute-start | bytes 786440 | tf_op jit(solution)/shard_map/ppermute | solution.py:26
  97.4 5.1 %collective-permute-start.14 = (bf16[4,256,128]{2,1,0:T(8,128)(2,1)S(1)}, bf16[4,256,128]{2,1,0:T(8,128)(2,1)S(1)}, u32[]{:S(2)}, u32[]{:S(2)}) collective-permute-start(bf16[4,256,128]{2,1,0:T(8,128)(2,1)S(1)} %bitcast.24), channel_id=1, source_target_pairs={{0,8},{8,0},{16,24},{24,16},{1,9},{9,1},{17,25},{25,17},{2,10},{10... | collective-permute-start | bytes 786440 | tf_op jit(solution)/shard_map/ppermute | solution.py:26
  97.4 5.1 %collective-permute-start.16 = (bf16[4,256,128]{2,1,0:T(8,128)(2,1)S(1)}, bf16[4,256,128]{2,1,0:T(8,128)(2,1)}, u32[]{:S(2)}, u32[]{:S(2)}) collective-permute-start(bf16[4,256,128]{2,1,0:T(8,128)(2,1)S(1)} %collective-permute-done.15.refs_2_), channel_id=1, source_target_pairs={{0,8},{8,0},{16,24},{24,16},{1,9},{9,1},{17,25},{25,17},{2,10},{10... | collective-permute-start | bytes 786440 | tf_op jit(solution)/shard_map/ppermute | solution.py:26
  97.9 4.6 %collective-permute-start.25 = (bf16[4,256,128]{2,1,0:T(8,128)(2,1)S(1)}, bf16[4,256,128]{2,1,0:T(8,128)(2,1)}, u32[]{:S(2)}, u32[]{:S(2)}) collective-permute-start(bf16[4,256,128]{2,1,0:T(8,128)(2,1)S(1)} %bitcast.30), channel_id=1, source_target_pairs={{0,8},{8,0},{16,24},{24,16},{1,9},{9,1},{17,25},{25,17},{2,10},{10... | collective-permute-start | bytes 786440 | tf_op jit(solution)/shard_map/ppermute | solution.py:26
  102.3 1.7 %collective-permute-start.27 = (bf16[4,256,128]{2,1,0:T(8,128)(2,1)S(1)}, bf16[4,256,128]{2,1,0:T(8,128)(2,1)}, u32[]{:S(2)}, u32[]{:S(2)}) collective-permute-start(bf16[4,256,128]{2,1,0:T(8,128)(2,1)S(1)} %collective-permute-done.26.refs_6_), channel_id=1, source_target_pairs={{0,8},{8,0},{16,24},{24,16},{1,9},{9,1},{17,25},{25,17},{2,10},{10... | collective-permute-start | bytes 786440 | tf_op jit(solution)/shard_map/ppermute | solution.py:26
  104.0 1.6 %copy-start.4 = (f32[8,256,256]{2,1,0:T(8,128)S(1)}, f32[8,256,256]{2,1,0:T(8,128)}, u32[]{:S(2)}) copy-start(f32[8,256,256]{2,1,0:T(8,128)} %copy-done.3) | copy-start | bytes 6291460

commit v4 on v3

--- a/solution.py
+++ b/solution.py
@@ -34,7 +34,7 @@
     return first, sum(bit * (1 << k) for k, bit in enumerate(others))
 
 
-def pick_kernel(order, target_ref, table_ref, blocks_ref, *refs):
+def pick_kernel(order, target_ref, targets_ref, rows_ref, blocks_ref, *refs):
     out_ref = refs[-1]
     here = lax.axis_index("tile")
 
@@ -48,20 +48,20 @@
         return count + crosses
 
     lax.fori_loop(0, blocks_ref.shape[0], body, jnp.int32(0))
-    blocks = table_ref.shape[1]
+    blocks = targets_ref.shape[1]
     last = out_ref.shape[0] - 1
     parts, lanes = out_ref.shape[2:]
     table = jnp.zeros((parts, lanes), jnp.float32)
-    wide = jnp.concatenate(
-        [table_ref[...].astype(jnp.float32), jnp.zeros((2, lanes - blocks), jnp.float32)], axis=1
-    )
     row = lax.broadcasted_iota(jnp.int32, (parts, lanes), 0)
-    for k in range(2):
-        table = jnp.where(row == k, wide[k : k + 1], table)
+    for k, ref in enumerate((targets_ref, rows_ref)):
+        line = ref[...].astype(jnp.float32)
+        if lanes > blocks:
+            line = jnp.concatenate([line, jnp.zeros((1, lanes - blocks), jnp.float32)], axis=1)
+        table = jnp.where(row == k, line, table)
     out_ref[last, 0] = table.astype(out_ref.dtype)
 
 
-def pick(targets, table, view, chunk, slots, tokens):
+def pick(targets, first_rows, view, chunk, slots, tokens):
     date, order = chunk
     blocks, height, _, parts, lanes = view.shape
     return pl.pallas_call(
@@ -69,7 +69,8 @@
         grid=(1,),
         in_specs=[
             SMEM,
-            VMEM,
+            pl.BlockSpec((1, blocks), lambda i: (0, 0)),
+            pl.BlockSpec((1, blocks), lambda i: (0, 0)),
             pl.BlockSpec((blocks, height, 1, parts, lanes), lambda i: (0, 0, date, 0, 0)),
         ]
         + [ANY] * len(tokens),
@@ -78,7 +79,7 @@
         cost_estimate=CHEAP,
         compiler_params=params(PICK_MIB),
         name="pick",
-    )(targets, table, view, *tokens)
+    )(targets, targets.reshape(1, blocks), first_rows.reshape(1, blocks), view, *tokens)
 
 
 def own_kernel(date, order, target_ref, row_ref, view_ref, token_ref, acc_ref, own_ref, sem):
@@ -267,31 +268,20 @@
     return jnp.concatenate(sides, axis=-1).astype(jnp.float32)
 
 
-def power_box(box, ref, cols):
-    halves = cols // LANES
-    u0, u1 = component(ref, 0, halves), component(ref, 1, halves)
-    return box(u0 * u0 + u1 * u1)
-
-
-def early_kernel(*refs):
-    *field_refs, token_ref, stack_ref, power_ref, end_ref = refs
-    del token_ref
+def collect_kernel(*refs):
+    *field_refs, _, stack_ref, end_ref = refs
     end_ref[0] = 0
-    cols = power_ref.shape[2]
-    box = boxes(cols)
     for k, ref in enumerate(field_refs):
         stack_ref[k] = ref[...]
-        power_ref[k] = power_box(box, ref, cols)
-
-
-def collect(fields, rows, cols, token):
-    return pl.pallas_call(
-        early_kernel,
+
+
+def collect(fields, token):
+    return pl.pallas_call(
+        collect_kernel,
         in_specs=[VMEM] * len(fields) + [ANY],
-        out_specs=[VMEM, VMEM, SMEM],
+        out_specs=[VMEM, SMEM],
         out_shape=[
             jax.ShapeDtypeStruct((len(fields),) + fields[0].shape, fields[0].dtype),
-            jax.ShapeDtypeStruct((len(fields), rows, cols), jnp.float32),
             jax.ShapeDtypeStruct((1,), jnp.int32),
         ],
         cost_estimate=CHEAP,
@@ -301,7 +291,7 @@
 
 
 def coherence_kernel(pairs_ref, *refs):
-    *field_refs, stack_ref, power_ref, out_ref, stack, power, done, sems = refs
+    *field_refs, stack_ref, out_ref, stack, done, sems = refs
     rows, pairs, cols = out_ref.shape
     halves = cols // LANES
     strips = rows // SUBLANES
@@ -309,10 +299,8 @@
     early = stack_ref.shape[0]
     for k in range(early):
         stack[k] = stack_ref[k]
-        power[k] = power_ref[k]
     for k, ref in enumerate(field_refs):
         stack[early + k] = ref[...]
-        power[early + k] = power_box(box, ref, cols)
     for p in range(pairs):
         first, second = pairs_ref[2 * p], pairs_ref[2 * p + 1]
         u, v = stack.at[first], stack.at[second]
@@ -320,8 +308,10 @@
         v0, v1 = component(v, 0, halves), component(v, 1, halves)
         box_re = box(u0 * v0 + u1 * v1)
         box_im = box(u1 * v0 - u0 * v1)
+        box_a = box(u0 * u0 + u1 * u1)
+        box_e = box(v0 * v0 + v1 * v1)
         value = jnp.sqrt(box_re * box_re + box_im * box_im) * lax.rsqrt(
-            jnp.maximum(power[first] * power[second], 1.0)
+            jnp.maximum(box_a * box_e, 1.0)
         )
         for half in range(halves):
             side = done.at[half].reshape(rows * pairs, LANES)
@@ -338,23 +328,22 @@
         copy.wait()
 
 
-def coherence(pairs, fields, stack, power, out_shape):
+def coherence(pairs, fields, stack, out_shape):
     rows, pair_count, cols = out_shape
     total = len(fields) + stack.shape[0]
     return pl.pallas_call(
         coherence_kernel,
-        in_specs=[SMEM] + [VMEM] * (len(fields) + 2),
+        in_specs=[SMEM] + [VMEM] * (len(fields) + 1),
         out_specs=ANY,
         out_shape=jax.ShapeDtypeStruct(out_shape, jnp.float32),
         scratch_shapes=[
             pltpu.VMEM((total,) + fields[0].shape, fields[0].dtype),
-            pltpu.VMEM((total, rows, cols), jnp.float32),
             pltpu.VMEM((cols // LANES, rows, pair_count, LANES), jnp.float32),
             pltpu.SemaphoreType.DMA((cols // LANES,)),
         ],
         compiler_params=params(LAST_MIB),
         name="coherence",
-    )(pairs, *fields, stack, power)
+    )(pairs, *fields, stack)
 
 
 def chunk_plan(dates, bits):
@@ -387,10 +376,18 @@
 
     chunks = chunk_plan(dates_here, bits)
     targets = destination_panel[:, 0]
-    table = jnp.stack([targets, panel_line_shift])
     order = ORDER
     if len(order) != len(chunks) * stages:
         order = [c for _, c in sorted((2 * k + c, c) for c in range(len(chunks)) for k in range(stages))]
+    slot_of = [0] * dates_here
+    finishing = [c for k, c in enumerate(order) if c not in order[k + 1 :]]
+    for k, c in enumerate(finishing):
+        slot_of[chunks[c][0]] = k * group_count
+    pairs_here = epoch_couples.shape[0] // group_count
+    mine = lax.dynamic_slice_in_dim(epoch_couples, group * pairs_here, pairs_here, axis=0)
+    date = mine % dates_here
+    slot = sum([jnp.where(date == k, first, 0) for k, first in enumerate(slot_of)], jnp.zeros_like(date))
+    place = (slot + jnp.bitwise_xor(mine // dates_here, group)).reshape(-1)
     state = [None] * len(chunks)
     step = [0] * len(chunks)
     fields = [None] * dates_here
@@ -402,7 +399,7 @@
         step[c] += 1
         flip = [lambda value, bit=bit: swap(value, "tile", 1 << bit) for bit in bit_order]
         if k == 0:
-            token = pick(targets, table, view, chunks[c], slots, tokens)
+            token = pick(targets, panel_line_shift, view, chunks[c], slots, tokens)
             tokens = [token]
             state[c] = flip[0](token)
             continue
@@ -430,7 +427,7 @@
             continue
         if len(finished) == len(chunks) - 1:
             held = [fields[chunks[e][0]][g] for e in finished[:-1] for g in range(group_count)]
-            stack, power, token = collect(held, TR, cols, token)
+            stack, token = collect(held, token)
         finished.append(c)
         token = merge(addends + [(far, range(1))], view.dtype, token)
         known = {0: token[0]}
@@ -441,15 +438,7 @@
         fields[date] = known
 
     late = [fields[chunks[e][0]][g] for e in finished[-2:] for g in range(group_count)]
-    slot_of = [0] * dates_here
-    for k, e in enumerate(finished):
-        slot_of[chunks[e][0]] = k * group_count
-    pairs_here = epoch_couples.shape[0] // group_count
-    mine = lax.dynamic_slice_in_dim(epoch_couples, group * pairs_here, pairs_here, axis=0)
-    date = mine % dates_here
-    slot = sum([jnp.where(date == k, first, 0) for k, first in enumerate(slot_of)], jnp.zeros_like(date))
-    place = slot + jnp.bitwise_xor(mine // dates_here, group)
-    return coherence(place.reshape(-1), late, stack, power, (TR, pairs_here, cols))
+    return coherence(place, late, stack, (TR, pairs_here, cols))
 
 
 def solution(mesh):

time: 114 us -> 112 us (0.982)
  waiting for transfers between devices: 28.6 us -> 31.6 us
  local copies, waits for them, and re-layouts: 6.42 us -> 3.51 us
  other arithmetic: 1.31 us -> 0.08 us
    ppermute x28, waiting for transfers between devices: 28.6 us -> 31.6 us  [swap(): return lax.ppermute(value, axis, pairs)]
    unnamed x16 -> x12, local copies, waits for them, and re-layouts: 6.25 us -> 3.35 us
    another operation x1 -> x0, other arithmetic: 1.22 us -> none  [local(): table = jnp.stack([targets, panel_line_shift])]
  transfers between devices with their start and end apart: 28 -> 28, of which waited for: 11 -> 11; matrix products, arithmetic and copies ran while one was open for 0% -> 0% of each run, Pallas kernels for 30% -> 29%
where the time goes in v4:
time: 112 us
  Pallas kernels  44 us (39%)
  starting transfers between devices  32.3 us (29%)
  waiting for transfers between devices  31.6 us (28%)
  local copies, waits for them, and re-layouts  3.51 us (3%)
    ppermute x28, starting transfers between devices, swap(): return lax.ppermute(value, axis, pairs)  32.3 us
    ppermute x28, waiting for transfers between devices, swap(): return lax.ppermute(value, axis, pairs)  31.6 us
    pallas_call x4, Pallas kernels, pick(): pl.pallas_call(functools.partial(pick_kernel, order), grid=(1,), in_specs...  12.4 us
    pallas_call x4, Pallas kernels, deposit(): pl.pallas_call(functools.partial(deposit_kernel, order, blocks), in_specs...  12.3 us
    pallas_call x4, Pallas kernels, own_sums(): pl.pallas_call(functools.partial(own_kernel, date, order), in_specs=[SMEM...  8.92 us
    pallas_call x1, Pallas kernels, coherence(): pl.pallas_call(coherence_kernel, in_specs=[SMEM] + [VMEM] * (len(fields)...  8.45 us
    unnamed x12, local copies, waits for them, and re-layouts  3.35 us
  transfers between devices with their start and end apart: 28, of which 11 were waited for; matrix products, arithmetic and copies ran while one was open for 0% of the time, Pallas kernels for 29%

profile of v4, /device:TPU:0, one launch (start us, length us, event | category | flops | bytes accessed | tf_op | source)
XLA Modules:
  0.0 111.8 jit_solution(15294934622556205525)
XLA Ops:
  0.0 3.1 %pick.4.refs_0_ = bf16[49,16,4,128]{3,2,1,0:T(4,128)(2,1)} custom-call(s32[64]{0:T(128)} %bitcast.32, s32[1,64]{1,0:T(1,128)} %bitcast.33, s32[1,64]{1,0:T(1,128)} %bitcast.44, bf16[64,16,4,4,128]{4,3,2,1,0:T(4,128)(2,1)} %bitcast.12), custom_call_target="tpu_custom_call" | custom-call | flops 1 | bytes 1 | tf_op jit(solution)/shard_map/pick/pallas_call | solution.py:67
  3.1 2.9 %collective-permute-start.1 = (bf16[49,16,4,128]{3,2,1,0:T(4,128)(2,1)}, bf16[49,16,4,128]{3,2,1,0:T(4,128)(2,1)S(1)}, u32[]{:S(2)}, u32[]{:S(2)}) collective-permute-start(bf16[49,16,4,128]{3,2,1,0:T(4,128)(2,1)} %pick.4.refs_0_), channel_id=1, source_target_pairs={{0,1},{1,0},{2,3},{3,2},{4,5},{5,4},{6,7},{7,6},{8,9},{9,8},{10,11... | collective-permute-start | bytes 2408456 | tf_op jit(solution)/shard_map/ppermute | solution.py:26
  6.0 3.1 %pick.5.refs_0_ = bf16[49,16,4,128]{3,2,1,0:T(4,128)(2,1)} custom-call(s32[64]{0:T(128)} %bitcast.34, s32[1,64]{1,0:T(1,128)} %bitcast.35, s32[1,64]{1,0:T(1,128)} %bitcast.45, bf16[64,16,4,4,128]{4,3,2,1,0:T(4,128)(2,1)} %bitcast.13, bf16[49,16,4,128]{3,2,1,0:T(4,128)(2,1)} %pick.4.refs_0_), custom_call_target="tpu_custom_call" | custom-call | flops 1 | bytes 1 | tf_op jit(solution)/shard_map/pick/pallas_call | solution.py:67
  9.2 1.6 %collective-permute-start = (bf16[49,16,4,128]{3,2,1,0:T(4,128)(2,1)}, bf16[49,16,4,128]{3,2,1,0:T(4,128)(2,1)S(1)}, u32[]{:S(2)}, u32[]{:S(2)}) collective-permute-start(bf16[49,16,4,128]{3,2,1,0:T(4,128)(2,1)} %pick.5.refs_0_), channel_id=1, source_target_pairs={{0,2},{1,3},{2,0},{3,1},{4,6},{5,7},{6,4},{7,5},{8,10},{9,11},{10,... | collective-permute-start | bytes 2408456 | tf_op jit(solution)/shard_map/ppermute | solution.py:26
  10.8 3.1 %pick.6.refs_0_ = bf16[49,16,4,128]{3,2,1,0:T(4,128)(2,1)} custom-call(s32[64]{0:T(128)} %bitcast.36, s32[1,64]{1,0:T(1,128)} %bitcast.37, s32[1,64]{1,0:T(1,128)} %bitcast.46, bf16[64,16,4,4,128]{4,3,2,1,0:T(4,128)(2,1)} %bitcast.14, bf16[49,16,4,128]{3,2,1,0:T(4,128)(2,1)} %pick.5.refs_0_), custom_call_target="tpu_custom_call" | custom-call | flops 1 | bytes 1 | tf_op jit(solution)/shard_map/pick/pallas_call | solution.py:67
  13.9 0.5 collective-permute-start.4
  14.4 3.1 %pick.7.token_ref = bf16[49,16,4,128]{3,2,1,0:T(4,128)(2,1)} custom-call(s32[64]{0:T(128)} %bitcast.38, s32[1,64]{1,0:T(1,128)} %bitcast.39, s32[1,64]{1,0:T(1,128)} %bitcast.47, bf16[64,16,4,4,128]{4,3,2,1,0:T(4,128)(2,1)} %bitcast.15, bf16[49,16,4,128]{3,2,1,0:T(4,128)(2,1)} %pick.6.refs_0_), custom_call_target="tpu_custom_call" | custom-call | flops 1 | bytes 1 | tf_op jit(solution)/shard_map/pick/pallas_call | solution.py:67
  17.5 1.5 %collective-permute-start.9 = (bf16[49,16,4,128]{3,2,1,0:T(4,128)(2,1)}, bf16[49,16,4,128]{3,2,1,0:T(4,128)(2,1)S(1)}, u32[]{:S(2)}, u32[]{:S(2)}) collective-permute-start(bf16[49,16,4,128]{3,2,1,0:T(4,128)(2,1)} %pick.7.token_ref), channel_id=1, source_target_pairs={{0,1},{1,0},{2,3},{3,2},{4,5},{5,4},{6,7},{7,6},{8,9},{9,8},{10,11... | collective-permute-start | bytes 2408456 | tf_op jit(solution)/shard_map/ppermute | solution.py:26
  19.0 2.2 %copy-done = bf16[64,16,4,2,256]{4,3,2,1,0:T(2,128)(2,1)S(1)} copy-done((bf16[64,16,4,2,256]{4,3,2,1,0:T(2,128)(2,1)S(1)}, bf16[64,16,4,2,256]{4,3,2,1,0:T(2,128)(2,1)}, u32[]{:S(2)}) %copy-start) | copy-done | bytes 4194328
  21.2 1.1 %copy-done.2 = bf16[49,16,4,128]{3,2,1,0:T(4,128)(2,1)S(1)} copy-done((bf16[49,16,4,128]{3,2,1,0:T(4,128)(2,1)S(1)}, bf16[49,16,4,128]{3,2,1,0:T(4,128)(2,1)}, u32[]{:S(2)}) %copy-start.2) | copy-done | bytes 802840
  22.4 2.2 %own.4.token_ref.sums_ref = f32[4,256,4,128]{3,2,1,0:T(4,128)S(1)} custom-call(s32[64]{0:T(128)S(1)} %bitcast.40, s32[64]{0:T(128)S(1)} %copy-done.4, bf16[64,16,4,4,128]{4,3,2,1,0:T(4,128)(2,1)S(1)} %bitcast.16, bf16[49,16,4,128]{3,2,1,0:T(4,128)(2,1)S(1)} %copy-done.2), custom_call_target="tpu_custom_call" | custom-call | flops 1 | bytes 1 | tf_op jit(solution)/shard_map/own/pallas_call | solution.py:117
  24.6 2.2 %own.5.token_ref.sums_ref = f32[4,256,4,128]{3,2,1,0:T(4,128)S(1)} custom-call(s32[64]{0:T(128)S(1)} %bitcast.41, s32[64]{0:T(128)S(1)} %copy-done.4, bf16[64,16,4,4,128]{4,3,2,1,0:T(4,128)(2,1)S(1)} %bitcast.17, f32[4,256,4,128]{3,2,1,0:T(4,128)S(1)} %own.4.token_ref.sums_ref), custom_call_target="tpu_custom_call" | custom-call | flops 1 | bytes 1 | tf_op jit(solution)/shard_map/own/pallas_call | solution.py:117
  26.8 0.0 collective-permute-done.1.got_ref
  26.8 0.0 copy-start.1
  26.9 3.0 %deposit.4 = (bf16[1,4,256,128]{3,2,1,0:T(8,128)(2,1)S(1)}, bf16[1,4,256,128]{3,2,1,0:T(8,128)(2,1)S(1)}, f32[2,4,256,128]{3,2,1,0:T(8,128)S(1)}) custom-call(f32[4,256,4,128]{3,2,1,0:T(4,128)S(1)} %own.4.token_ref.sums_ref, bf16[49,16,4,128]{3,2,1,0:T(4,128)(2,1)S(1)} %collective-permute-done.1.got_ref, f32[4,256,4,128]{3,2,1,0:T(4,128)S(1)} %own.5.token_ref.sums_ref), custom_call_target="tpu_custom_call" | custom-call | flops 1 | bytes 1 | tf_op jit(solution)/shard_map/deposit/pallas_call | solution.py:190
  29.9 0.6 collective-permute-start.5
  30.5 3.1 %deposit.5 = (bf16[1,4,256,128]{3,2,1,0:T(8,128)(2,1)S(1)}, bf16[1,4,256,128]{3,2,1,0:T(8,128)(2,1)S(1)}, f32[2,4,256,128]{3,2,1,0:T(8,128)S(1)}) custom-call(f32[4,256,4,128]{3,2,1,0:T(4,128)S(1)} %own.5.token_ref.sums_ref, bf16[49,16,4,128]{3,2,1,0:T(4,128)(2,1)S(1)} %collective-permute-done.got_ref, bf16[1,4,256,128]{3,2,1,0:T(8,128)(2,1)S(1)} %get-tuple-element.19.token_ref), custom_call_target="tpu_custom_call" | custom-call | flops 1 | bytes 1 | tf_op jit(solution)/shard_map/deposit/pallas_call | solution.py:190
  33.6 2.2 %own.6.refs_2_.sums_ref = f32[4,256,4,128]{3,2,1,0:T(4,128)S(1)} custom-call(s32[64]{0:T(128)S(1)} %bitcast.42, s32[64]{0:T(128)S(1)} %copy-done.4, bf16[64,16,4,4,128]{4,3,2,1,0:T(4,128)(2,1)S(1)} %bitcast.18, bf16[1,4,256,128]{3,2,1,0:T(8,128)(2,1)S(1)} %get-tuple-element.22.token_ref), custom_call_target="tpu_custom_call" | custom-call | flops 1 | bytes 1 | tf_op jit(solution)/shard_map/own/pallas_call | solution.py:117
  35.8 1.6 %collective-permute-start.7 = (bf16[1,4,256,128]{3,2,1,0:T(8,128)(2,1)S(1)}, bf16[1,4,256,128]{3,2,1,0:T(8,128)(2,1)S(1)}, u32[]{:S(2)}, u32[]{:S(2)}) collective-permute-start(bf16[1,4,256,128]{3,2,1,0:T(8,128)(2,1)S(1)} %get-tuple-element.26), channel_id=1, source_target_pairs={{0,2},{1,3},{2,0},{3,1},{4,6},{5,7},{6,4},{7,5},{8,10},{9,11},{10,... | collective-permute-start | bytes 786440 | tf_op jit(solution)/shard_map/ppermute | solution.py:26
  37.4 0.0 collective-permute-done.5.refs_1_
  37.5 2.7 %collective-permute-start.8 = (bf16[1,4,256,128]{3,2,1,0:T(8,128)(2,1)S(1)}, bf16[1,4,256,128]{3,2,1,0:T(8,128)(2,1)S(1)}, u32[]{:S(2)}, u32[]{:S(2)}) collective-permute-start(bf16[1,4,256,128]{3,2,1,0:T(8,128)(2,1)S(1)} %merge.8.token_ref), channel_id=1, source_target_pairs={{0,4},{1,5},{2,6},{3,7},{4,0},{5,1},{6,2},{7,3},{8,12},{9,13},{10,... | collective-permute-start | bytes 786440 | tf_op jit(solution)/shard_map/ppermute | solution.py:26
  40.1 2.0 %collective-permute-done.4.got_ref = bf16[49,16,4,128]{3,2,1,0:T(4,128)(2,1)S(1)} collective-permute-done((bf16[49,16,4,128]{3,2,1,0:T(4,128)(2,1)}, bf16[49,16,4,128]{3,2,1,0:T(4,128)(2,1)S(1)}, u32[]{:S(2)}, u32[]{:S(2)}) %collective-permute-start.4) | collective-permute-done | bytes 802848 | tf_op jit(solution)/shard_map/ppermute | solution.py:26
  42.2 3.0 %deposit.6 = (bf16[1,4,256,128]{3,2,1,0:T(8,128)(2,1)S(1)}, bf16[1,4,256,128]{3,2,1,0:T(8,128)(2,1)S(1)}, f32[2,4,256,128]{3,2,1,0:T(8,128)S(1)}) custom-call(f32[4,256,4,128]{3,2,1,0:T(4,128)S(1)} %own.6.refs_2_.sums_ref, bf16[49,16,4,128]{3,2,1,0:T(4,128)(2,1)S(1)} %collective-permute-done.4.got_ref, bf16[1,4,256,128]{3,2,1,0:T(8,128)(2,1)S(1)} %merge.8.token_ref), custom_call_target="tpu_custom_call" | custom-call | flops 1 | bytes 1 | tf_op jit(solution)/shard_map/deposit/pallas_call | solution.py:190
  45.2 2.2 %collective-permute-start.6 = (bf16[1,4,256,128]{3,2,1,0:T(8,128)(2,1)S(1)}, bf16[1,4,256,128]{3,2,1,0:T(8,128)(2,1)S(1)}, u32[]{:S(2)}, u32[]{:S(2)}) collective-permute-start(bf16[1,4,256,128]{3,2,1,0:T(8,128)(2,1)S(1)} %get-tuple-element.25.refs_3_), channel_id=1, source_target_pairs={{0,2},{1,3},{2,0},{3,1},{4,6},{5,7},{6,4},{7,5},{8,10},{9,11},{10,... | collective-permute-start | bytes 786440 | tf_op jit(solution)/shard_map/ppermute | solution.py:26
  47.4 1.6 %collective-permute-start.3 = (bf16[1,4,256,128]{3,2,1,0:T(8,128)(2,1)S(1)}, bf16[1,4,256,128]{3,2,1,0:T(8,128)(2,1)S(1)}, u32[]{:S(2)}, u32[]{:S(2)}) collective-permute-start(bf16[1,4,256,128]{3,2,1,0:T(8,128)(2,1)S(1)} %get-tuple-element.22.token_ref), channel_id=1, source_target_pairs={{0,1},{1,0},{2,3},{3,2},{4,5},{5,4},{6,7},{7,6},{8,9},{9,8},{10,11... | collective-permute-start | bytes 786440 | tf_op jit(solution)/shard_map/ppermute | solution.py:26
  49.0 0.1 collective-permute-done.7.refs_1_
  49.1 0.3 collective-permute-start.12
  49.5 0.0 collective-permute-done.8.refs_2_
  49.5 0.1 merge.9.refs_2_
  49.6 5.2 %collective-permute-done.6.refs_1_ = bf16[1,4,256,128]{3,2,1,0:T(8,128)(2,1)S(1)} collective-permute-done((bf16[1,4,256,128]{3,2,1,0:T(8,128)(2,1)S(1)}, bf16[1,4,256,128]{3,2,1,0:T(8,128)(2,1)S(1)}, u32[]{:S(2)}, u32[]{:S(2)}) %collective-permute-start.6) | collective-permute-done | bytes 262176 | tf_op jit(solution)/shard_map/ppermute | solution.py:26
  54.8 3.5 %collective-permute-start.13 = (bf16[1,4,256,128]{3,2,1,0:T(8,128)(2,1)S(1)}, bf16[1,4,256,128]{3,2,1,0:T(8,128)(2,1)S(1)}, u32[]{:S(2)}, u32[]{:S(2)}) collective-permute-start(bf16[1,4,256,128]{3,2,1,0:T(8,128)(2,1)S(1)} %merge.10.token_ref), channel_id=1, source_target_pairs={{0,4},{1,5},{2,6},{3,7},{4,0},{5,1},{6,2},{7,3},{8,12},{9,13},{10,... | collective-permute-start | bytes 786440 | tf_op jit(solution)/shard_map/ppermute | solution.py:26
  58.3 2.2 %own.7.sums_ref.token_ref = f32[4,256,4,128]{3,2,1,0:T(4,128)S(1)} custom-call(s32[64]{0:T(128)S(1)} %bitcast.43, s32[64]{0:T(128)S(1)} %copy-done.4, bf16[64,16,4,4,128]{4,3,2,1,0:T(4,128)(2,1)S(1)} %bitcast.19, bf16[1,4,256,128]{3,2,1,0:T(8,128)(2,1)S(1)} %merge.10.token_ref), custom_call_target="tpu_custom_call" | custom-call | flops 1 | bytes 1 | tf_op jit(solution)/shard_map/own/pallas_call | solution.py:117
  60.6 0.0 collective-permute-done.9.got_ref
  60.6 3.2 %deposit.7 = (bf16[1,4,256,128]{3,2,1,0:T(8,128)(2,1)S(1)}, bf16[1,4,256,128]{3,2,1,0:T(8,128)(2,1)S(1)}, f32[2,4,256,128]{3,2,1,0:T(8,128)S(1)}) custom-call(f32[4,256,4,128]{3,2,1,0:T(4,128)S(1)} %own.7.sums_ref.token_ref, bf16[49,16,4,128]{3,2,1,0:T(4,128)(2,1)S(1)} %collective-permute-done.9.got_ref, f32[4,256,4,128]{3,2,1,0:T(4,128)S(1)} %own.7.sums_ref.token_ref), custom_call_target="tpu_custom_call" | custom-call | flops 1 | bytes 1 | tf_op jit(solution)/shard_map/deposit/pallas_call | solution.py:190
  63.8 1.1 %collective-permute-start.11 = (bf16[1,4,256,128]{3,2,1,0:T(8,128)(2,1)S(1)}, bf16[1,4,256,128]{3,2,1,0:T(8,128)(2,1)S(1)}, u32[]{:S(2)}, u32[]{:S(2)}) collective-permute-start(bf16[1,4,256,128]{3,2,1,0:T(8,128)(2,1)S(1)} %get-tuple-element.27.refs_2_), channel_id=1, source_target_pairs={{0,2},{1,3},{2,0},{3,1},{4,6},{5,7},{6,4},{7,5},{8,10},{9,11},{10,... | collective-permute-start | bytes 786440 | tf_op jit(solution)/shard_map/ppermute | solution.py:26
  64.9 1.7 %collective-permute-start.2 = (bf16[1,4,256,128]{3,2,1,0:T(8,128)(2,1)S(1)}, bf16[1,4,256,128]{3,2,1,0:T(8,128)(2,1)S(1)}, u32[]{:S(2)}, u32[]{:S(2)}) collective-permute-start(bf16[1,4,256,128]{3,2,1,0:T(8,128)(2,1)S(1)} %get-tuple-element.21), channel_id=1, source_target_pairs={{0,1},{1,0},{2,3},{3,2},{4,5},{5,4},{6,7},{7,6},{8,9},{9,8},{10,11... | collective-permute-start | bytes 786440 | tf_op jit(solution)/shard_map/ppermute | solution.py:26
  66.6 1.5 %collective-permute-start.20 = (bf16[4,256,128]{2,1,0:T(8,128)(2,1)S(1)}, bf16[4,256,128]{2,1,0:T(8,128)(2,1)S(1)}, u32[]{:S(2)}, u32[]{:S(2)}) collective-permute-start(bf16[4,256,128]{2,1,0:T(8,128)(2,1)S(1)} %bitcast.20), channel_id=1, source_target_pairs={{0,16},{8,24},{16,0},{24,8},{1,17},{9,25},{17,1},{25,9},{2,18},{10... | collective-permute-start | bytes 786440 | tf_op jit(solution)/shard_map/ppermute | solution.py:26
  68.2 0.0 collective-permute-done.12.refs_1_
  68.2 0.1 merge.12.refs_2_
  68.3 1.2 %collective-permute-start.23 = (bf16[4,256,128]{2,1,0:T(8,128)(2,1)S(1)}, bf16[4,256,128]{2,1,0:T(8,128)(2,1)S(1)}, u32[]{:S(2)}, u32[]{:S(2)}) collective-permute-start(bf16[4,256,128]{2,1,0:T(8,128)(2,1)S(1)} %bitcast.26), channel_id=1, source_target_pairs={{0,16},{8,24},{16,0},{24,8},{1,17},{9,25},{17,1},{25,9},{2,18},{10... | collective-permute-start | bytes 786440 | tf_op jit(solution)/shard_map/ppermute | solution.py:26
  69.5 1.7 %collective-permute-start.10 = (bf16[1,4,256,128]{3,2,1,0:T(8,128)(2,1)S(1)}, bf16[1,4,256,128]{3,2,1,0:T(8,128)(2,1)S(1)}, u32[]{:S(2)}, u32[]{:S(2)}) collective-permute-start(bf16[1,4,256,128]{3,2,1,0:T(8,128)(2,1)S(1)} %merge.11.refs_3_), channel_id=1, source_target_pairs={{0,4},{1,5},{2,6},{3,7},{4,0},{5,1},{6,2},{7,3},{8,12},{9,13},{10,... | collective-permute-start | bytes 786440 | tf_op jit(solution)/shard_map/ppermute | solution.py:26
  71.2 2.2 %collective-permute-done.11.refs_1_ = bf16[1,4,256,128]{3,2,1,0:T(8,128)(2,1)S(1)} collective-permute-done((bf16[1,4,256,128]{3,2,1,0:T(8,128)(2,1)S(1)}, bf16[1,4,256,128]{3,2,1,0:T(8,128)(2,1)S(1)}, u32[]{:S(2)}, u32[]{:S(2)}) %collective-permute-start.11) | collective-permute-done | bytes 262176 | tf_op jit(solution)/shard_map/ppermute | solution.py:26
  73.5 0.6 collective-permute-start.22
  74.0 0.6 collective-permute-done.20.refs_2_
  74.7 2.8 %collective-permute-done.23.refs_6_ = bf16[4,256,128]{2,1,0:T(8,128)(2,1)S(1)} collective-permute-done((bf16[4,256,128]{2,1,0:T(8,128)(2,1)S(1)}, bf16[4,256,128]{2,1,0:T(8,128)(2,1)S(1)}, u32[]{:S(2)}, u32[]{:S(2)}) %collective-permute-start.23) | collective-permute-done | bytes 262176 | tf_op jit(solution)/shard_map/ppermute | solution.py:26
  77.5 3.4 %collective-permute-done.10.refs_2_ = bf16[1,4,256,128]{3,2,1,0:T(8,128)(2,1)S(1)} collective-permute-done((bf16[1,4,256,128]{3,2,1,0:T(8,128)(2,1)S(1)}, bf16[1,4,256,128]{3,2,1,0:T(8,128)(2,1)S(1)}, u32[]{:S(2)}, u32[]{:S(2)}) %collective-permute-start.10) | collective-permute-done | bytes 262176 | tf_op jit(solution)/shard_map/ppermute | solution.py:26
  80.9 3.3 %collective-permute-start.18 = (bf16[1,4,256,128]{3,2,1,0:T(8,128)(2,1)S(1)}, bf16[1,4,256,128]{3,2,1,0:T(8,128)(2,1)S(1)}, u32[]{:S(2)}, u32[]{:S(2)}) collective-permute-start(bf16[1,4,256,128]{3,2,1,0:T(8,128)(2,1)S(1)} %merge.13.refs_3_), channel_id=1, source_target_pairs={{0,4},{1,5},{2,6},{3,7},{4,0},{5,1},{6,2},{7,3},{8,12},{9,13},{10,... | collective-permute-start | bytes 786440 | tf_op jit(solution)/shard_map/ppermute | solution.py:26
  84.2 0.1 merge.14.refs_8_
  84.3 0.0 copy-start.5
  84.3 1.3 %collective-permute-start.15 = (bf16[4,256,128]{2,1,0:T(8,128)(2,1)S(1)}, bf16[4,256,128]{2,1,0:T(8,128)(2,1)S(1)}, u32[]{:S(2)}, u32[]{:S(2)}) collective-permute-start(bf16[4,256,128]{2,1,0:T(8,128)(2,1)S(1)} %bitcast.23), channel_id=1, source_target_pairs={{0,16},{8,24},{16,0},{24,8},{1,17},{9,25},{17,1},{25,9},{2,18},{10... | collective-permute-start | bytes 786440 | tf_op jit(solution)/shard_map/ppermute | solution.py:26
  85.7 0.7 collect.1
  86.3 5.5 %collective-permute-done.17.refs_1_ = bf16[1,4,256,128]{3,2,1,0:T(8,128)(2,1)S(1)} collective-permute-done((bf16[1,4,256,128]{3,2,1,0:T(8,128)(2,1)S(1)}, bf16[1,4,256,128]{3,2,1,0:T(8,128)(2,1)S(1)}, u32[]{:S(2)}, u32[]{:S(2)}) %collective-permute-start.17) | collective-permute-done | bytes 262176 | tf_op jit(solution)/shard_map/ppermute | solution.py:26
  91.9 2.5 %collective-permute-done.18.refs_2_ = bf16[1,4,256,128]{3,2,1,0:T(8,128)(2,1)S(1)} collective-permute-done((bf16[1,4,256,128]{3,2,1,0:T(8,128)(2,1)S(1)}, bf16[1,4,256,128]{3,2,1,0:T(8,128)(2,1)S(1)}, u32[]{:S(2)}, u32[]{:S(2)}) %collective-permute-start.18) | collective-permute-done | bytes 262176 | tf_op jit(solution)/shard_map/ppermute | solution.py:26
  94.4 0.7 merge.15
  95.1 0.1 collective-permute-start.26
  95.2 0.1 collective-permute-start.14
  95.3 0.5 collective-permute-start.16
  95.8 0.1 collective-permute-start.25
  95.9 5.7 %collective-permute-done.26.refs_6_ = bf16[4,256,128]{2,1,0:T(8,128)(2,1)S(1)} collective-permute-done((bf16[4,256,128]{2,1,0:T(8,128)(2,1)S(1)}, bf16[4,256,128]{2,1,0:T(8,128)(2,1)S(1)}, u32[]{:S(2)}, u32[]{:S(2)}) %collective-permute-start.26) | collective-permute-done | bytes 262176 | tf_op jit(solution)/shard_map/ppermute | solution.py:26
  101.5 0.1 fusion.2
  101.6 0.1 copy.7
  101.7 0.1 reshape.15.pairs_ref
  101.8 1.4 %collective-permute-done.27.refs_7_ = bf16[4,256,128]{2,1,0:T(8,128)(2,1)} collective-permute-done((bf16[4,256,128]{2,1,0:T(8,128)(2,1)S(1)}, bf16[4,256,128]{2,1,0:T(8,128)(2,1)}, u32[]{:S(2)}, u32[]{:S(2)}) %collective-permute-start.27) | collective-permute-done | bytes 262176 | tf_op jit(solution)/shard_map/ppermute | solution.py:26
  103.2 8.5 %coherence.1 = f32[256,8,256]{2,1,0:T(8,128)} custom-call(s32[16]{0:T(128)S(1)} %reshape.15.pairs_ref, bf16[4,256,128]{2,1,0:T(8,128)(2,1)S(1)} %bitcast.25, bf16[4,256,128]{2,1,0:T(8,128)(2,1)S(1)} %collective-permute-done.14.refs_1_, bf16[4,256,128]{2,1,0:T(8,128)(2,1)S(1)} %collective-permute-done.15.refs_2_, ...), custom_call_target="tpu_custom_call" | custom-call | tf_op jit(solution)/shard_map/coherence/pallas_call | solution.py:334
  (29 shorter events, 0.2 us)
Async XLA Ops:
  3.1 23.7 %collective-permute-start.1 = (bf16[49,16,4,128]{3,2,1,0:T(4,128)(2,1)}, bf16[49,16,4,128]{3,2,1,0:T(4,128)(2,1)S(1)}, u32[]{:S(2)}, u32[]{:S(2)}) collective-permute-start(bf16[49,16,4,128]{3,2,1,0:T(4,128)(2,1)} %pick.4.refs_0_), channel_id=1, source_target_pairs={{0,1},{1,0},{2,3},{3,2},{4,5},{5,4},{6,7},{7,6},{8,9},{9,8},{10,11... | collective-permute-start | bytes 2408456 | tf_op jit(solution)/shard_map/ppermute | solution.py:26
  9.2 21.3 %collective-permute-start = (bf16[49,16,4,128]{3,2,1,0:T(4,128)(2,1)}, bf16[49,16,4,128]{3,2,1,0:T(4,128)(2,1)S(1)}, u32[]{:S(2)}, u32[]{:S(2)}) collective-permute-start(bf16[49,16,4,128]{3,2,1,0:T(4,128)(2,1)} %pick.5.refs_0_), channel_id=1, source_target_pairs={{0,2},{1,3},{2,0},{3,1},{4,6},{5,7},{6,4},{7,5},{8,10},{9,11},{10,... | collective-permute-start | bytes 2408456 | tf_op jit(solution)/shard_map/ppermute | solution.py:26
  13.9 5.1 %copy-start.3 = (s32[64,1]{0,1:T(1,128)S(1)}, s32[64,1]{0,1:T(1,128)}, u32[]{:S(2)}) copy-start(s32[64,1]{0,1:T(1,128)} %param.5) | copy-start | bytes 772
  13.9 5.1 %copy-start.4 = (s32[64]{0:T(128)S(1)}, s32[64]{0:T(128)}, u32[]{:S(2)}) copy-start(s32[64]{0:T(128)} %row_ref.7) | copy-start | bytes 772
  13.9 28.3 %collective-permute-start.4 = (bf16[49,16,4,128]{3,2,1,0:T(4,128)(2,1)}, bf16[49,16,4,128]{3,2,1,0:T(4,128)(2,1)S(1)}, u32[]{:S(2)}, u32[]{:S(2)}) collective-permute-start(bf16[49,16,4,128]{3,2,1,0:T(4,128)(2,1)} %pick.6.refs_0_), channel_id=1, source_target_pairs={{0,1},{1,0},{2,3},{3,2},{4,5},{5,4},{6,7},{7,6},{8,9},{9,8},{10,11... | collective-permute-start | bytes 2408456 | tf_op jit(solution)/shard_map/ppermute | solution.py:26
  17.5 43.0 %collective-permute-start.9 = (bf16[49,16,4,128]{3,2,1,0:T(4,128)(2,1)}, bf16[49,16,4,128]{3,2,1,0:T(4,128)(2,1)S(1)}, u32[]{:S(2)}, u32[]{:S(2)}) collective-permute-start(bf16[49,16,4,128]{3,2,1,0:T(4,128)(2,1)} %pick.7.token_ref), channel_id=1, source_target_pairs={{0,1},{1,0},{2,3},{3,2},{4,5},{5,4},{6,7},{7,6},{8,9},{9,8},{10,11... | collective-permute-start | bytes 2408456 | tf_op jit(solution)/shard_map/ppermute | solution.py:26
  19.0 2.2 %copy-start = (bf16[64,16,4,2,256]{4,3,2,1,0:T(2,128)(2,1)S(1)}, bf16[64,16,4,2,256]{4,3,2,1,0:T(2,128)(2,1)}, u32[]{:S(2)}) copy-start(bf16[64,16,4,2,256]{4,3,2,1,0:T(2,128)(2,1)} %param.4) | copy-start | bytes 12582916
  21.2 1.1 %copy-start.2 = (bf16[49,16,4,128]{3,2,1,0:T(4,128)(2,1)S(1)}, bf16[49,16,4,128]{3,2,1,0:T(4,128)(2,1)}, u32[]{:S(2)}) copy-start(bf16[49,16,4,128]{3,2,1,0:T(4,128)(2,1)} %pick.7.token_ref) | copy-start | bytes 2408452
  26.8 6.7 %copy-start.1 = (bf16[64,16,4,2,256]{4,3,2,1,0:T(2,128)(2,1)S(1)}, bf16[64,16,4,2,256]{4,3,2,1,0:T(2,128)(2,1)}, u32[]{:S(2)}) copy-start(bf16[64,16,4,2,256]{4,3,2,1,0:T(2,128)(2,1)} %param.4) | copy-start | bytes 12582916
  29.9 7.5 %collective-permute-start.5 = (bf16[1,4,256,128]{3,2,1,0:T(8,128)(2,1)S(1)}, bf16[1,4,256,128]{3,2,1,0:T(8,128)(2,1)S(1)}, u32[]{:S(2)}, u32[]{:S(2)}) collective-permute-start(bf16[1,4,256,128]{3,2,1,0:T(8,128)(2,1)S(1)} %get-tuple-element.19.token_ref), channel_id=1, source_target_pairs={{0,2},{1,3},{2,0},{3,1},{4,6},{5,7},{6,4},{7,5},{8,10},{9,11},{10,... | collective-permute-start | bytes 786440 | tf_op jit(solution)/shard_map/ppermute | solution.py:26
  35.8 13.4 %collective-permute-start.7 = (bf16[1,4,256,128]{3,2,1,0:T(8,128)(2,1)S(1)}, bf16[1,4,256,128]{3,2,1,0:T(8,128)(2,1)S(1)}, u32[]{:S(2)}, u32[]{:S(2)}) collective-permute-start(bf16[1,4,256,128]{3,2,1,0:T(8,128)(2,1)S(1)} %get-tuple-element.26), channel_id=1, source_target_pairs={{0,2},{1,3},{2,0},{3,1},{4,6},{5,7},{6,4},{7,5},{8,10},{9,11},{10,... | collective-permute-start | bytes 786440 | tf_op jit(solution)/shard_map/ppermute | solution.py:26
  37.5 12.0 %collective-permute-start.8 = (bf16[1,4,256,128]{3,2,1,0:T(8,128)(2,1)S(1)}, bf16[1,4,256,128]{3,2,1,0:T(8,128)(2,1)S(1)}, u32[]{:S(2)}, u32[]{:S(2)}) collective-permute-start(bf16[1,4,256,128]{3,2,1,0:T(8,128)(2,1)S(1)} %merge.8.token_ref), channel_id=1, source_target_pairs={{0,4},{1,5},{2,6},{3,7},{4,0},{5,1},{6,2},{7,3},{8,12},{9,13},{10,... | collective-permute-start | bytes 786440 | tf_op jit(solution)/shard_map/ppermute | solution.py:26
  45.2 9.5 %collective-permute-start.6 = (bf16[1,4,256,128]{3,2,1,0:T(8,128)(2,1)S(1)}, bf16[1,4,256,128]{3,2,1,0:T(8,128)(2,1)S(1)}, u32[]{:S(2)}, u32[]{:S(2)}) collective-permute-start(bf16[1,4,256,128]{3,2,1,0:T(8,128)(2,1)S(1)} %get-tuple-element.25.refs_3_), channel_id=1, source_target_pairs={{0,2},{1,3},{2,0},{3,1},{4,6},{5,7},{6,4},{7,5},{8,10},{9,11},{10,... | collective-permute-start | bytes 786440 | tf_op jit(solution)/shard_map/ppermute | solution.py:26
  47.4 19.2 %collective-permute-start.3 = (bf16[1,4,256,128]{3,2,1,0:T(8,128)(2,1)S(1)}, bf16[1,4,256,128]{3,2,1,0:T(8,128)(2,1)S(1)}, u32[]{:S(2)}, u32[]{:S(2)}) collective-permute-start(bf16[1,4,256,128]{3,2,1,0:T(8,128)(2,1)S(1)} %get-tuple-element.22.token_ref), channel_id=1, source_target_pairs={{0,1},{1,0},{2,3},{3,2},{4,5},{5,4},{6,7},{7,6},{8,9},{9,8},{10,11... | collective-permute-start | bytes 786440 | tf_op jit(solution)/shard_map/ppermute | solution.py:26
  49.1 19.1 %collective-permute-start.12 = (bf16[1,4,256,128]{3,2,1,0:T(8,128)(2,1)S(1)}, bf16[1,4,256,128]{3,2,1,0:T(8,128)(2,1)S(1)}, u32[]{:S(2)}, u32[]{:S(2)}) collective-permute-start(bf16[1,4,256,128]{3,2,1,0:T(8,128)(2,1)S(1)} %get-tuple-element.29), channel_id=1, source_target_pairs={{0,2},{1,3},{2,0},{3,1},{4,6},{5,7},{6,4},{7,5},{8,10},{9,11},{10,... | collective-permute-start | bytes 786440 | tf_op jit(solution)/shard_map/ppermute | solution.py:26
  54.8 13.4 %collective-permute-start.13 = (bf16[1,4,256,128]{3,2,1,0:T(8,128)(2,1)S(1)}, bf16[1,4,256,128]{3,2,1,0:T(8,128)(2,1)S(1)}, u32[]{:S(2)}, u32[]{:S(2)}) collective-permute-start(bf16[1,4,256,128]{3,2,1,0:T(8,128)(2,1)S(1)} %merge.10.token_ref), channel_id=1, source_target_pairs={{0,4},{1,5},{2,6},{3,7},{4,0},{5,1},{6,2},{7,3},{8,12},{9,13},{10,... | collective-permute-start | bytes 786440 | tf_op jit(solution)/shard_map/ppermute | solution.py:26
  63.8 9.6 %collective-permute-start.11 = (bf16[1,4,256,128]{3,2,1,0:T(8,128)(2,1)S(1)}, bf16[1,4,256,128]{3,2,1,0:T(8,128)(2,1)S(1)}, u32[]{:S(2)}, u32[]{:S(2)}) collective-permute-start(bf16[1,4,256,128]{3,2,1,0:T(8,128)(2,1)S(1)} %get-tuple-element.27.refs_2_), channel_id=1, source_target_pairs={{0,2},{1,3},{2,0},{3,1},{4,6},{5,7},{6,4},{7,5},{8,10},{9,11},{10,... | collective-permute-start | bytes 786440 | tf_op jit(solution)/shard_map/ppermute | solution.py:26
  64.9 8.6 %collective-permute-start.2 = (bf16[1,4,256,128]{3,2,1,0:T(8,128)(2,1)S(1)}, bf16[1,4,256,128]{3,2,1,0:T(8,128)(2,1)S(1)}, u32[]{:S(2)}, u32[]{:S(2)}) collective-permute-start(bf16[1,4,256,128]{3,2,1,0:T(8,128)(2,1)S(1)} %get-tuple-element.21), channel_id=1, source_target_pairs={{0,1},{1,0},{2,3},{3,2},{4,5},{5,4},{6,7},{7,6},{8,9},{9,8},{10,11... | collective-permute-start | bytes 786440 | tf_op jit(solution)/shard_map/ppermute | solution.py:26
  66.6 8.0 %collective-permute-start.20 = (bf16[4,256,128]{2,1,0:T(8,128)(2,1)S(1)}, bf16[4,256,128]{2,1,0:T(8,128)(2,1)S(1)}, u32[]{:S(2)}, u32[]{:S(2)}) collective-permute-start(bf16[4,256,128]{2,1,0:T(8,128)(2,1)S(1)} %bitcast.20), channel_id=1, source_target_pairs={{0,16},{8,24},{16,0},{24,8},{1,17},{9,25},{17,1},{25,9},{2,18},{10... | collective-permute-start | bytes 786440 | tf_op jit(solution)/shard_map/ppermute | solution.py:26
  68.3 9.2 %collective-permute-start.23 = (bf16[4,256,128]{2,1,0:T(8,128)(2,1)S(1)}, bf16[4,256,128]{2,1,0:T(8,128)(2,1)S(1)}, u32[]{:S(2)}, u32[]{:S(2)}) collective-permute-start(bf16[4,256,128]{2,1,0:T(8,128)(2,1)S(1)} %bitcast.26), channel_id=1, source_target_pairs={{0,16},{8,24},{16,0},{24,8},{1,17},{9,25},{17,1},{25,9},{2,18},{10... | collective-permute-start | bytes 786440 | tf_op jit(solution)/shard_map/ppermute | solution.py:26
  69.5 11.4 %collective-permute-start.10 = (bf16[1,4,256,128]{3,2,1,0:T(8,128)(2,1)S(1)}, bf16[1,4,256,128]{3,2,1,0:T(8,128)(2,1)S(1)}, u32[]{:S(2)}, u32[]{:S(2)}) collective-permute-start(bf16[1,4,256,128]{3,2,1,0:T(8,128)(2,1)S(1)} %merge.11.refs_3_), channel_id=1, source_target_pairs={{0,4},{1,5},{2,6},{3,7},{4,0},{5,1},{6,2},{7,3},{8,12},{9,13},{10,... | collective-permute-start | bytes 786440 | tf_op jit(solution)/shard_map/ppermute | solution.py:26
  73.4 7.5 %collective-permute-start.19 = (bf16[4,256,128]{2,1,0:T(8,128)(2,1)S(1)}, bf16[4,256,128]{2,1,0:T(8,128)(2,1)S(1)}, u32[]{:S(2)}, u32[]{:S(2)}) collective-permute-start(bf16[4,256,128]{2,1,0:T(8,128)(2,1)S(1)} %bitcast.21), channel_id=1, source_target_pairs={{0,8},{8,0},{16,24},{24,16},{1,9},{9,1},{17,25},{25,17},{2,10},{10... | collective-permute-start | bytes 786440 | tf_op jit(solution)/shard_map/ppermute | solution.py:26
  73.5 10.8 %collective-permute-start.22 = (bf16[4,256,128]{2,1,0:T(8,128)(2,1)S(1)}, bf16[4,256,128]{2,1,0:T(8,128)(2,1)S(1)}, u32[]{:S(2)}, u32[]{:S(2)}) collective-permute-start(bf16[4,256,128]{2,1,0:T(8,128)(2,1)S(1)} %bitcast.27), channel_id=1, source_target_pairs={{0,8},{8,0},{16,24},{24,16},{1,9},{9,1},{17,25},{25,17},{2,10},{10... | collective-permute-start | bytes 786440 | tf_op jit(solution)/shard_map/ppermute | solution.py:26
  74.7 11.0 %collective-permute-start.21 = (bf16[4,256,128]{2,1,0:T(8,128)(2,1)S(1)}, bf16[4,256,128]{2,1,0:T(8,128)(2,1)S(1)}, u32[]{:S(2)}, u32[]{:S(2)}) collective-permute-start(bf16[4,256,128]{2,1,0:T(8,128)(2,1)S(1)} %collective-permute-done.20.refs_2_), channel_id=1, source_target_pairs={{0,8},{8,0},{16,24},{24,16},{1,9},{9,1},{17,25},{25,17},{2,10},{10... | collective-permute-start | bytes 786440 | tf_op jit(solution)/shard_map/ppermute | solution.py:26
  77.5 8.2 %collective-permute-start.24 = (bf16[4,256,128]{2,1,0:T(8,128)(2,1)S(1)}, bf16[4,256,128]{2,1,0:T(8,128)(2,1)S(1)}, u32[]{:S(2)}, u32[]{:S(2)}) collective-permute-start(bf16[4,256,128]{2,1,0:T(8,128)(2,1)S(1)} %collective-permute-done.23.refs_6_), channel_id=1, source_target_pairs={{0,8},{8,0},{16,24},{24,16},{1,9},{9,1},{17,25},{25,17},{2,10},{10... | collective-permute-start | bytes 786440 | tf_op jit(solution)/shard_map/ppermute | solution.py:26
  80.9 11.0 %collective-permute-start.17 = (bf16[1,4,256,128]{3,2,1,0:T(8,128)(2,1)S(1)}, bf16[1,4,256,128]{3,2,1,0:T(8,128)(2,1)S(1)}, u32[]{:S(2)}, u32[]{:S(2)}) collective-permute-start(bf16[1,4,256,128]{3,2,1,0:T(8,128)(2,1)S(1)} %get-tuple-element.30), channel_id=1, source_target_pairs={{0,2},{1,3},{2,0},{3,1},{4,6},{5,7},{6,4},{7,5},{8,10},{9,11},{10,... | collective-permute-start | bytes 786440 | tf_op jit(solution)/shard_map/ppermute | solution.py:26
  80.9 13.5 %collective-permute-start.18 = (bf16[1,4,256,128]{3,2,1,0:T(8,128)(2,1)S(1)}, bf16[1,4,256,128]{3,2,1,0:T(8,128)(2,1)S(1)}, u32[]{:S(2)}, u32[]{:S(2)}) collective-permute-start(bf16[1,4,256,128]{3,2,1,0:T(8,128)(2,1)S(1)} %merge.13.refs_3_), channel_id=1, source_target_pairs={{0,4},{1,5},{2,6},{3,7},{4,0},{5,1},{6,2},{7,3},{8,12},{9,13},{10,... | collective-permute-start | bytes 786440 | tf_op jit(solution)/shard_map/ppermute | solution.py:26
  84.3 17.2 %copy-start.5 = (s32[32,2]{0,1:T(2,128)S(1)}, s32[32,2]{0,1:T(2,128)}, u32[]{:S(2)}) copy-start(s32[32,2]{0,1:T(2,128)} %param.7) | copy-start | bytes 772
  84.3 11.0 %collective-permute-start.15 = (bf16[4,256,128]{2,1,0:T(8,128)(2,1)S(1)}, bf16[4,256,128]{2,1,0:T(8,128)(2,1)S(1)}, u32[]{:S(2)}, u32[]{:S(2)}) collective-permute-start(bf16[4,256,128]{2,1,0:T(8,128)(2,1)S(1)} %bitcast.23), channel_id=1, source_target_pairs={{0,16},{8,24},{16,0},{24,8},{1,17},{9,25},{17,1},{25,9},{2,18},{10... | collective-permute-start | bytes 786440 | tf_op jit(solution)/shard_map/ppermute | solution.py:26
  95.1 6.4 %collective-permute-start.26 = (bf16[4,256,128]{2,1,0:T(8,128)(2,1)S(1)}, bf16[4,256,128]{2,1,0:T(8,128)(2,1)S(1)}, u32[]{:S(2)}, u32[]{:S(2)}) collective-permute-start(bf16[4,256,128]{2,1,0:T(8,128)(2,1)S(1)} %bitcast.29), channel_id=1, source_target_pairs={{0,16},{8,24},{16,0},{24,8},{1,17},{9,25},{17,1},{25,9},{2,18},{10... | collective-permute-start | bytes 786440 | tf_op jit(solution)/shard_map/ppermute | solution.py:26
  95.2 6.6 %collective-permute-start.14 = (bf16[4,256,128]{2,1,0:T(8,128)(2,1)S(1)}, bf16[4,256,128]{2,1,0:T(8,128)(2,1)S(1)}, u32[]{:S(2)}, u32[]{:S(2)}) collective-permute-start(bf16[4,256,128]{2,1,0:T(8,128)(2,1)S(1)} %bitcast.24), channel_id=1, source_target_pairs={{0,8},{8,0},{16,24},{24,16},{1,9},{9,1},{17,25},{25,17},{2,10},{10... | collective-permute-start | bytes 786440 | tf_op jit(solution)/shard_map/ppermute | solution.py:26
  95.3 6.5 %collective-permute-start.16 = (bf16[4,256,128]{2,1,0:T(8,128)(2,1)S(1)}, bf16[4,256,128]{2,1,0:T(8,128)(2,1)}, u32[]{:S(2)}, u32[]{:S(2)}) collective-permute-start(bf16[4,256,128]{2,1,0:T(8,128)(2,1)S(1)} %collective-permute-done.15.refs_2_), channel_id=1, source_target_pairs={{0,8},{8,0},{16,24},{24,16},{1,9},{9,1},{17,25},{25,17},{2,10},{10... | collective-permute-start | bytes 786440 | tf_op jit(solution)/shard_map/ppermute | solution.py:26
  95.8 6.1 %collective-permute-start.25 = (bf16[4,256,128]{2,1,0:T(8,128)(2,1)S(1)}, bf16[4,256,128]{2,1,0:T(8,128)(2,1)}, u32[]{:S(2)}, u32[]{:S(2)}) collective-permute-start(bf16[4,256,128]{2,1,0:T(8,128)(2,1)S(1)} %bitcast.30), channel_id=1, source_target_pairs={{0,8},{8,0},{16,24},{24,16},{1,9},{9,1},{17,25},{25,17},{2,10},{10... | collective-permute-start | bytes 786440 | tf_op jit(solution)/shard_map/ppermute | solution.py:26
  101.5 1.7 %collective-permute-start.27 = (bf16[4,256,128]{2,1,0:T(8,128)(2,1)S(1)}, bf16[4,256,128]{2,1,0:T(8,128)(2,1)}, u32[]{:S(2)}, u32[]{:S(2)}) collective-permute-start(bf16[4,256,128]{2,1,0:T(8,128)(2,1)S(1)} %collective-permute-done.26.refs_6_), channel_id=1, source_target_pairs={{0,8},{8,0},{16,24},{24,16},{1,9},{9,1},{17,25},{25,17},{2,10},{10... | collective-permute-start | bytes 786440 | tf_op jit(solution)/shard_map/ppermute | solution.py:26
